TPU v7x, 32 devices: a whole 2x2x4 slice. The times are simulated.
32 devices in a mesh: groups: 2 (over y), row: 4 (over z), col: 4 (over x, core).
Axes of the slice: x: 2, y: 2, z: 4, core: 2. Of those that a mesh axis runs over, the one named last changes fastest.
Arguments:
- embeddings: bfloat16 [8192, 256], P(('groups', 'row', 'col')), parts along dimension 0, may hold values from -6 to 6
- tile_list: int32 [8, 4, 2, 48], P(('groups', 'row'), 'col'), parts along dimension 0, may hold values from 0 to 7, as said below
- tile_count: int32 [8, 4], P(('groups', 'row'), 'col'), parts along dimension 0, may hold values from 8 to 48, as said below
- seeds: int32 [128, 128], P('groups'), parts along dimension 0, may hold values from 0 to 4095
Outputs:
- ranks: float32 [8192, 64], P(('groups', 'row', 'col')), parts along dimension 0
There are 2 independent parts, one for each index of `groups`. A program takes and returns all parts, laid end to end along the dimension named above; each array names one. Nothing has to cross between parts.
Inputs may be any that keep to these rules, and one draw needn't show every extreme that they name: `tile_list`: row tile entries are below 8, column tile entries below 8; within a cell the 48 slots name distinct pairs, and slot p names row tile p for p < 8. `tile_count`: some cell in every draw has all 48 slots live.
All inputs are finite; a program needn't handle non-finite values.
Results may differ from a plain program's by a relative error of at most 0.006.
Values may be sent and summed in bfloat16 or wider, within the bound.
No kernel may reach another device: no remote copies, remote signals or barrier semaphores. Data moves between devices by JAX's collectives and lax.ppermute only.
A program may use at most 64 MiB of HBM per device.

v0:
```python
import jax
import jax.numpy as jnp
from jax import lax
from jax.sharding import PartitionSpec as P

TILE = 128
ITERS = 3
SEED_SHARE = 32


KERNEL_GAIN = 4.0
DAMPING = 0.85
EPSILON = 1e-06


def normalize(rows_in):
    widened = rows_in.astype(jnp.float32)
    factor = lax.rsqrt(jnp.mean(widened * widened, axis=-1, keepdims=True) + EPSILON)
    return (widened * factor * widened.shape[-1] ** (-0.5)).astype(jnp.bfloat16)


def block_width():
    for option_width in (16, 8, 4, 2):
        return option_width
    return 1


def seed_mass(seed_index, is_valid, length):
    spots = jnp.arange(length, dtype=jnp.int32)

    def one_column(pieces):
        index_row, valid_row = pieces
        hits = (index_row[:, None] == spots[None, :]) & valid_row[:, None]
        return jnp.sum(hits.astype(jnp.float32), axis=0) * float(SEED_SHARE)

    table = lax.map(one_column, (seed_index, is_valid))
    return table.T


def local(embeddings, tile_list, tile_count, seeds):
    n_row = lax.axis_size("row")
    n_col = lax.axis_size("col")
    row_pos = lax.axis_index("row")
    col_pos = lax.axis_index("col")
    slice_rows = embeddings.shape[0]
    grid_rows = slice_rows * n_col
    row_tiles = grid_rows // TILE
    col_tiles = slice_rows * n_row // TILE
    seed_cols = seeds.shape[0]
    unit_rows = normalize(embeddings)
    row_emb = lax.all_gather(unit_rows, "col", axis=0, tiled=True).reshape(row_tiles, TILE, -1)
    col_emb = lax.all_gather(unit_rows, "row", axis=0, tiled=True).reshape(col_tiles, TILE, -1)
    slots = tile_list.shape[3]
    width_b = block_width()
    turn_count = slots // width_b
    row_ids = tile_list[0, 0, 0]
    col_ids = tile_list[0, 0, 1]
    live_mask = (jnp.arange(slots, dtype=jnp.int32) < tile_count[0, 0]).astype(jnp.float32)
    row_blocks = row_ids.reshape(turn_count, width_b)
    col_blocks = col_ids.reshape(turn_count, width_b)
    live_blocks = live_mask.reshape(turn_count, width_b)

    def kernel_turn(degree, pieces):
        row_part, col_part, live_part = pieces
        left_tiles = jnp.take(row_emb, row_part, axis=0)
        right_tiles = jnp.take(col_emb, col_part, axis=0)
        inner_prod = jnp.einsum(
            "bie,bje->bij", left_tiles, right_tiles, preferred_element_type=jnp.float32
        )
        values = jnp.exp(KERNEL_GAIN * (2.0 * inner_prod - 2.0)).astype(jnp.bfloat16)
        row_total = jnp.sum(values.astype(jnp.float32), axis=2)
        degree = degree.at[row_part].add(row_total * live_part[:, None])
        return (degree, values)

    degree_part, kernel = lax.scan(
        kernel_turn,
        jnp.zeros((row_tiles, TILE), jnp.float32),
        (row_blocks, col_blocks, live_blocks),
    )
    degree_part = degree_part.reshape(grid_rows)

    def spread(ranks_col):
        col_ranks = ranks_col.reshape(col_tiles, TILE, seed_cols)

        def rank_turn(running, pieces):
            row_part, col_part, live_part, values = pieces
            right_tiles = jnp.take(col_ranks, col_part, axis=0)
            product = jnp.einsum(
                "bij,bjk->bik", values, right_tiles, preferred_element_type=jnp.float32
            )
            running = running.at[row_part].add(product * live_part[:, None, None])
            return (running, None)

        running, unused = lax.scan(
            rank_turn,
            jnp.zeros((row_tiles, TILE, seed_cols), jnp.float32),
            (row_blocks, col_blocks, live_blocks, kernel),
        )
        return running.reshape(grid_rows, seed_cols)

    own_start = (row_pos * n_col + col_pos) * slice_rows
    own_index = seeds - own_start
    seed_own = seed_mass(own_index, (own_index >= 0) & (own_index < slice_rows), slice_rows)
    degree = lax.psum_scatter(degree_part, "col", scatter_dimension=0, tiled=True)
    opening = lax.all_gather(seed_own.astype(jnp.bfloat16), "row", axis=0, tiled=True)
    partial_rows = spread(opening)
    summed = lax.psum_scatter(partial_rows, "col", scatter_dimension=0, tiled=True)
    rank_rows = (1.0 - DAMPING) * seed_own + DAMPING * summed / degree[:, None]
    for sweep_idx in range(ITERS - 1):
        gathered = lax.all_gather(rank_rows.astype(jnp.bfloat16), "row", axis=0, tiled=True)
        partial_rows = spread(gathered)
        summed = lax.psum_scatter(partial_rows, "col", scatter_dimension=0, tiled=True)
        rank_rows = (1.0 - DAMPING) * seed_own + DAMPING * summed / degree[:, None]
    return rank_rows


def solution(mesh):
    return jax.shard_map(
        local,
        mesh=mesh,
        in_specs=(
            P(("groups", "row", "col"), None),
            P(("groups", "row"), "col", None, None),
            P(("groups", "row"), "col"),
            P("groups", None),
        ),
        out_specs=P(("groups", "row", "col"), None),
        check_vma=False,
    )
```

profile of v0, /device:TPU:0, one launch (start us, length us, event | category | flops | bytes accessed | tf_op | source)
XLA Modules:
  0.0 212.9 jit_solution(8264447443407357415)
XLA Ops:
  8.6 8.6 %all_gather.15 = bf16[1024,256]{1,0:T(8,128)(2,1)S(1)} all-gather(bf16[256,256]{1,0:T(8,128)(2,1)S(1)} %fusion.54), channel_id=1, replica_groups=mesh['groups'=2,'row'=4,'col'=4] {'col'}, dimensions={0}, use_global_device_ids=true | all-gather | bytes 655360 | tf_op jit(solution)/shard_map/all_gather | solution.py:51
  17.2 16.3 %all_gather.16 = bf16[1024,256]{1,0:T(8,128)(2,1)S(1)} all-gather(bf16[256,256]{1,0:T(8,128)(2,1)S(1)} %fusion.54), channel_id=1, replica_groups=mesh['groups'=2,'row'=4,'col'=4] {'row'}, dimensions={0}, use_global_device_ids=true | all-gather | bytes 655360 | tf_op jit(solution)/shard_map/all_gather | solution.py:52
  34.4 25.1 %while.55 = (s32[]{:T(128)}, f32[8,128]{1,0:T(8,128)S(1)}, bf16[3,16,128,128]{3,2,1,0:T(8,128)(2,1)S(1)}, s32[3,16]{1,0:T(4,128)S(1)}, bf16[8,128,256]{2,1,0:T(8...) while((s32[]{:T(128)}, f32[8,128]{1,0:T(8,128)S(1)}, ...), condition=%wide.region_7.9_spmd, body=%wide.region_4.0_spmd.sunk | while | flops 136843504 | bytes 8943021 | solution.py:75
  34.5 1.6 gather_fusion
  36.1 1.6 gather_fusion.1
  37.7 2.9 %convert_reduce_fusion.4 = (f32[16,128]{1,0:T(8,128)S(1)}, bf16[16,128,128]{1,2,0:T(8,128)(2,1)}) fusion(bf16[16,128,256]{2,1,0:T(8,128)(2,1)} %gather_fusion, pred[16]{0:T(512)(128)(4,1)S(1)} %get-tuple-element.601, bf16[16,128,256]{2,1,0:T(8,128)(2,1)} %gather_fusion.1, pred[16]{0:T(512)(128)(4,1)S(1)} %get-tuple-element.603), kind=kOutput, calls=%fused_computation.23.clone.1 | convolution fusion | flops 136837120 | bytes 2629664 | tf_op jit(solution)/shard_map/while/body/eval_jaxpr/bie,bje->bij/dot_general | solution.py:67
  42.9 1.6 gather_fusion
  44.5 1.6 gather_fusion.1
  46.1 2.9 %convert_reduce_fusion.4 = (f32[16,128]{1,0:T(8,128)S(1)}, bf16[16,128,128]{1,2,0:T(8,128)(2,1)}) fusion(bf16[16,128,256]{2,1,0:T(8,128)(2,1)} %gather_fusion, pred[16]{0:T(512)(128)(4,1)S(1)} %get-tuple-element.601, bf16[16,128,256]{2,1,0:T(8,128)(2,1)} %gather_fusion.1, pred[16]{0:T(512)(128)(4,1)S(1)} %get-tuple-element.603), kind=kOutput, calls=%fused_computation.23.clone.1 | convolution fusion | flops 136837120 | bytes 2629664 | tf_op jit(solution)/shard_map/while/body/eval_jaxpr/bie,bje->bij/dot_general | solution.py:67
  51.2 1.6 gather_fusion
  52.8 1.6 gather_fusion.1
  54.5 2.9 %convert_reduce_fusion.4 = (f32[16,128]{1,0:T(8,128)S(1)}, bf16[16,128,128]{1,2,0:T(8,128)(2,1)}) fusion(bf16[16,128,256]{2,1,0:T(8,128)(2,1)} %gather_fusion, pred[16]{0:T(512)(128)(4,1)S(1)} %get-tuple-element.601, bf16[16,128,256]{2,1,0:T(8,128)(2,1)} %gather_fusion.1, pred[16]{0:T(512)(128)(4,1)S(1)} %get-tuple-element.603), kind=kOutput, calls=%fused_computation.23.clone.1 | convolution fusion | flops 136837120 | bytes 2629664 | tf_op jit(solution)/shard_map/while/body/eval_jaxpr/bie,bje->bij/dot_general | solution.py:67
  59.6 14.4 %while.59 = (s32[]{:T(128)}, f32[64,256]{1,0:T(8,128)S(1)}, s32[64,128]{1,0:T(8,128)S(1)}, pred[64,128]{1,0:T(8,128)(4,1)S(1)}, s32[]{:T(128)}, /*index=5*/s32[]{:T(128)}) while((s32[]{:T(128)}, f32[64,256]{1,0:T(8,128)S(1)}, s32[64,128]{1,0:T(8,128)S(1)}, pred[64,128]{1,0:T(8,128)(4,1)S(1)}, s32[]{:T(128)}, ...), condition=%wide.region_2.3_spmd.clone, body=%wide.region_0.2_spmd.clone.sunk | while | flops 131074 | bytes 7121 | solution.py:36
  74.1 13.4 %all_gather.17 = bf16[1024,64]{0,1:T(8,128)(2,1)S(1)} all-gather(bf16[256,64]{0,1:T(8,128)(2,1)S(1)} %convert_bitcast_fusion), channel_id=1, replica_groups=mesh['groups'=2,'row'=4,'col'=4] {'row'}, dimensions={0}, use_global_device_ids=true | all-gather | bytes 163840 | tf_op jit(solution)/shard_map/all_gather | solution.py:105
  87.7 7.9 %while.56 = (s32[]{:T(128)}, f32[8,128,64]{1,2,0:T(8,128)S(1)}, s32[3,16]{1,0:T(4,128)S(1)}, bf16[3,16,128,128]{3,2,1,0:T(8,128)(2,1)S(1)}, s32[3,16]{1,0:T(4,12...) while((s32[]{:T(128)}, f32[8,128,64]{1,2,0:T(8,128)S(1)}, ...), condition=%wide.region_10.13_spmd, body=%wide.region_8.12_spmd.sunk | while | flops 33948816 | bytes 3675829 | solution.py:94
  97.6 5.7 %all-reduce = f32[1024]{0:T(1024)S(1)} all-reduce(f32[1024]{0:T(1024)S(1)} %bitcast.153), channel_id=3, replica_groups=mesh['groups'=2,'row'=4,'col'=4] {'col'}, use_global_device_ids=true, to_apply=%region_12.15.clone | all-reduce | flops 1024 | bytes 8192
  103.3 14.2 %reduce-scatter.4.cloned.1.call-done = f32[256,64]{0,1:T(8,128)} async-done(((f32[1024,64]{0,1:T(8,128)}), f32[256,64]{0,1:T(8,128)}) %reduce-scatter.4.cloned.1.call-update) | async-done | bytes 65552 | tf_op jit(solution)/shard_map/reduce_scatter | solution.py:107
  118.4 13.4 %all_gather.18 = bf16[1024,64]{0,1:T(8,128)(2,1)S(1)} all-gather(bf16[256,64]{0,1:T(8,128)(2,1)S(1)} %fusion.55), channel_id=1, replica_groups=mesh['groups'=2,'row'=4,'col'=4] {'row'}, dimensions={0}, use_global_device_ids=true | all-gather | bytes 163840 | tf_op jit(solution)/shard_map/all_gather | solution.py:110
  132.0 7.9 %while.57 = (s32[]{:T(128)}, f32[8,128,64]{1,2,0:T(8,128)S(1)}, s32[3,16]{1,0:T(4,128)S(1)}, bf16[3,16,128,128]{3,2,1,0:T(8,128)(2,1)S(1)}, s32[3,16]{1,0:T(4,12...) while((s32[]{:T(128)}, f32[8,128,64]{1,2,0:T(8,128)S(1)}, ...), condition=%wide.region_15.18_spmd, body=%wide.region_13.17_spmd.sunk | while | flops 33948816 | bytes 3675829 | solution.py:94
  140.8 20.5 %reduce-scatter.6.cloned.1.call-done = f32[256,64]{0,1:T(8,128)} async-done(((f32[1024,64]{0,1:T(8,128)}), f32[256,64]{0,1:T(8,128)}) %reduce-scatter.6.cloned.1.call-update) | async-done | bytes 65552 | tf_op jit(solution)/shard_map/reduce_scatter | solution.py:112
  162.1 13.4 %all_gather.19 = bf16[1024,64]{0,1:T(8,128)(2,1)S(1)} all-gather(bf16[256,64]{0,1:T(8,128)(2,1)S(1)} %fusion.56), channel_id=1, replica_groups=mesh['groups'=2,'row'=4,'col'=4] {'row'}, dimensions={0}, use_global_device_ids=true | all-gather | bytes 163840 | tf_op jit(solution)/shard_map/all_gather | solution.py:110
  175.7 7.9 %while.58 = (s32[]{:T(128)}, f32[8,128,64]{1,2,0:T(8,128)S(1)}, s32[3,16]{1,0:T(4,128)S(1)}, bf16[3,16,128,128]{3,2,1,0:T(8,128)(2,1)S(1)}, s32[3,16]{1,0:T(4,12...) while((s32[]{:T(128)}, f32[8,128,64]{1,2,0:T(8,128)S(1)}, ...), condition=%wide.region_19.22_spmd, body=%wide.region_17.21_spmd.sunk | while | flops 33948816 | bytes 3675829 | solution.py:94
  184.4 20.5 %reduce-scatter.8.cloned.1.call-done = f32[256,64]{0,1:T(8,128)} async-done(((f32[1024,64]{0,1:T(8,128)}), f32[256,64]{0,1:T(8,128)}) %reduce-scatter.8.cloned.1.call-update) | async-done | bytes 65552 | tf_op jit(solution)/shard_map/reduce_scatter | solution.py:112
  204.9 1.5 bitcast_add_fusion
  (444 shorter events, 49.3 us)
Async XLA Ops:
  6.5 27.0 %copy-start.1 = (s32[1,1,2,48]{3,2,1,0:T(2,128)S(1)}, s32[1,1,2,48]{3,2,1,0:T(2,128)}, u32[]{:S(2)}) copy-start(s32[1,1,2,48]{3,2,1,0:T(2,128)} %param.19) | copy-start | bytes 1156
  6.5 111.0 %reduce-scatter.4.cloned.1.call-start = ((), (), s32[]{:S(2)}) async-start(), calls=%async_computation.3 | async-start | bytes 327680 | tf_op jit(solution)/shard_map/reduce_scatter | solution.py:107
  34.4 25.1 %copy-start = (s32[64,128]{1,0:T(8,128)S(1)}, s32[64,128]{1,0:T(8,128)}, u32[]{:S(2)}) copy-start(s32[64,128]{1,0:T(8,128)} %param.21) | copy-start | bytes 98308
  87.6 8.8 %copy-start.2 = (u32[32]{0:T(128)S(1)}, u32[32]{0:T(128)}, u32[]{:S(2)}) copy-start(u32[32]{0:T(128)} %constant.156) | copy-start | bytes 388
  96.3 64.9 %reduce-scatter.6.cloned.1.call-start = ((), (), s32[]{:S(2)}) async-start(), calls=%async_computation.4 | async-start | bytes 327680 | tf_op jit(solution)/shard_map/reduce_scatter | solution.py:112
  140.7 64.2 %reduce-scatter.8.cloned.1.call-start = ((), (), s32[]{:S(2)}) async-start(), calls=%async_computation.5 | async-start | bytes 327680 | tf_op jit(solution)/shard_map/reduce_scatter | solution.py:112
Sparse Core Ops, SparseCore 0:
  96.5 21.0 reduce-scatter.3
  140.8 20.3 reduce-scatter.5
  184.5 20.3 reduce-scatter.7
where the time goes:
time: 213 us
  blocking collectives  70.8 us (33%)
  waiting for transfers between devices  55.3 us (26%)
  local copies, waits for them, and re-layouts  27.7 us (13%)
  other arithmetic  27.6 us (13%)
  between operations  14.5 us (7%)
  matrix products  13.8 us (6%)
  loops' own time  3.05 us (1%)
    reduce_scatter x3, waiting for transfers between devices, local(): lax.psum_scatter(partial_rows, 'col', scatter_dimension=0, tiled=True)  55.3 us
    all_gather x2, blocking collectives, local(): lax.all_gather(rank_rows.astype(jnp.bfloat16), 'row', axis=0, tiled=True)  26.8 us
    all_gather x1, blocking collectives, local(): lax.all_gather(unit_rows, 'row', axis=0, tiled=True)  16.3 us
    all_gather x1, blocking collectives, local(): lax.all_gather(seed_own.astype(jnp.bfloat16), 'row', axis=0, tiled=True)  13.4 us
    scatter-add x9, other arithmetic, rank_turn(): running = running.at[row_part].add(product * live_part[:, None, None])  12.1 us
    dot_general x3, matrix products, kernel_turn(): jnp.einsum('bie,bje->bij', left_tiles, right_tiles, preferred_element_typ...  8.78 us
    all_gather x1, blocking collectives, local(): lax.all_gather(unit_rows, 'col', axis=0, tiled=True)  8.62 us
    reduce_sum x64, other arithmetic, one_column(): return jnp.sum(hits.astype(jnp.float32), axis=0) * float(SEED_SHARE)  7.41 us
  transfers between devices with their start and end apart: 3, of which 3 were waited for; matrix products, arithmetic and copies ran while one was open for 0% of the time, Pallas kernels for 0%

commit v1 on v0

--- a/solution.py
+++ b/solution.py
@@ -1,6 +1,11 @@
+import functools
+import math
+
 import jax
 import jax.numpy as jnp
 from jax import lax
+from jax.experimental import pallas as pl
+from jax.experimental.pallas import tpu as pltpu
 from jax.sharding import PartitionSpec as P
 
 TILE = 128
@@ -12,11 +17,264 @@
 DAMPING = 0.85
 EPSILON = 1e-06
 
+SLOPE = 2.0 * KERNEL_GAIN * math.log2(math.e)
+DEAD = -1e9
+MASK_ROWS = 16
+EXTRA_ROWS = 16
+
+F32 = jnp.float32
+BF16 = jnp.bfloat16
+
 
 def normalize(rows_in):
-    widened = rows_in.astype(jnp.float32)
+    widened = rows_in.astype(F32)
     factor = lax.rsqrt(jnp.mean(widened * widened, axis=-1, keepdims=True) + EPSILON)
-    return (widened * factor * widened.shape[-1] ** (-0.5)).astype(jnp.bfloat16)
+    return (widened * factor * widened.shape[-1] ** (-0.5)).astype(BF16)
+
+
+def dot_nt(lhs, rhs):
+    return lax.dot_general(lhs, rhs, (((1,), (1,)), ((), ())), preferred_element_type=F32)
+
+
+def dot_nn(lhs, rhs):
+    return lax.dot_general(lhs, rhs, (((1,), (0,)), ((), ())), preferred_element_type=F32)
+
+
+def payload_kernel(count_ref, emb_ref, list_ref, out_ref):
+    rows = emb_ref.shape[0]
+    width = emb_ref.shape[1]
+    slots = list_ref.shape[1]
+    out_ref[0:rows, :] = normalize(emb_ref[...])
+    live = lax.broadcasted_iota(jnp.int32, (1, slots), 1) < count_ref[0, 0]
+    col_hot = (lax.broadcasted_iota(jnp.int32, (EXTRA_ROWS, slots), 0) == list_ref[1:2, :]) & live
+    row_hot = lax.broadcasted_iota(jnp.int32, (width, slots), 0) == list_ref[0:1, :]
+    table = dot_nt(col_hot.astype(F32).astype(BF16), row_hot.astype(F32).astype(BF16))
+    out_ref[rows : rows + EXTRA_ROWS, :] = table.astype(BF16)
+
+
+def restart_kernel(me_ref, seeds_ref, out_ref, counts):
+    seed_cols = seeds_ref.shape[0]
+    tiles = counts.shape[1]
+    me = me_ref[0]
+    spot = lax.broadcasted_iota(jnp.int32, (tiles, TILE), 0)
+    kk, xs, zs, half = spot // 16, (spot // 8) % 2, (spot // 2) % 4, spot % 2
+    tile_ids = (me ^ (zs * 4 + xs * 2 + kk)) * 2 + half
+    lows = lax.broadcasted_iota(jnp.int32, (TILE, TILE), 0)
+
+    @pl.loop(0, seed_cols, unroll=4)
+    def _(k):
+        row = seeds_ref[pl.ds(k, 1), :]
+        high_hot = (tile_ids == row // TILE).astype(F32).astype(BF16)
+        low_hot = (lows == row % TILE).astype(F32).astype(BF16)
+        counts[k] = dot_nt(high_hot, low_hot) * float(SEED_SHARE)
+
+    for t in range(tiles):
+        out_ref[0:seed_cols, t * TILE : (t + 1) * TILE] = counts[:, t, :].astype(BF16)
+    rest = out_ref.shape[0] - seed_cols
+    first = lax.broadcasted_iota(jnp.int32, (rest, out_ref.shape[1]), 0) == 0
+    out_ref[seed_cols:, :] = first.astype(F32).astype(BF16)
+
+
+def build_kernel(me_ref, rt_ref, *refs):
+    blocks = refs[:16]
+    kt_ref, next_ref, gain_ref, units, masks, bias, sems = refs[16:]
+    me = me_ref[0]
+    core, x_pos, z_pos = me % 2, (me // 2) % 2, me // 4
+    rows = units.shape[0] // 16
+    copies = []
+    for s in range(16):
+        copies.append(
+            (
+                pltpu.make_async_copy(
+                    blocks[s].at[pl.ds(0, rows)], units.at[pl.ds(s * rows, rows)], sems.at[2 * s]
+                ),
+                pltpu.make_async_copy(
+                    blocks[s].at[pl.ds(rows, EXTRA_ROWS)],
+                    masks.at[pl.ds(s * EXTRA_ROWS, EXTRA_ROWS)],
+                    sems.at[2 * s + 1],
+                ),
+            )
+        )
+    for one, two in copies:
+        two.start()
+    for one, two in copies:
+        one.start()
+    for one, two in copies:
+        two.wait()
+    width = masks.shape[1]
+    pick_row = lax.broadcasted_iota(jnp.int32, (width, 512), 0)
+    pick_col = lax.broadcasted_iota(jnp.int32, (width, 512), 1) // TILE
+    wanted = 4 * (x_pos ^ (pick_col // 2)) + 2 * core + pick_col % 2
+    pick = (pick_row == wanted).astype(F32).astype(BF16)
+    spread_mask = dot_nn(masks[...], pick)
+    spread_bias = jnp.where(spread_mask > 0.5, -SLOPE, DEAD)
+    for group in range(4):
+        for zs in range(4):
+            cell = group * 4 + zs
+            for xs in range(2):
+                lane = (xs * 4 + zs) * rows
+                bias[group * 8 : group * 8 + 8, lane : lane + rows] = spread_bias[
+                    cell * EXTRA_ROWS : cell * EXTRA_ROWS + 8, xs * rows : (xs + 1) * rows
+                ]
+    for one, two in copies:
+        one.wait()
+    own = 8 * rows
+    chunk = 512
+
+    @pl.loop(0, 16)
+    def _(s):
+        group, zs = s // 4, s % 4
+        start = pl.multiple_of(s * rows, rows)
+        source = units[pl.ds(start, rows), :]
+        bias_row = group * 8 + 2 * (z_pos ^ zs)
+        for c in range(own // chunk):
+            lanes = slice(c * chunk, (c + 1) * chunk)
+            inner = dot_nt(source, units[lanes, :])
+            for half in range(rows // TILE):
+                shift = bias[pl.ds(bias_row + half, 1), lanes]
+                value = jnp.exp2(inner[half * TILE : (half + 1) * TILE] * SLOPE + shift)
+                kt_ref[pl.ds(pl.multiple_of(start + half * TILE, TILE), TILE), lanes] = value.astype(BF16)
+
+    seed_cols = next_ref.shape[0]
+    for c in range(own // chunk):
+        lanes = slice(c * chunk, (c + 1) * chunk)
+        total = dot_nn(rt_ref[...], kt_ref[:, lanes])
+        gain = DAMPING / total[seed_cols : seed_cols + 8]
+        gain_ref[:, lanes] = gain
+        next_ref[:, lanes] = (
+            (1.0 - DAMPING) * rt_ref[0:seed_cols, lanes].astype(F32) + total[0:seed_cols] * gain[0:1]
+        ).astype(BF16)
+
+
+def step_kernel(rt_ref, kt_ref, gain_ref, mine_ref, other_ref, out_ref):
+    seed_cols = out_ref.shape[0]
+    own = out_ref.shape[1]
+    chunk = 512
+    for c in range(own // chunk):
+        lanes = slice(c * chunk, (c + 1) * chunk)
+        total = dot_nn(mine_ref[...], kt_ref[0:own, lanes]) + dot_nn(other_ref[...], kt_ref[own:, lanes])
+        out_ref[:, lanes] = (
+            (1.0 - DAMPING) * rt_ref[0:seed_cols, lanes].astype(F32) + total * gain_ref[0:1, lanes]
+        ).astype(BF16)
+
+
+def last_kernel(rt_ref, kt_ref, gain_ref, mine_ref, other_ref, out_ref):
+    seed_cols = out_ref.shape[1]
+    rows = out_ref.shape[0]
+    own = mine_ref.shape[1]
+    total = dot_nn(mine_ref[...], kt_ref[0:own, 0:rows]) + dot_nn(other_ref[...], kt_ref[own:, 0:rows])
+    ranks = (1.0 - DAMPING) * rt_ref[0:seed_cols, 0:rows].astype(F32) + total * gain_ref[0:1, 0:rows]
+    out_ref[...] = ranks.T
+
+
+WHOLE = pl.BlockSpec(memory_space=pltpu.VMEM)
+SCALARS = pl.BlockSpec(memory_space=pltpu.SMEM)
+REMAIN = pl.BlockSpec(memory_space=pl.ANY)
+
+
+def params():
+    return pltpu.CompilerParams(vmem_limit_bytes=20 * 2**20)
+
+
+def swap(array, mapping):
+    pairs = [(device, mapping(device)) for device in range(16)]
+    return lax.ppermute(array, ("row", "col"), pairs)
+
+
+def outer_pair(device):
+    return device ^ 4
+
+
+def inner_pair(device):
+    z = device // 4
+    return device ^ 12 if z in (1, 2) else device
+
+
+def across(device):
+    return device ^ 2
+
+
+def sibling(device):
+    return device ^ 1
+
+
+def chip_local(embeddings, tile_list, tile_count, seeds):
+    row_pos = lax.axis_index("row")
+    me = (row_pos * 4 + lax.axis_index("col")).reshape(1)
+    rows, width = embeddings.shape
+    seed_cols = seeds.shape[0]
+    sessions = rows * 16
+    own = rows * 8
+    slots = tile_list.shape[3]
+    block = pl.pallas_call(
+        payload_kernel,
+        in_specs=[SCALARS, WHOLE, WHOLE],
+        out_specs=WHOLE,
+        out_shape=jax.ShapeDtypeStruct((rows + EXTRA_ROWS, width), BF16),
+        compiler_params=params(),
+        name="payload",
+    )(tile_count, embeddings, tile_list.reshape(2, slots))
+
+    is_end = (row_pos == 0) | (row_pos == 3)
+    z1 = swap(block, outer_pair)
+    near = swap(block, inner_pair)
+    x0 = swap(block, across)
+    far_a = swap(near, outer_pair)
+    far_b = swap(z1, inner_pair)
+    x1 = swap(z1, across)
+    z2 = jnp.where(is_end, far_a, far_b)
+    last = swap(far_b, outer_pair)
+    x2 = swap(z2, across)
+    z3 = jnp.where(is_end, last, near)
+    x3 = swap(z3, across)
+    mine = [block, z1, z2, z3, x0, x1, x2, x3]
+    other = [swap(one, sibling) for one in mine]
+
+    rt = pl.pallas_call(
+        restart_kernel,
+        in_specs=[SCALARS, WHOLE],
+        out_specs=WHOLE,
+        out_shape=jax.ShapeDtypeStruct((seed_cols + 16, sessions), BF16),
+        scratch_shapes=[pltpu.VMEM((seed_cols, sessions // TILE, TILE), F32)],
+        compiler_params=params(),
+        name="restart",
+    )(me, seeds)
+
+    kt, ranks, gain = pl.pallas_call(
+        build_kernel,
+        in_specs=[SCALARS, WHOLE] + [REMAIN] * 16,
+        out_specs=[WHOLE] * 3,
+        out_shape=[
+            pltpu.VMEM((sessions, own), BF16),
+            jax.ShapeDtypeStruct((seed_cols, own), BF16),
+            jax.ShapeDtypeStruct((8, own), F32),
+        ],
+        scratch_shapes=[
+            pltpu.VMEM((sessions, width), BF16),
+            pltpu.VMEM((16 * EXTRA_ROWS, width), BF16),
+            pltpu.VMEM((32, own), F32),
+            pltpu.SemaphoreType.DMA((32,)),
+        ],
+        compiler_params=params(),
+        name="build",
+    )(me, rt, *mine, *other)
+    for sweep in range(ITERS - 2):
+        ranks = pl.pallas_call(
+            step_kernel,
+            in_specs=[WHOLE] * 5,
+            out_specs=WHOLE,
+            out_shape=jax.ShapeDtypeStruct((seed_cols, own), BF16),
+            compiler_params=params(),
+            name="step",
+        )(rt, kt, gain, ranks, swap(ranks, sibling))
+    return pl.pallas_call(
+        last_kernel,
+        in_specs=[WHOLE] * 5,
+        out_specs=WHOLE,
+        out_shape=jax.ShapeDtypeStruct((rows, seed_cols), F32),
+        compiler_params=params(),
+        name="last",
+    )(rt, kt, gain, ranks, swap(ranks, sibling))
 
 
 def block_width():
@@ -37,7 +295,7 @@
     return table.T
 
 
-def local(embeddings, tile_list, tile_count, seeds):
+def grid_local(embeddings, tile_list, tile_count, seeds):
     n_row = lax.axis_size("row")
     n_col = lax.axis_size("col")
     row_pos = lax.axis_index("row")
@@ -115,6 +373,14 @@
 
 
 def solution(mesh):
+    n_row, n_col = mesh.shape["row"], mesh.shape["col"]
+
+    def local(embeddings, tile_list, tile_count, seeds):
+        small = n_row == 4 and n_col == 4 and embeddings.shape == (2 * TILE, 2 * TILE)
+        if small and seeds.shape == (64, TILE):
+            return chip_local(embeddings, tile_list, tile_count, seeds)
+        return grid_local(embeddings, tile_list, tile_count, seeds)
+
     return jax.shard_map(
         local,
         mesh=mesh,

time: 213 us -> 58.1 us (0.27)
  blocking collectives: 70.8 us -> 0 us
  waiting for transfers between devices: 55.3 us -> 9.59 us
  other arithmetic: 27.6 us -> 0.03 us
  local copies, waits for them, and re-layouts: 27.7 us -> 3.05 us
  Pallas kernels: 0 us -> 22.4 us
  starting transfers between devices: 0.09 us -> 22 us
  matrix products: 13.8 us -> 0 us
  between operations: 14.5 us -> 0.79 us
  loops' own time: 3.05 us -> 0 us
    all_gather x5 -> x0, blocking collectives: 65.2 us -> none  [the longest x2 26.8 us: local(): lax.all_gather(rank_rows.astype(jnp.bfloat16), 'row', axis=0, tiled=True)]
    reduce_scatter x3 -> x0, waiting for transfers between devices: 55.3 us -> none  [local(): lax.psum_scatter(partial_rows, 'col', scatter_dimension=0, tiled=True)]
    pallas_call x0 -> x5, Pallas kernels: none -> 22.4 us  [the longest x1 14.4 us: chip_local(): pl.pallas_call(build_kernel, in_specs=[SCALARS, WHOLE] + [REMAIN] * 16, o...]
    ppermute x0 -> x19, starting transfers between devices: none -> 22 us  [swap(): return lax.ppermute(array, ('row', 'col'), pairs)]
    gather x15 -> x0, local copies, waits for them, and re-layouts: 15.6 us -> none  [the longest x9 5.84 us: rank_turn(): right_tiles = jnp.take(col_ranks, col_part, axis=0)]
    scatter-add x12 -> x0, other arithmetic: 14.1 us -> none  [the longest x9 12.1 us: rank_turn(): running = running.at[row_part].add(product * live_part[:, None, None])]
    dot_general x12 -> x0, matrix products: 13.8 us -> none  [the longest x3 8.78 us: kernel_turn(): jnp.einsum('bie,bje->bij', left_tiles, right_tiles, preferred_element_typ...]
    ppermute x0 -> x19, waiting for transfers between devices: none -> 9.59 us  [swap(): return lax.ppermute(array, ('row', 'col'), pairs)]
  transfers between devices with their start and end apart: 3 -> 19, of which waited for: 3 -> 7; matrix products, arithmetic and copies ran while one was open for 0% -> 0% of each run, Pallas kernels for 0% -> 7%
where the time goes in v1:
time: 58.1 us; the launch traced here: 57.8 us
  Pallas kernels  22.4 us (39%)
  starting transfers between devices  22 us (38%)
  waiting for transfers between devices  9.59 us (17%)
  local copies, waits for them, and re-layouts  3.05 us (5%)
  between operations  0.79 us (1%)
    ppermute x19, starting transfers between devices, swap(): return lax.ppermute(array, ('row', 'col'), pairs)  22 us
    pallas_call x1, Pallas kernels, chip_local(): pl.pallas_call(build_kernel, in_specs=[SCALARS, WHOLE] + [REMAIN] * 16, o...  14.4 us
    ppermute x19, waiting for transfers between devices, swap(): return lax.ppermute(array, ('row', 'col'), pairs)  9.59 us
    pallas_call x1, Pallas kernels, chip_local(): pl.pallas_call(restart_kernel, in_specs=[SCALARS, WHOLE], out_specs=WHOLE...  4.18 us
    pallas_call x1, Pallas kernels, chip_local(): pl.pallas_call(step_kernel, in_specs=[WHOLE] * 5, out_specs=WHOLE, out_sh...  3.08 us
    unnamed x6, local copies, waits for them, and re-layouts  2.33 us
  transfers between devices with their start and end apart: 19, of which 7 were waited for; matrix products, arithmetic and copies ran while one was open for 0% of the time, Pallas kernels for 7%

profile of v1, /device:TPU:0, one launch (start us, length us, event | category | flops | bytes accessed | tf_op | source)
XLA Modules:
  0.0 57.8 jit_solution(11924967246530940214)
XLA Ops:
  0.7 0.9 %copy-done = bf16[256,256]{1,0:T(8,128)(2,1)S(1)} copy-done((bf16[256,256]{1,0:T(8,128)(2,1)S(1)}, bf16[256,256]{1,0:T(8,128)(2,1)}, u32[]{:S(2)}) %copy-start) | copy-done | bytes 131096
  1.6 0.7 %copy-done.2 = s32[1,1,2,48]{3,2,1,0:T(2,128)S(1)} copy-done((s32[1,1,2,48]{3,2,1,0:T(2,128)S(1)}, s32[1,1,2,48]{3,2,1,0:T(2,128)}, u32[]{:S(2)}) %copy-start.2) | copy-done | bytes 408
  2.4 0.7 %collective-permute-start.1 = (bf16[272,256]{1,0:T(8,128)(2,1)S(1)}, bf16[272,256]{1,0:T(8,128)(2,1)S(1)}, u32[]{:S(2)}, u32[]{:S(2)}) collective-permute-start(bf16[272,256]{1,0:T(8,128)(2,1)S(1)} %payload.1.refs_0_), channel_id=1, source_target_pairs={{0,0},{1,1},{2,2},{3,3},{4,8},{5,9},{6,10},{7,11},{8,4},{9,5},{10,... | collective-permute-start | bytes 417800 | tf_op jit(solution)/shard_map/ppermute | solution.py:181
  3.1 5.9 %collective-permute-start = (bf16[272,256]{1,0:T(8,128)(2,1)S(1)}, bf16[272,256]{1,0:T(8,128)(2,1)S(1)}, u32[]{:S(2)}, u32[]{:S(2)}) collective-permute-start(bf16[272,256]{1,0:T(8,128)(2,1)S(1)} %payload.1.refs_0_), channel_id=1, source_target_pairs={{0,4},{1,5},{2,6},{3,7},{4,0},{5,1},{6,2},{7,3},{8,12},{9,13},{10,... | collective-permute-start | bytes 417800 | tf_op jit(solution)/shard_map/ppermute | solution.py:181
  9.0 1.5 %collective-permute-start.5 = (bf16[272,256]{1,0:T(8,128)(2,1)S(1)}, bf16[272,256]{1,0:T(8,128)(2,1)S(1)}, u32[]{:S(2)}, u32[]{:S(2)}) collective-permute-start(bf16[272,256]{1,0:T(8,128)(2,1)S(1)} %payload.1.refs_0_), channel_id=1, source_target_pairs={{0,2},{1,3},{2,0},{3,1},{4,6},{5,7},{6,4},{7,5},{8,10},{9,11},{10,... | collective-permute-start | bytes 417800 | tf_op jit(solution)/shard_map/ppermute | solution.py:181
  10.5 2.3 %collective-permute-start.2 = (bf16[272,256]{1,0:T(8,128)(2,1)S(1)}, bf16[272,256]{1,0:T(8,128)(2,1)S(1)}, u32[]{:S(2)}, u32[]{:S(2)}) collective-permute-start(bf16[272,256]{1,0:T(8,128)(2,1)S(1)} %collective-permute-done.1), channel_id=1, source_target_pairs={{0,4},{1,5},{2,6},{3,7},{4,0},{5,1},{6,2},{7,3},{8,12},{9,13},{10,... | collective-permute-start | bytes 417800 | tf_op jit(solution)/shard_map/ppermute | solution.py:181
  12.7 0.7 %collective-permute-start.3 = (bf16[272,256]{1,0:T(8,128)(2,1)S(1)}, bf16[272,256]{1,0:T(8,128)(2,1)S(1)}, u32[]{:S(2)}, u32[]{:S(2)}) collective-permute-start(bf16[272,256]{1,0:T(8,128)(2,1)S(1)} %collective-permute-done.refs_1_), channel_id=1, source_target_pairs={{0,0},{1,1},{2,2},{3,3},{4,8},{5,9},{6,10},{7,11},{8,4},{9,5},{10,... | collective-permute-start | bytes 417800 | tf_op jit(solution)/shard_map/ppermute | solution.py:181
  14.0 1.5 %collective-permute-start.6 = (bf16[272,256]{1,0:T(8,128)(2,1)S(1)}, bf16[272,256]{1,0:T(8,128)(2,1)S(1)}, u32[]{:S(2)}, u32[]{:S(2)}) collective-permute-start(bf16[272,256]{1,0:T(8,128)(2,1)S(1)} %collective-permute-done.refs_1_), channel_id=1, source_target_pairs={{0,2},{1,3},{2,0},{3,1},{4,6},{5,7},{6,4},{7,5},{8,10},{9,11},{10,... | collective-permute-start | bytes 417800 | tf_op jit(solution)/shard_map/ppermute | solution.py:181
  15.8 5.3 %collective-permute-start.4 = (bf16[272,256]{1,0:T(8,128)(2,1)S(1)}, bf16[272,256]{1,0:T(8,128)(2,1)S(1)}, u32[]{:S(2)}, u32[]{:S(2)}) collective-permute-start(bf16[272,256]{1,0:T(8,128)(2,1)S(1)} %collective-permute-done.3), channel_id=1, source_target_pairs={{0,4},{1,5},{2,6},{3,7},{4,0},{5,1},{6,2},{7,3},{8,12},{9,13},{10,... | collective-permute-start | bytes 417800 | tf_op jit(solution)/shard_map/ppermute | solution.py:181
  21.1 3.0 %collective-permute-done.4 = bf16[272,256]{1,0:T(8,128)(2,1)S(1)} collective-permute-done((bf16[272,256]{1,0:T(8,128)(2,1)S(1)}, bf16[272,256]{1,0:T(8,128)(2,1)S(1)}, u32[]{:S(2)}, u32[]{:S(2)}) %collective-permute-start.4) | collective-permute-done | bytes 139296 | tf_op jit(solution)/shard_map/ppermute | solution.py:181
  24.1 1.5 %collective-permute-start.7 = (bf16[272,256]{1,0:T(8,128)(2,1)S(1)}, bf16[272,256]{1,0:T(8,128)(2,1)S(1)}, u32[]{:S(2)}, u32[]{:S(2)}) collective-permute-start(bf16[272,256]{1,0:T(8,128)(2,1)S(1)} %broadcast_select_fusion.1.refs_2_), channel_id=1, source_target_pairs={{0,2},{1,3},{2,0},{3,1},{4,6},{5,7},{6,4},{7,5},{8,10},{9,11},{10,... | collective-permute-start | bytes 417800 | tf_op jit(solution)/shard_map/ppermute | solution.py:181
  25.6 0.6 %collective-permute-start.8 = (bf16[272,256]{1,0:T(8,128)(2,1)S(1)}, bf16[272,256]{1,0:T(8,128)(2,1)S(1)}, u32[]{:S(2)}, u32[]{:S(2)}) collective-permute-start(bf16[272,256]{1,0:T(8,128)(2,1)S(1)} %broadcast_select_fusion.refs_3_), channel_id=1, source_target_pairs={{0,2},{1,3},{2,0},{3,1},{4,6},{5,7},{6,4},{7,5},{8,10},{9,11},{10,... | collective-permute-start | bytes 417800 | tf_op jit(solution)/shard_map/ppermute | solution.py:181
  26.2 0.5 collective-permute-start.14
  26.8 2.3 %collective-permute-done.7.refs_6_ = bf16[272,256]{1,0:T(8,128)(2,1)S(1)} collective-permute-done((bf16[272,256]{1,0:T(8,128)(2,1)S(1)}, bf16[272,256]{1,0:T(8,128)(2,1)S(1)}, u32[]{:S(2)}, u32[]{:S(2)}) %collective-permute-start.7) | collective-permute-done | bytes 139296 | tf_op jit(solution)/shard_map/ppermute | solution.py:181
  29.1 1.6 %collective-permute-done.8.refs_7_ = bf16[272,256]{1,0:T(8,128)(2,1)S(1)} collective-permute-done((bf16[272,256]{1,0:T(8,128)(2,1)S(1)}, bf16[272,256]{1,0:T(8,128)(2,1)S(1)}, u32[]{:S(2)}, u32[]{:S(2)}) %collective-permute-start.8) | collective-permute-done | bytes 139296 | tf_op jit(solution)/shard_map/ppermute | solution.py:181
  30.7 0.8 %copy-done.1 = s32[64,128]{1,0:T(8,128)S(1)} copy-done((s32[64,128]{1,0:T(8,128)S(1)}, s32[64,128]{1,0:T(8,128)}, u32[]{:S(2)}) %copy-start.1) | copy-done | bytes 32792
  31.5 4.2 %restart.1.rt_ref = bf16[80,4096]{1,0:T(8,128)(2,1)S(1)} custom-call(s32[1]{0:T(128)} %bitcast.me_ref, s32[64,128]{1,0:T(8,128)S(1)} %copy-done.1), custom_call_target="tpu_custom_call" | custom-call | tf_op jit(solution)/shard_map/restart/pallas_call | solution.py:233
  35.7 14.4 %build.1 = (bf16[4096,2048]{1,0:T(8,128)(2,1)S(1)}, bf16[64,2048]{1,0:T(8,128)(2,1)S(1)}, f32[8,2048]{1,0:T(8,128)S(1)}) custom-call(s32[1]{0:T(128)} %bitcast.me_ref, bf16[80,4096]{1,0:T(8,128)(2,1)S(1)} %restart.1.rt_ref, bf16[272,256]{1,0:T(8,128)(2,1)S(1)} %payload.1.refs_0_, bf16[272,256]{1,0:T(8,128)(2,1)S(1)} %collective-permute-done.refs_1_, ...), custom_call_target="tpu_custom_call" | custom-call | tf_op jit(solution)/shard_map/build/pallas_call | solution.py:243
  50.1 0.6 collective-permute-start.17
  50.7 1.2 %collective-permute-done.17.other_ref = bf16[64,2048]{1,0:T(8,128)(2,1)S(1)} collective-permute-done((bf16[64,2048]{1,0:T(8,128)(2,1)S(1)}, bf16[64,2048]{1,0:T(8,128)(2,1)S(1)}, u32[]{:S(2)}, u32[]{:S(2)}) %collective-permute-start.17) | collective-permute-done | bytes 262176 | tf_op jit(solution)/shard_map/ppermute | solution.py:181
  51.8 3.1 %step.1.mine_ref = bf16[64,2048]{1,0:T(8,128)(2,1)S(1)} custom-call(bf16[80,4096]{1,0:T(8,128)(2,1)S(1)} %restart.1.rt_ref, bf16[4096,2048]{1,0:T(8,128)(2,1)S(1)} %get-tuple-element.8.kt_ref, f32[8,2048]{1,0:T(8,128)S(1)} %get-tuple-element.9.gain_ref, bf16[64,2048]{1,0:T(8,128)(2,1)S(1)} %get-tuple-element.10.mine_ref, ...), custom_call_target="tpu_custom_call" | custom-call | tf_op jit(solution)/shard_map/step/pallas_call | solution.py:262
  55.3 1.2 %collective-permute-done.18.other_ref = bf16[64,2048]{1,0:T(8,128)(2,1)S(1)} collective-permute-done((bf16[64,2048]{1,0:T(8,128)(2,1)S(1)}, bf16[64,2048]{1,0:T(8,128)(2,1)S(1)}, u32[]{:S(2)}, u32[]{:S(2)}) %collective-permute-start.18) | collective-permute-done | bytes 262176 | tf_op jit(solution)/shard_map/ppermute | solution.py:181
  56.5 0.6 %last.1 = f32[256,64]{1,0:T(8,128)S(1)} custom-call(bf16[80,4096]{1,0:T(8,128)(2,1)S(1)} %restart.1.rt_ref, bf16[4096,2048]{1,0:T(8,128)(2,1)S(1)} %get-tuple-element.8.kt_ref, f32[8,2048]{1,0:T(8,128)S(1)} %get-tuple-element.9.gain_ref, bf16[64,2048]{1,0:T(8,128)(2,1)S(1)} %step.1.mine_ref, bf16[64,2048]{1,0:T(8,128)(2,1)S(1)} %collective-permute-done.18.other_ref), custom_call_target="tpu_custom_call" | custom-call | tf_op jit(solution)/shard_map/last/pallas_call | solution.py:270
  57.1 0.7 %copy.5 = f32[256,64]{0,1:T(8,128)} copy(f32[256,64]{1,0:T(8,128)S(1)} %last.1) | data formatting | bytes 131072 | tf_op jit(solution)/shard_map/last/pallas_call | solution.py:270
  (28 shorter events, 1.6 us)
Async XLA Ops:
  0.7 0.9 %copy-start = (bf16[256,256]{1,0:T(8,128)(2,1)S(1)}, bf16[256,256]{1,0:T(8,128)(2,1)}, u32[]{:S(2)}) copy-start(bf16[256,256]{1,0:T(8,128)(2,1)} %emb_ref.1) | copy-start | bytes 393220
  1.6 0.7 %copy-start.2 = (s32[1,1,2,48]{3,2,1,0:T(2,128)S(1)}, s32[1,1,2,48]{3,2,1,0:T(2,128)}, u32[]{:S(2)}) copy-start(s32[1,1,2,48]{3,2,1,0:T(2,128)} %param.5) | copy-start | bytes 1156
  2.4 8.1 %collective-permute-start.1 = (bf16[272,256]{1,0:T(8,128)(2,1)S(1)}, bf16[272,256]{1,0:T(8,128)(2,1)S(1)}, u32[]{:S(2)}, u32[]{:S(2)}) collective-permute-start(bf16[272,256]{1,0:T(8,128)(2,1)S(1)} %payload.1.refs_0_), channel_id=1, source_target_pairs={{0,0},{1,1},{2,2},{3,3},{4,8},{5,9},{6,10},{7,11},{8,4},{9,5},{10,... | collective-permute-start | bytes 417800 | tf_op jit(solution)/shard_map/ppermute | solution.py:181
  3.1 9.7 %collective-permute-start = (bf16[272,256]{1,0:T(8,128)(2,1)S(1)}, bf16[272,256]{1,0:T(8,128)(2,1)S(1)}, u32[]{:S(2)}, u32[]{:S(2)}) collective-permute-start(bf16[272,256]{1,0:T(8,128)(2,1)S(1)} %payload.1.refs_0_), channel_id=1, source_target_pairs={{0,4},{1,5},{2,6},{3,7},{4,0},{5,1},{6,2},{7,3},{8,12},{9,13},{10,... | collective-permute-start | bytes 417800 | tf_op jit(solution)/shard_map/ppermute | solution.py:181
  9.0 5.1 %collective-permute-start.5 = (bf16[272,256]{1,0:T(8,128)(2,1)S(1)}, bf16[272,256]{1,0:T(8,128)(2,1)S(1)}, u32[]{:S(2)}, u32[]{:S(2)}) collective-permute-start(bf16[272,256]{1,0:T(8,128)(2,1)S(1)} %payload.1.refs_0_), channel_id=1, source_target_pairs={{0,2},{1,3},{2,0},{3,1},{4,6},{5,7},{6,4},{7,5},{8,10},{9,11},{10,... | collective-permute-start | bytes 417800 | tf_op jit(solution)/shard_map/ppermute | solution.py:181
  10.5 5.3 %collective-permute-start.2 = (bf16[272,256]{1,0:T(8,128)(2,1)S(1)}, bf16[272,256]{1,0:T(8,128)(2,1)S(1)}, u32[]{:S(2)}, u32[]{:S(2)}) collective-permute-start(bf16[272,256]{1,0:T(8,128)(2,1)S(1)} %collective-permute-done.1), channel_id=1, source_target_pairs={{0,4},{1,5},{2,6},{3,7},{4,0},{5,1},{6,2},{7,3},{8,12},{9,13},{10,... | collective-permute-start | bytes 417800 | tf_op jit(solution)/shard_map/ppermute | solution.py:181
  12.7 3.0 %collective-permute-start.3 = (bf16[272,256]{1,0:T(8,128)(2,1)S(1)}, bf16[272,256]{1,0:T(8,128)(2,1)S(1)}, u32[]{:S(2)}, u32[]{:S(2)}) collective-permute-start(bf16[272,256]{1,0:T(8,128)(2,1)S(1)} %collective-permute-done.refs_1_), channel_id=1, source_target_pairs={{0,0},{1,1},{2,2},{3,3},{4,8},{5,9},{6,10},{7,11},{8,4},{9,5},{10,... | collective-permute-start | bytes 417800 | tf_op jit(solution)/shard_map/ppermute | solution.py:181
  13.4 12.2 %collective-permute-start.9 = (bf16[272,256]{1,0:T(8,128)(2,1)S(1)}, bf16[272,256]{1,0:T(8,128)(2,1)S(1)}, u32[]{:S(2)}, u32[]{:S(2)}) collective-permute-start(bf16[272,256]{1,0:T(8,128)(2,1)S(1)} %payload.1.refs_0_), channel_id=1, source_target_pairs={{0,1},{1,0},{2,3},{3,2},{4,5},{5,4},{6,7},{7,6},{8,9},{9,8},{10,11... | collective-permute-start | bytes 417800 | tf_op jit(solution)/shard_map/ppermute | solution.py:181
  13.5 13.2 %collective-permute-start.10 = (bf16[272,256]{1,0:T(8,128)(2,1)S(1)}, bf16[272,256]{1,0:T(8,128)(2,1)S(1)}, u32[]{:S(2)}, u32[]{:S(2)}) collective-permute-start(bf16[272,256]{1,0:T(8,128)(2,1)S(1)} %collective-permute-done.refs_1_), channel_id=1, source_target_pairs={{0,1},{1,0},{2,3},{3,2},{4,5},{5,4},{6,7},{7,6},{8,9},{9,8},{10,11... | collective-permute-start | bytes 417800 | tf_op jit(solution)/shard_map/ppermute | solution.py:181
  14.0 12.2 %collective-permute-start.6 = (bf16[272,256]{1,0:T(8,128)(2,1)S(1)}, bf16[272,256]{1,0:T(8,128)(2,1)S(1)}, u32[]{:S(2)}, u32[]{:S(2)}) collective-permute-start(bf16[272,256]{1,0:T(8,128)(2,1)S(1)} %collective-permute-done.refs_1_), channel_id=1, source_target_pairs={{0,2},{1,3},{2,0},{3,1},{4,6},{5,7},{6,4},{7,5},{8,10},{9,11},{10,... | collective-permute-start | bytes 417800 | tf_op jit(solution)/shard_map/ppermute | solution.py:181
  15.7 10.4 %collective-permute-start.13 = (bf16[272,256]{1,0:T(8,128)(2,1)S(1)}, bf16[272,256]{1,0:T(8,128)(2,1)S(1)}, u32[]{:S(2)}, u32[]{:S(2)}) collective-permute-start(bf16[272,256]{1,0:T(8,128)(2,1)S(1)} %collective-permute-done.5.refs_4_), channel_id=1, source_target_pairs={{0,1},{1,0},{2,3},{3,2},{4,5},{5,4},{6,7},{7,6},{8,9},{9,8},{10,11... | collective-permute-start | bytes 417800 | tf_op jit(solution)/shard_map/ppermute | solution.py:181
  15.8 8.3 %collective-permute-start.4 = (bf16[272,256]{1,0:T(8,128)(2,1)S(1)}, bf16[272,256]{1,0:T(8,128)(2,1)S(1)}, u32[]{:S(2)}, u32[]{:S(2)}) collective-permute-start(bf16[272,256]{1,0:T(8,128)(2,1)S(1)} %collective-permute-done.3), channel_id=1, source_target_pairs={{0,4},{1,5},{2,6},{3,7},{4,0},{5,1},{6,2},{7,3},{8,12},{9,13},{10,... | collective-permute-start | bytes 417800 | tf_op jit(solution)/shard_map/ppermute | solution.py:181
  24.1 5.1 %collective-permute-start.7 = (bf16[272,256]{1,0:T(8,128)(2,1)S(1)}, bf16[272,256]{1,0:T(8,128)(2,1)S(1)}, u32[]{:S(2)}, u32[]{:S(2)}) collective-permute-start(bf16[272,256]{1,0:T(8,128)(2,1)S(1)} %broadcast_select_fusion.1.refs_2_), channel_id=1, source_target_pairs={{0,2},{1,3},{2,0},{3,1},{4,6},{5,7},{6,4},{7,5},{8,10},{9,11},{10,... | collective-permute-start | bytes 417800 | tf_op jit(solution)/shard_map/ppermute | solution.py:181
  25.6 5.1 %collective-permute-start.8 = (bf16[272,256]{1,0:T(8,128)(2,1)S(1)}, bf16[272,256]{1,0:T(8,128)(2,1)S(1)}, u32[]{:S(2)}, u32[]{:S(2)}) collective-permute-start(bf16[272,256]{1,0:T(8,128)(2,1)S(1)} %broadcast_select_fusion.refs_3_), channel_id=1, source_target_pairs={{0,2},{1,3},{2,0},{3,1},{4,6},{5,7},{6,4},{7,5},{8,10},{9,11},{10,... | collective-permute-start | bytes 417800 | tf_op jit(solution)/shard_map/ppermute | solution.py:181
  26.2 9.5 %collective-permute-start.11 = (bf16[272,256]{1,0:T(8,128)(2,1)S(1)}, bf16[272,256]{1,0:T(8,128)(2,1)S(1)}, u32[]{:S(2)}, u32[]{:S(2)}) collective-permute-start(bf16[272,256]{1,0:T(8,128)(2,1)S(1)} %broadcast_select_fusion.1.refs_2_), channel_id=1, source_target_pairs={{0,1},{1,0},{2,3},{3,2},{4,5},{5,4},{6,7},{7,6},{8,9},{9,8},{10,11... | collective-permute-start | bytes 417800 | tf_op jit(solution)/shard_map/ppermute | solution.py:181
  26.2 9.5 %collective-permute-start.14 = (bf16[272,256]{1,0:T(8,128)(2,1)S(1)}, bf16[272,256]{1,0:T(8,128)(2,1)S(1)}, u32[]{:S(2)}, u32[]{:S(2)}) collective-permute-start(bf16[272,256]{1,0:T(8,128)(2,1)S(1)} %collective-permute-done.6.refs_5_), channel_id=1, source_target_pairs={{0,1},{1,0},{2,3},{3,2},{4,5},{5,4},{6,7},{7,6},{8,9},{9,8},{10,11... | collective-permute-start | bytes 417800 | tf_op jit(solution)/shard_map/ppermute | solution.py:181
  26.7 9.0 %collective-permute-start.12 = (bf16[272,256]{1,0:T(8,128)(2,1)S(1)}, bf16[272,256]{1,0:T(8,128)(2,1)S(1)}, u32[]{:S(2)}, u32[]{:S(2)}) collective-permute-start(bf16[272,256]{1,0:T(8,128)(2,1)S(1)} %broadcast_select_fusion.refs_3_), channel_id=1, source_target_pairs={{0,1},{1,0},{2,3},{3,2},{4,5},{5,4},{6,7},{7,6},{8,9},{9,8},{10,11... | collective-permute-start | bytes 417800 | tf_op jit(solution)/shard_map/ppermute | solution.py:181
  29.1 6.6 %collective-permute-start.15 = (bf16[272,256]{1,0:T(8,128)(2,1)S(1)}, bf16[272,256]{1,0:T(8,128)(2,1)S(1)}, u32[]{:S(2)}, u32[]{:S(2)}) collective-permute-start(bf16[272,256]{1,0:T(8,128)(2,1)S(1)} %collective-permute-done.7.refs_6_), channel_id=1, source_target_pairs={{0,1},{1,0},{2,3},{3,2},{4,5},{5,4},{6,7},{7,6},{8,9},{9,8},{10,11... | collective-permute-start | bytes 417800 | tf_op jit(solution)/shard_map/ppermute | solution.py:181
  30.7 5.0 %collective-permute-start.16 = (bf16[272,256]{1,0:T(8,128)(2,1)S(1)}, bf16[272,256]{1,0:T(8,128)(2,1)S(1)}, u32[]{:S(2)}, u32[]{:S(2)}) collective-permute-start(bf16[272,256]{1,0:T(8,128)(2,1)S(1)} %collective-permute-done.8.refs_7_), channel_id=1, source_target_pairs={{0,1},{1,0},{2,3},{3,2},{4,5},{5,4},{6,7},{7,6},{8,9},{9,8},{10,11... | collective-permute-start | bytes 417800 | tf_op jit(solution)/shard_map/ppermute | solution.py:181
  30.7 0.8 %copy-start.1 = (s32[64,128]{1,0:T(8,128)S(1)}, s32[64,128]{1,0:T(8,128)}, u32[]{:S(2)}) copy-start(s32[64,128]{1,0:T(8,128)} %seeds_ref.1) | copy-start | bytes 98308
  50.1 1.7 %collective-permute-start.17 = (bf16[64,2048]{1,0:T(8,128)(2,1)S(1)}, bf16[64,2048]{1,0:T(8,128)(2,1)S(1)}, u32[]{:S(2)}, u32[]{:S(2)}) collective-permute-start(bf16[64,2048]{1,0:T(8,128)(2,1)S(1)} %get-tuple-element.10.mine_ref), channel_id=1, source_target_pairs={{0,1},{1,0},{2,3},{3,2},{4,5},{5,4},{6,7},{7,6},{8,9},{9,8},{10,11... | collective-permute-start | bytes 786440 | tf_op jit(solution)/shard_map/ppermute | solution.py:181
  54.9 1.6 %collective-permute-start.18 = (bf16[64,2048]{1,0:T(8,128)(2,1)S(1)}, bf16[64,2048]{1,0:T(8,128)(2,1)S(1)}, u32[]{:S(2)}, u32[]{:S(2)}) collective-permute-start(bf16[64,2048]{1,0:T(8,128)(2,1)S(1)} %step.1.mine_ref), channel_id=1, source_target_pairs={{0,1},{1,0},{2,3},{3,2},{4,5},{5,4},{6,7},{7,6},{8,9},{9,8},{10,11... | collective-permute-start | bytes 786440 | tf_op jit(solution)/shard_map/ppermute | solution.py:181

commit v2 on v1

--- a/solution.py
+++ b/solution.py
@@ -32,6 +32,49 @@
     return (widened * factor * widened.shape[-1] ** (-0.5)).astype(BF16)
 
 
+ORDER = ((0, 0), (1, 0), (2, 0), (1, 1), (0, 1), (2, 1), (3, 0), (3, 1))
+PLACE = {block: place for place, block in enumerate(ORDER)}
+OWN_STAGES = (
+    ((0, 0), (1, 0), (0, 1), (2, 0), (1, 1)),
+    ((3, 0), (2, 1)),
+    (),
+    ((3, 1),),
+    (),
+)
+OTHER_STAGES = (
+    ((0, 0), (1, 0), (0, 1)),
+    ((2, 0), (1, 1)),
+    ((3, 0), (2, 1)),
+    (),
+    ((3, 1),),
+)
+
+
+def runs_of(places):
+    found = []
+    for place in sorted(places):
+        if found and found[-1][1] == place:
+            found[-1][1] = place + 1
+        else:
+            found.append([place, place + 1])
+    return found
+
+
+def stage_tasks(stage):
+    here, before = set(), set()
+    for at_stage in range(stage + 1):
+        before = set(here)
+        blocks = [set(sum(names[: at_stage + 1], ())) for names in (OWN_STAGES, OTHER_STAGES)]
+        for target in blocks[0]:
+            for side in (0, 1):
+                for source in blocks[side]:
+                    if (target[0], source[1]) in blocks[side]:
+                        here.add((PLACE[target], side * 8 + PLACE[source]))
+    new = here - before
+    targets = sorted({target for target, _ in new})
+    return [(one, runs_of([source for target, source in new if target == one])) for one in targets]
+
+
 def dot_nt(lhs, rhs):
     return lax.dot_general(lhs, rhs, (((1,), (1,)), ((), ())), preferred_element_type=F32)
 
@@ -40,10 +83,16 @@
     return lax.dot_general(lhs, rhs, (((1,), (0,)), ((), ())), preferred_element_type=F32)
 
 
-def payload_kernel(count_ref, emb_ref, list_ref, out_ref):
+def payload_kernel(count_ref, emb_in, list_in, out_ref, emb_ref, list_ref, sems):
     rows = emb_ref.shape[0]
     width = emb_ref.shape[1]
     slots = list_ref.shape[1]
+    emb_copy = pltpu.make_async_copy(emb_in, emb_ref, sems.at[0])
+    list_copy = pltpu.make_async_copy(list_in, list_ref, sems.at[1])
+    emb_copy.start()
+    list_copy.start()
+    emb_copy.wait()
+    list_copy.wait()
     out_ref[0:rows, :] = normalize(emb_ref[...])
     live = lax.broadcasted_iota(jnp.int32, (1, slots), 1) < count_ref[0, 0]
     col_hot = (lax.broadcasted_iota(jnp.int32, (EXTRA_ROWS, slots), 0) == list_ref[1:2, :]) & live
@@ -57,11 +106,13 @@
     tiles = counts.shape[1]
     me = me_ref[0]
     spot = lax.broadcasted_iota(jnp.int32, (tiles, TILE), 0)
-    kk, xs, zs, half = spot // 16, (spot // 8) % 2, (spot // 2) % 4, spot % 2
-    tile_ids = (me ^ (zs * 4 + xs * 2 + kk)) * 2 + half
+    offset = spot // 16
+    for place, (z, x) in enumerate(ORDER):
+        offset = offset + jnp.where((spot // 2) % 8 == place, 4 * z + 2 * x, 0)
+    tile_ids = (me ^ offset) * 2 + spot % 2
     lows = lax.broadcasted_iota(jnp.int32, (TILE, TILE), 0)
 
-    @pl.loop(0, seed_cols, unroll=4)
+    @pl.loop(0, seed_cols, unroll=16)
     def _(k):
         row = seeds_ref[pl.ds(k, 1), :]
         high_hot = (tile_ids == row // TILE).astype(F32).astype(BF16)
@@ -75,96 +126,103 @@
     out_ref[seed_cols:, :] = first.astype(F32).astype(BF16)
 
 
-def build_kernel(me_ref, rt_ref, *refs):
-    blocks = refs[:16]
-    kt_ref, next_ref, gain_ref, units, masks, bias, sems = refs[16:]
+def stage_kernel(stage, me_ref, rt_ref, *refs):
+    own_names, other_names = OWN_STAGES[stage], OTHER_STAGES[stage]
+    count = len(own_names) + len(other_names)
+    arrivals, refs = refs[:count], refs[count:]
+    if stage > 0:
+        refs = refs[4 if stage == len(OWN_STAGES) - 1 else 5 :]
+    units, bias, kt_ref, total_ref = refs[:4]
+    refs = refs[4:]
     me = me_ref[0]
     core, x_pos, z_pos = me % 2, (me // 2) % 2, me // 4
     rows = units.shape[0] // 16
-    copies = []
-    for s in range(16):
-        copies.append(
-            (
-                pltpu.make_async_copy(
-                    blocks[s].at[pl.ds(0, rows)], units.at[pl.ds(s * rows, rows)], sems.at[2 * s]
-                ),
-                pltpu.make_async_copy(
-                    blocks[s].at[pl.ds(rows, EXTRA_ROWS)],
-                    masks.at[pl.ds(s * EXTRA_ROWS, EXTRA_ROWS)],
-                    sems.at[2 * s + 1],
-                ),
-            )
+    names = [(0, one) for one in own_names] + [(1, one) for one in other_names]
+    for (side, one), ref in zip(names, arrivals):
+        place = side * 8 + PLACE[one]
+        units[place * rows : (place + 1) * rows] = ref[0:rows]
+    if names:
+        pick_row = lax.broadcasted_iota(jnp.int32, (TILE, 4 * TILE), 0)
+        pick_col = lax.broadcasted_iota(jnp.int32, (TILE, 4 * TILE), 1) // TILE
+        wanted = 4 * (x_pos ^ (pick_col // 2)) + 2 * core + pick_col % 2
+        pick = (pick_row == wanted).astype(F32).astype(BF16)
+        tables = jnp.concatenate(
+            [ref[rows : rows + EXTRA_ROWS, 0:TILE] for ref in arrivals], axis=0
         )
-    for one, two in copies:
-        two.start()
-    for one, two in copies:
-        one.start()
-    for one, two in copies:
-        two.wait()
-    width = masks.shape[1]
-    pick_row = lax.broadcasted_iota(jnp.int32, (width, 512), 0)
-    pick_col = lax.broadcasted_iota(jnp.int32, (width, 512), 1) // TILE
-    wanted = 4 * (x_pos ^ (pick_col // 2)) + 2 * core + pick_col % 2
-    pick = (pick_row == wanted).astype(F32).astype(BF16)
-    spread_mask = dot_nn(masks[...], pick)
-    spread_bias = jnp.where(spread_mask > 0.5, -SLOPE, DEAD)
-    for group in range(4):
-        for zs in range(4):
-            cell = group * 4 + zs
+        live = jnp.where(dot_nn(tables, pick) > 0.5, -SLOPE, DEAD)
+        for at, (side, (z, x)) in enumerate(names):
+            group = (side * 2 + x) * 8
             for xs in range(2):
-                lane = (xs * 4 + zs) * rows
-                bias[group * 8 : group * 8 + 8, lane : lane + rows] = spread_bias[
-                    cell * EXTRA_ROWS : cell * EXTRA_ROWS + 8, xs * rows : (xs + 1) * rows
+                lane = PLACE[(z, xs)] * rows
+                bias[group : group + 8, lane : lane + rows] = live[
+                    at * EXTRA_ROWS : at * EXTRA_ROWS + 8, xs * rows : (xs + 1) * rows
                 ]
-    for one, two in copies:
-        one.wait()
-    own = 8 * rows
+    if stage == 0:
+        total_ref[...] = jnp.zeros_like(total_ref)
+    for target, spans in stage_tasks(stage):
+        lanes = slice(target * rows, (target + 1) * rows)
+        for low, high in spans:
+            inner = dot_nt(units[low * rows : high * rows, :], units[lanes, :])
+            for tile in range((high - low) * rows // TILE):
+                source = low + tile // 2
+                z, x = ORDER[source % 8]
+                bias_row = (source // 8 * 2 + x) * 8 + 2 * (z_pos ^ z) + tile % 2
+                shift = bias[pl.ds(bias_row, 1), lanes]
+                value = jnp.exp2(inner[tile * TILE : (tile + 1) * TILE] * SLOPE + shift)
+                kt_ref[low * rows + tile * TILE : low * rows + (tile + 1) * TILE, lanes] = value.astype(BF16)
+        total = total_ref[:, lanes]
+        for low, high in spans:
+            total = total + dot_nn(rt_ref[:, low * rows : high * rows], kt_ref[low * rows : high * rows, lanes])
+        total_ref[:, lanes] = total
+    if stage < len(OWN_STAGES) - 1:
+        refs[0][...] = jnp.zeros_like(refs[0])
+        return
+    next_ref, gain_ref = refs
+    seed_cols = next_ref.shape[0]
     chunk = 512
-
-    @pl.loop(0, 16)
-    def _(s):
-        group, zs = s // 4, s % 4
-        start = pl.multiple_of(s * rows, rows)
-        source = units[pl.ds(start, rows), :]
-        bias_row = group * 8 + 2 * (z_pos ^ zs)
-        for c in range(own // chunk):
-            lanes = slice(c * chunk, (c + 1) * chunk)
-            inner = dot_nt(source, units[lanes, :])
-            for half in range(rows // TILE):
-                shift = bias[pl.ds(bias_row + half, 1), lanes]
-                value = jnp.exp2(inner[half * TILE : (half + 1) * TILE] * SLOPE + shift)
-                kt_ref[pl.ds(pl.multiple_of(start + half * TILE, TILE), TILE), lanes] = value.astype(BF16)
-
-    seed_cols = next_ref.shape[0]
-    for c in range(own // chunk):
+    for c in range(next_ref.shape[1] // chunk):
         lanes = slice(c * chunk, (c + 1) * chunk)
-        total = dot_nn(rt_ref[...], kt_ref[:, lanes])
-        gain = DAMPING / total[seed_cols : seed_cols + 8]
+        gain = DAMPING / total_ref[seed_cols : seed_cols + 8, lanes]
         gain_ref[:, lanes] = gain
         next_ref[:, lanes] = (
-            (1.0 - DAMPING) * rt_ref[0:seed_cols, lanes].astype(F32) + total[0:seed_cols] * gain[0:1]
+            (1.0 - DAMPING) * rt_ref[0:seed_cols, lanes].astype(F32) + total_ref[0:seed_cols, lanes] * gain[0:1]
         ).astype(BF16)
 
 
-def step_kernel(rt_ref, kt_ref, gain_ref, mine_ref, other_ref, out_ref):
-    seed_cols = out_ref.shape[0]
-    own = out_ref.shape[1]
+def padded(ranks):
+    return jnp.concatenate([ranks, jnp.zeros_like(ranks)], axis=0)
+
+
+def half_kernel(kt_ref, mine_ref, out_ref):
+    seed_cols, own = mine_ref.shape
+    mine = padded(mine_ref[...])
     chunk = 512
     for c in range(own // chunk):
         lanes = slice(c * chunk, (c + 1) * chunk)
-        total = dot_nn(mine_ref[...], kt_ref[0:own, lanes]) + dot_nn(other_ref[...], kt_ref[own:, lanes])
+        out_ref[:, lanes] = dot_nn(mine, kt_ref[0:own, lanes])[0:seed_cols]
+
+
+def step_kernel(rt_ref, kt_ref, gain_ref, half_ref, other_ref, out_ref):
+    seed_cols, own = out_ref.shape
+    other = padded(other_ref[...])
+    chunk = 512
+    for c in range(own // chunk):
+        lanes = slice(c * chunk, (c + 1) * chunk)
+        total = half_ref[:, lanes] + dot_nn(other, kt_ref[own:, lanes])[0:seed_cols]
         out_ref[:, lanes] = (
             (1.0 - DAMPING) * rt_ref[0:seed_cols, lanes].astype(F32) + total * gain_ref[0:1, lanes]
         ).astype(BF16)
 
 
 def last_kernel(rt_ref, kt_ref, gain_ref, mine_ref, other_ref, out_ref):
-    seed_cols = out_ref.shape[1]
-    rows = out_ref.shape[0]
+    seed_cols, rows = out_ref.shape
     own = mine_ref.shape[1]
-    total = dot_nn(mine_ref[...], kt_ref[0:own, 0:rows]) + dot_nn(other_ref[...], kt_ref[own:, 0:rows])
-    ranks = (1.0 - DAMPING) * rt_ref[0:seed_cols, 0:rows].astype(F32) + total * gain_ref[0:1, 0:rows]
-    out_ref[...] = ranks.T
+    total = dot_nn(padded(mine_ref[...]), kt_ref[0:own, 0:rows]) + dot_nn(
+        padded(other_ref[...]), kt_ref[own:, 0:rows]
+    )
+    out_ref[...] = (1.0 - DAMPING) * rt_ref[0:seed_cols, 0:rows].astype(F32) + total[
+        0:seed_cols
+    ] * gain_ref[0:1, 0:rows]
 
 
 WHOLE = pl.BlockSpec(memory_space=pltpu.VMEM)
@@ -176,18 +234,21 @@
     return pltpu.CompilerParams(vmem_limit_bytes=20 * 2**20)
 
 
+def work(micros):
+    return pl.CostEstimate(flops=int(micros * 1e9), bytes_accessed=int(micros * 3e6), transcendentals=0)
+
+
 def swap(array, mapping):
     pairs = [(device, mapping(device)) for device in range(16)]
     return lax.ppermute(array, ("row", "col"), pairs)
 
 
-def outer_pair(device):
+def near(device):
     return device ^ 4
 
 
-def inner_pair(device):
-    z = device // 4
-    return device ^ 12 if z in (1, 2) else device
+def far(device):
+    return device ^ 8
 
 
 def across(device):
@@ -208,73 +269,110 @@
     slots = tile_list.shape[3]
     block = pl.pallas_call(
         payload_kernel,
-        in_specs=[SCALARS, WHOLE, WHOLE],
+        in_specs=[SCALARS, REMAIN, REMAIN],
         out_specs=WHOLE,
         out_shape=jax.ShapeDtypeStruct((rows + EXTRA_ROWS, width), BF16),
+        scratch_shapes=[
+            pltpu.VMEM((rows, width), BF16),
+            pltpu.VMEM((2, slots), jnp.int32),
+            pltpu.SemaphoreType.DMA((2,)),
+        ],
         compiler_params=params(),
         name="payload",
     )(tile_count, embeddings, tile_list.reshape(2, slots))
 
-    is_end = (row_pos == 0) | (row_pos == 3)
-    z1 = swap(block, outer_pair)
-    near = swap(block, inner_pair)
+    state_shapes = [
+        pltpu.VMEM((sessions, width), BF16),
+        pltpu.VMEM((32, own), F32),
+        pltpu.VMEM((sessions, own), BF16),
+        pltpu.VMEM((2 * seed_cols, own), F32),
+    ]
+    mark = [jax.ShapeDtypeStruct((8, TILE), F32)]
+
+    def run_stage(stage, rt, arrivals, state, extra, *after):
+        first_state = 2 + len(arrivals)
+        outs = pl.pallas_call(
+            functools.partial(stage_kernel, stage),
+            in_specs=[SCALARS] + [WHOLE] * (1 + len(arrivals) + len(state)) + [REMAIN] * len(after),
+            out_specs=[WHOLE] * (4 + len(extra)),
+            out_shape=state_shapes + extra,
+            input_output_aliases={first_state + k: k for k in range(len(state))},
+            compiler_params=params(),
+            cost_estimate=work(2.5),
+            name=f"stage{stage}",
+        )(me, rt, *arrivals, *state, *after)
+        return outs[:4], outs[4:]
+
+    z2 = swap(block, far)
+    z1 = swap(block, near)
     x0 = swap(block, across)
-    far_a = swap(near, outer_pair)
-    far_b = swap(z1, inner_pair)
+    b00 = swap(block, sibling)
     x1 = swap(z1, across)
-    z2 = jnp.where(is_end, far_a, far_b)
-    last = swap(far_b, outer_pair)
-    x2 = swap(z2, across)
-    z3 = jnp.where(is_end, last, near)
-    x3 = swap(z3, across)
-    mine = [block, z1, z2, z3, x0, x1, x2, x3]
-    other = [swap(one, sibling) for one in mine]
-
+    b10 = swap(z1, sibling)
+    b01 = swap(x0, sibling)
+    seeds, z1, x0 = lax.optimization_barrier((seeds, z1, x0))
     rt = pl.pallas_call(
         restart_kernel,
         in_specs=[SCALARS, WHOLE],
         out_specs=WHOLE,
-        out_shape=jax.ShapeDtypeStruct((seed_cols + 16, sessions), BF16),
+        out_shape=jax.ShapeDtypeStruct((2 * seed_cols, sessions), BF16),
         scratch_shapes=[pltpu.VMEM((seed_cols, sessions // TILE, TILE), F32)],
         compiler_params=params(),
+        cost_estimate=work(2.6),
         name="restart",
     )(me, seeds)
-
-    kt, ranks, gain = pl.pallas_call(
-        build_kernel,
-        in_specs=[SCALARS, WHOLE] + [REMAIN] * 16,
-        out_specs=[WHOLE] * 3,
-        out_shape=[
-            pltpu.VMEM((sessions, own), BF16),
-            jax.ShapeDtypeStruct((seed_cols, own), BF16),
-            jax.ShapeDtypeStruct((8, own), F32),
-        ],
-        scratch_shapes=[
-            pltpu.VMEM((sessions, width), BF16),
-            pltpu.VMEM((16 * EXTRA_ROWS, width), BF16),
-            pltpu.VMEM((32, own), F32),
-            pltpu.SemaphoreType.DMA((32,)),
-        ],
-        compiler_params=params(),
-        name="build",
-    )(me, rt, *mine, *other)
+    z2, x1, b00, b10, b01, rt = lax.optimization_barrier((z2, x1, b00, b10, b01, rt))
+    z3 = swap(z2, near)
+    x2 = swap(z2, across)
+    b20 = swap(z2, sibling)
+    b11 = swap(x1, sibling)
+    state, (done,) = run_stage(0, rt, [block, z1, x0, z2, x1, b00, b10, b01], [], mark)
+    z3, x2, done = lax.optimization_barrier((z3, x2, done))
+    x3 = swap(z3, across)
+    b30 = swap(z3, sibling)
+    b21 = swap(x2, sibling)
+    state, (done,) = run_stage(1, rt, [z3, x2, b20, b11], state, mark, done)
+    state, (done,) = run_stage(2, rt, [b30, b21], state, mark, done)
+    x3, done = lax.optimization_barrier((x3, done))
+    b31 = swap(x3, sibling)
+    state, (done,) = run_stage(3, rt, [x3], state, mark, done)
+    state, (ranks, gain) = run_stage(
+        4,
+        rt,
+        [b31],
+        state,
+        [jax.ShapeDtypeStruct((seed_cols, own), BF16), jax.ShapeDtypeStruct((8, own), F32)],
+    )
+    kt = state[2]
     for sweep in range(ITERS - 2):
+        half = pl.pallas_call(
+            half_kernel,
+            in_specs=[WHOLE] * 2,
+            out_specs=WHOLE,
+            out_shape=jax.ShapeDtypeStruct((seed_cols, own), F32),
+            compiler_params=params(),
+            cost_estimate=work(1.5),
+            name="half",
+        )(kt, ranks)
         ranks = pl.pallas_call(
             step_kernel,
             in_specs=[WHOLE] * 5,
             out_specs=WHOLE,
             out_shape=jax.ShapeDtypeStruct((seed_cols, own), BF16),
             compiler_params=params(),
+            cost_estimate=work(1.5),
             name="step",
-        )(rt, kt, gain, ranks, swap(ranks, sibling))
-    return pl.pallas_call(
+        )(rt, kt, gain, half, swap(ranks, sibling))
+    result = pl.pallas_call(
         last_kernel,
         in_specs=[WHOLE] * 5,
         out_specs=WHOLE,
-        out_shape=jax.ShapeDtypeStruct((rows, seed_cols), F32),
+        out_shape=jax.ShapeDtypeStruct((seed_cols, rows), F32),
         compiler_params=params(),
+        cost_estimate=work(0.5),
         name="last",
     )(rt, kt, gain, ranks, swap(ranks, sibling))
+    return result.T
 
 
 def block_width():

time: 58.1 us -> 41.6 us (0.72)
  starting transfers between devices: 22 us -> 12.5 us
  Pallas kernels: 22.4 us -> 19.1 us
  waiting for transfers between devices: 9.59 us -> 6.55 us
  local copies, waits for them, and re-layouts: 3.05 us -> 2.33 us
    ppermute x19 -> x17, starting transfers between devices: 22 us -> 12.5 us  [swap(): return lax.ppermute(array, ('row', 'col'), pairs)]
    ppermute x19 -> x17, waiting for transfers between devices: 9.59 us -> 6.55 us  [swap(): return lax.ppermute(array, ('row', 'col'), pairs)]
    pallas_call x1, Pallas kernels: 3.08 us -> 1.33 us  [chip_local(): pl.pallas_call(step_kernel, in_specs=[WHOLE] * 5, out_specs=WHOLE, out_sh...]
    pallas_call x1, Pallas kernels: 4.18 us -> 2.7 us  [chip_local(): pl.pallas_call(restart_kernel, in_specs=[SCALARS, WHOLE], out_specs=WHOLE...]
    pallas_call x1 -> x0, local copies, waits for them, and re-layouts: 0.71 us -> none  [chip_local(): pl.pallas_call(last_kernel, in_specs=[WHOLE] * 5, out_specs=WHOLE, out_sh...]
    pallas_call x2 -> x7, Pallas kernels: 14.5 us -> 14 us  [the longest x5 12.2 us: run_stage(): pl.pallas_call(functools.partial(stage_kernel, stage), in_specs=[SCALARS]...]
  transfers between devices with their start and end apart: 19 -> 17, of which waited for: 7 -> 5; matrix products, arithmetic and copies ran while one was open for 0% -> 0% of each run, Pallas kernels for 7% -> 35%
where the time goes in v2:
time: 41.6 us; the launch traced here: 41.3 us
  Pallas kernels  19.1 us (46%)
  starting transfers between devices  12.5 us (30%)
  waiting for transfers between devices  6.55 us (16%)
  local copies, waits for them, and re-layouts  2.33 us (6%)
  between operations  0.79 us (2%)
    ppermute x17, starting transfers between devices, swap(): return lax.ppermute(array, ('row', 'col'), pairs)  12.5 us
    pallas_call x5, Pallas kernels, run_stage(): pl.pallas_call(functools.partial(stage_kernel, stage), in_specs=[SCALARS]...  12.2 us
    ppermute x17, waiting for transfers between devices, swap(): return lax.ppermute(array, ('row', 'col'), pairs)  6.55 us
    pallas_call x1, Pallas kernels, chip_local(): pl.pallas_call(restart_kernel, in_specs=[SCALARS, WHOLE], out_specs=WHOLE...  2.7 us
    unnamed x6, local copies, waits for them, and re-layouts  2.33 us
    pallas_call x1, Pallas kernels, chip_local(): pl.pallas_call(half_kernel, in_specs=[WHOLE] * 2, out_specs=WHOLE, out_sh...  1.48 us
    pallas_call x1, Pallas kernels, chip_local(): pl.pallas_call(step_kernel, in_specs=[WHOLE] * 5, out_specs=WHOLE, out_sh...  1.33 us
    pallas_call x1, Pallas kernels, chip_local(): pl.pallas_call(last_kernel, in_specs=[WHOLE] * 5, out_specs=WHOLE, out_sh...  1.1 us
  transfers between devices with their start and end apart: 17, of which 5 were waited for; matrix products, arithmetic and copies ran while one was open for 0% of the time, Pallas kernels for 35%

profile of v2, /device:TPU:0, one launch (start us, length us, event | category | flops | bytes accessed | tf_op | source)
XLA Modules:
  0.0 41.3 jit_solution(2550717236431660609)
XLA Ops:
  0.7 0.9 %copy-done = bf16[256,256]{1,0:T(8,128)(2,1)S(1)} copy-done((bf16[256,256]{1,0:T(8,128)(2,1)S(1)}, bf16[256,256]{1,0:T(8,128)(2,1)}, u32[]{:S(2)}) %copy-start) | copy-done | bytes 131096
  1.6 0.7 %copy-done.1 = s32[1,1,2,48]{3,2,1,0:T(2,128)S(1)} copy-done((s32[1,1,2,48]{3,2,1,0:T(2,128)S(1)}, s32[1,1,2,48]{3,2,1,0:T(2,128)}, u32[]{:S(2)}) %copy-start.1) | copy-done | bytes 408
  2.6 3.0 %collective-permute-start.5 = (bf16[272,256]{1,0:T(8,128)(2,1)S(1)}, bf16[272,256]{1,0:T(8,128)(2,1)S(1)}, u32[]{:S(2)}, u32[]{:S(2)}) collective-permute-start(bf16[272,256]{1,0:T(8,128)(2,1)S(1)} %payload.1.refs_0_), channel_id=1, source_target_pairs={{0,2},{1,3},{2,0},{3,1},{4,6},{5,7},{6,4},{7,5},{8,10},{9,11},{10,... | collective-permute-start | bytes 417800 | tf_op jit(solution)/shard_map/ppermute | solution.py:243
  5.6 1.6 %collective-permute-start.1 = (bf16[272,256]{1,0:T(8,128)(2,1)S(1)}, bf16[272,256]{1,0:T(8,128)(2,1)S(1)}, u32[]{:S(2)}, u32[]{:S(2)}) collective-permute-start(bf16[272,256]{1,0:T(8,128)(2,1)S(1)} %payload.1.refs_0_), channel_id=1, source_target_pairs={{0,4},{1,5},{2,6},{3,7},{4,0},{5,1},{6,2},{7,3},{8,12},{9,13},{10,... | collective-permute-start | bytes 417800 | tf_op jit(solution)/shard_map/ppermute | solution.py:243
  7.1 2.6 %collective-permute-start = (bf16[272,256]{1,0:T(8,128)(2,1)S(1)}, bf16[272,256]{1,0:T(8,128)(2,1)S(1)}, u32[]{:S(2)}, u32[]{:S(2)}) collective-permute-start(bf16[272,256]{1,0:T(8,128)(2,1)S(1)} %payload.1.refs_0_), channel_id=1, source_target_pairs={{0,8},{1,9},{2,10},{3,11},{4,12},{5,13},{6,14},{7,15},{8,0},{9,1},... | collective-permute-start | bytes 417800 | tf_op jit(solution)/shard_map/ppermute | solution.py:243
  9.7 1.0 %collective-permute-done.1.refs_1_ = bf16[272,256]{1,0:T(8,128)(2,1)S(1)} collective-permute-done((bf16[272,256]{1,0:T(8,128)(2,1)S(1)}, bf16[272,256]{1,0:T(8,128)(2,1)S(1)}, u32[]{:S(2)}, u32[]{:S(2)}) %collective-permute-start.1) | collective-permute-done | bytes 139296 | tf_op jit(solution)/shard_map/ppermute | solution.py:243
  10.7 0.5 %collective-permute-start.4 = (bf16[272,256]{1,0:T(8,128)(2,1)S(1)}, bf16[272,256]{1,0:T(8,128)(2,1)S(1)}, u32[]{:S(2)}, u32[]{:S(2)}) collective-permute-start(bf16[272,256]{1,0:T(8,128)(2,1)S(1)} %collective-permute-done.1.refs_1_), channel_id=1, source_target_pairs={{0,1},{1,0},{2,3},{3,2},{4,5},{5,4},{6,7},{7,6},{8,9},{9,8},{10,11... | collective-permute-start | bytes 417800 | tf_op jit(solution)/shard_map/ppermute | solution.py:243
  11.2 0.4 collective-permute-start.2
  11.6 0.8 %copy-done.2 = s32[64,128]{1,0:T(8,128)S(1)} copy-done((s32[64,128]{1,0:T(8,128)S(1)}, s32[64,128]{1,0:T(8,128)}, u32[]{:S(2)}) %copy-start.2) | copy-done | bytes 32792
  12.3 2.7 %restart.1.rt_ref = bf16[128,4096]{1,0:T(8,128)(2,1)S(1)} custom-call(s32[1]{0:T(128)} %bitcast.1.me_ref, s32[64,128]{1,0:T(8,128)S(1)} %copy-done.2), custom_call_target="tpu_custom_call" | custom-call | flops 2600000000 | bytes 7800000 | tf_op jit(solution)/shard_map/restart/pallas_call | solution.py:314
  15.0 2.1 %collective-permute-done.refs_3_ = bf16[272,256]{1,0:T(8,128)(2,1)S(1)} collective-permute-done((bf16[272,256]{1,0:T(8,128)(2,1)S(1)}, bf16[272,256]{1,0:T(8,128)(2,1)S(1)}, u32[]{:S(2)}, u32[]{:S(2)}) %collective-permute-start) | collective-permute-done | bytes 139296 | tf_op jit(solution)/shard_map/ppermute | solution.py:243
  17.2 0.6 %collective-permute-start.8 = (bf16[272,256]{1,0:T(8,128)(2,1)S(1)}, bf16[272,256]{1,0:T(8,128)(2,1)S(1)}, u32[]{:S(2)}, u32[]{:S(2)}) collective-permute-start(bf16[272,256]{1,0:T(8,128)(2,1)S(1)} %collective-permute-done.refs_3_), channel_id=1, source_target_pairs={{0,2},{1,3},{2,0},{3,1},{4,6},{5,7},{6,4},{7,5},{8,10},{9,11},{10,... | collective-permute-start | bytes 417800 | tf_op jit(solution)/shard_map/ppermute | solution.py:243
  17.8 1.1 %collective-permute-start.7 = (bf16[272,256]{1,0:T(8,128)(2,1)S(1)}, bf16[272,256]{1,0:T(8,128)(2,1)S(1)}, u32[]{:S(2)}, u32[]{:S(2)}) collective-permute-start(bf16[272,256]{1,0:T(8,128)(2,1)S(1)} %collective-permute-done.refs_3_), channel_id=1, source_target_pairs={{0,4},{1,5},{2,6},{3,7},{4,0},{5,1},{6,2},{7,3},{8,12},{9,13},{10,... | collective-permute-start | bytes 417800 | tf_op jit(solution)/shard_map/ppermute | solution.py:243
  18.9 2.4 %stage0.1 = (bf16[4096,256]{1,0:T(8,128)(2,1)S(1)}, f32[32,2048]{1,0:T(8,128)S(1)}, bf16[4096,2048]{1,0:T(8,128)(2,1)S(1)}, f32[128,2048]{1,0:T(8,128)S(1)}, f32[8,128]{1,0:T(8,128)S(1)}) custom-call(s32[1]{0:T(128)} %bitcast.1.me_ref, bf16[128,4096]{1,0:T(8,128)(2,1)S(1)} %restart.1.rt_ref, bf16[272,256]{1,0:T(8,128)(2,1)S(1)} %payload.1.refs_0_, ...), custom_call_target="tpu_custom_call" | custom-call | flops 2500000000 | bytes 7500000 | tf_op jit(solution)/shard_map/stage0/pallas_call | solution.py:294
  21.3 2.0 %collective-permute-done.8.refs_1_ = bf16[272,256]{1,0:T(8,128)(2,1)S(1)} collective-permute-done((bf16[272,256]{1,0:T(8,128)(2,1)S(1)}, bf16[272,256]{1,0:T(8,128)(2,1)S(1)}, u32[]{:S(2)}, u32[]{:S(2)}) %collective-permute-start.8) | collective-permute-done | bytes 139296 | tf_op jit(solution)/shard_map/ppermute | solution.py:243
  23.5 1.5 %collective-permute-start.9 = (bf16[272,256]{1,0:T(8,128)(2,1)S(1)}, bf16[272,256]{1,0:T(8,128)(2,1)S(1)}, u32[]{:S(2)}, u32[]{:S(2)}) collective-permute-start(bf16[272,256]{1,0:T(8,128)(2,1)S(1)} %collective-permute-done.7.refs_0_), channel_id=1, source_target_pairs={{0,2},{1,3},{2,0},{3,1},{4,6},{5,7},{6,4},{7,5},{8,10},{9,11},{10,... | collective-permute-start | bytes 417800 | tf_op jit(solution)/shard_map/ppermute | solution.py:243
  25.3 2.9 %stage1.1 = (bf16[4096,256]{1,0:T(8,128)(2,1)S(1)}, f32[32,2048]{1,0:T(8,128)S(1)}, bf16[4096,2048]{1,0:T(8,128)(2,1)S(1)}, f32[128,2048]{1,0:T(8,128)S(1)}, f32[8,128]{1,0:T(8,128)S(1)}) custom-call(s32[1]{0:T(128)} %bitcast.1.me_ref, bf16[128,4096]{1,0:T(8,128)(2,1)S(1)} %restart.1.rt_ref, ...), custom_call_target="tpu_custom_call", output_to_operand_aliasing={{0}: (6, {}), {1}: (7, {}), {2}: (8, {}), {3}: (9, {})} | custom-call | flops 2500000000 | bytes 7500000 | tf_op jit(solution)/shard_map/stage1/pallas_call | solution.py:294
  28.2 2.3 %stage2.1 = (bf16[4096,256]{1,0:T(8,128)(2,1)S(1)}, f32[32,2048]{1,0:T(8,128)S(1)}, bf16[4096,2048]{1,0:T(8,128)(2,1)S(1)}, f32[128,2048]{1,0:T(8,128)S(1)}, f32[8,128]{1,0:T(8,128)S(1)}) custom-call(s32[1]{0:T(128)} %bitcast.1.me_ref, bf16[128,4096]{1,0:T(8,128)(2,1)S(1)} %restart.1.rt_ref, ...), custom_call_target="tpu_custom_call", output_to_operand_aliasing={{0}: (4, {}), {1}: (5, {}), {2}: (6, {}), {3}: (7, {})} | custom-call | flops 2500000000 | bytes 7500000 | tf_op jit(solution)/shard_map/stage2/pallas_call | solution.py:294
  30.9 2.7 %stage3.1 = (bf16[4096,256]{1,0:T(8,128)(2,1)S(1)}, f32[32,2048]{1,0:T(8,128)S(1)}, bf16[4096,2048]{1,0:T(8,128)(2,1)S(1)}, f32[128,2048]{1,0:T(8,128)S(1)}, f32[8,128]{1,0:T(8,128)}) custom-call(s32[1]{0:T(128)} %bitcast.1.me_ref, bf16[128,4096]{1,0:T(8,128)(2,1)S(1)} %restart.1.rt_ref, ...), custom_call_target="tpu_custom_call", output_to_operand_aliasing={{0}: (3, {}), {1}: (4, {}), {2}: (5, {}), {3}: (6, {})} | custom-call | flops 2500000000 | bytes 7500000 | tf_op jit(solution)/shard_map/stage3/pallas_call | solution.py:294
  33.6 1.9 %stage4.1 = (bf16[4096,256]{1,0:T(8,128)(2,1)S(1)}, f32[32,2048]{1,0:T(8,128)S(1)}, bf16[4096,2048]{1,0:T(8,128)(2,1)S(1)}, f32[128,2048]{1,0:T(8,128)S(1)}, bf1...) custom-call(s32[1]{0:T(128)} %bitcast.1.me_ref, ...), custom_call_target="tpu_custom_call", output_to_operand_aliasing={{0}: (3, {}), {1}: (4, {}), {2}: (5, {}), {3}: (6, {})} | custom-call | flops 2500000000 | bytes 7500000 | tf_op jit(solution)/shard_map/stage4/pallas_call | solution.py:294
  35.8 1.5 %half.1.half_ref = f32[64,2048]{1,0:T(8,128)S(1)} custom-call(bf16[4096,2048]{1,0:T(8,128)(2,1)S(1)} %get-tuple-element.74.kt_ref, bf16[64,2048]{1,0:T(8,128)(2,1)S(1)} %get-tuple-element.76.mine_ref), custom_call_target="tpu_custom_call" | custom-call | flops 1500000000 | bytes 4500000 | tf_op jit(solution)/shard_map/half/pallas_call | solution.py:348
  37.3 1.3 %step.1.mine_ref = bf16[64,2048]{1,0:T(8,128)(2,1)S(1)} custom-call(bf16[128,4096]{1,0:T(8,128)(2,1)S(1)} %restart.1.rt_ref, bf16[4096,2048]{1,0:T(8,128)(2,1)S(1)} %get-tuple-element.74.kt_ref, f32[8,2048]{1,0:T(8,128)S(1)} %get-tuple-element.75.gain_ref, f32[64,2048]{1,0:T(8,128)S(1)} %half.1.half_ref, bf16[64,2048]{1,0:T(8,128)(2,1)S(1)} %collective-permute-done.15.other_ref), custom_call_target="tpu_custom_call" | custom-call | flops 1500000000 | bytes 4500000 | tf_op jit(solution)/shard_map/step/pallas_call | solution.py:357
  39.0 1.2 %collective-permute-done.16.other_ref = bf16[64,2048]{1,0:T(8,128)(2,1)S(1)} collective-permute-done((bf16[64,2048]{1,0:T(8,128)(2,1)S(1)}, bf16[64,2048]{1,0:T(8,128)(2,1)S(1)}, u32[]{:S(2)}, u32[]{:S(2)}) %collective-permute-start.16) | collective-permute-done | bytes 262176 | tf_op jit(solution)/shard_map/ppermute | solution.py:243
  40.2 1.1 %last.1 = f32[64,256]{1,0:T(8,128)} custom-call(bf16[128,4096]{1,0:T(8,128)(2,1)S(1)} %restart.1.rt_ref, bf16[4096,2048]{1,0:T(8,128)(2,1)S(1)} %get-tuple-element.74.kt_ref, f32[8,2048]{1,0:T(8,128)S(1)} %get-tuple-element.75.gain_ref, bf16[64,2048]{1,0:T(8,128)(2,1)S(1)} %step.1.mine_ref, bf16[64,2048]{1,0:T(8,128)(2,1)S(1)} %collective-permute-done.16.other_ref), custom_call_target="tpu_custom_call" | custom-call | flops 500000000 | bytes 1500000 | tf_op jit(solution)/shard_map/last/pallas_call | solution.py:366
  (26 shorter events, 1.9 us)
Async XLA Ops:
  0.7 0.9 %copy-start = (bf16[256,256]{1,0:T(8,128)(2,1)S(1)}, bf16[256,256]{1,0:T(8,128)(2,1)}, u32[]{:S(2)}) copy-start(bf16[256,256]{1,0:T(8,128)(2,1)} %emb_in.1) | copy-start | bytes 393220
  1.6 0.7 %copy-start.1 = (s32[1,1,2,48]{3,2,1,0:T(2,128)S(1)}, s32[1,1,2,48]{3,2,1,0:T(2,128)}, u32[]{:S(2)}) copy-start(s32[1,1,2,48]{3,2,1,0:T(2,128)} %param.5) | copy-start | bytes 1156
  2.6 7.2 %collective-permute-start.5 = (bf16[272,256]{1,0:T(8,128)(2,1)S(1)}, bf16[272,256]{1,0:T(8,128)(2,1)S(1)}, u32[]{:S(2)}, u32[]{:S(2)}) collective-permute-start(bf16[272,256]{1,0:T(8,128)(2,1)S(1)} %payload.1.refs_0_), channel_id=1, source_target_pairs={{0,2},{1,3},{2,0},{3,1},{4,6},{5,7},{6,4},{7,5},{8,10},{9,11},{10,... | collective-permute-start | bytes 417800 | tf_op jit(solution)/shard_map/ppermute | solution.py:243
  5.6 5.1 %collective-permute-start.1 = (bf16[272,256]{1,0:T(8,128)(2,1)S(1)}, bf16[272,256]{1,0:T(8,128)(2,1)S(1)}, u32[]{:S(2)}, u32[]{:S(2)}) collective-permute-start(bf16[272,256]{1,0:T(8,128)(2,1)S(1)} %payload.1.refs_0_), channel_id=1, source_target_pairs={{0,4},{1,5},{2,6},{3,7},{4,0},{5,1},{6,2},{7,3},{8,12},{9,13},{10,... | collective-permute-start | bytes 417800 | tf_op jit(solution)/shard_map/ppermute | solution.py:243
  7.1 7.9 %collective-permute-start.3 = (bf16[272,256]{1,0:T(8,128)(2,1)S(1)}, bf16[272,256]{1,0:T(8,128)(2,1)S(1)}, u32[]{:S(2)}, u32[]{:S(2)}) collective-permute-start(bf16[272,256]{1,0:T(8,128)(2,1)S(1)} %payload.1.refs_0_), channel_id=1, source_target_pairs={{0,1},{1,0},{2,3},{3,2},{4,5},{5,4},{6,7},{7,6},{8,9},{9,8},{10,11... | collective-permute-start | bytes 417800 | tf_op jit(solution)/shard_map/ppermute | solution.py:243
  7.1 10.0 %collective-permute-start = (bf16[272,256]{1,0:T(8,128)(2,1)S(1)}, bf16[272,256]{1,0:T(8,128)(2,1)S(1)}, u32[]{:S(2)}, u32[]{:S(2)}) collective-permute-start(bf16[272,256]{1,0:T(8,128)(2,1)S(1)} %payload.1.refs_0_), channel_id=1, source_target_pairs={{0,8},{1,9},{2,10},{3,11},{4,12},{5,13},{6,14},{7,15},{8,0},{9,1},... | collective-permute-start | bytes 417800 | tf_op jit(solution)/shard_map/ppermute | solution.py:243
  10.7 6.4 %collective-permute-start.6 = (bf16[272,256]{1,0:T(8,128)(2,1)S(1)}, bf16[272,256]{1,0:T(8,128)(2,1)S(1)}, u32[]{:S(2)}, u32[]{:S(2)}) collective-permute-start(bf16[272,256]{1,0:T(8,128)(2,1)S(1)} %collective-permute-done.5.refs_2_), channel_id=1, source_target_pairs={{0,1},{1,0},{2,3},{3,2},{4,5},{5,4},{6,7},{7,6},{8,9},{9,8},{10,11... | collective-permute-start | bytes 417800 | tf_op jit(solution)/shard_map/ppermute | solution.py:243
  10.7 6.4 %collective-permute-start.4 = (bf16[272,256]{1,0:T(8,128)(2,1)S(1)}, bf16[272,256]{1,0:T(8,128)(2,1)S(1)}, u32[]{:S(2)}, u32[]{:S(2)}) collective-permute-start(bf16[272,256]{1,0:T(8,128)(2,1)S(1)} %collective-permute-done.1.refs_1_), channel_id=1, source_target_pairs={{0,1},{1,0},{2,3},{3,2},{4,5},{5,4},{6,7},{7,6},{8,9},{9,8},{10,11... | collective-permute-start | bytes 417800 | tf_op jit(solution)/shard_map/ppermute | solution.py:243
  11.2 5.9 %collective-permute-start.2 = (bf16[272,256]{1,0:T(8,128)(2,1)S(1)}, bf16[272,256]{1,0:T(8,128)(2,1)S(1)}, u32[]{:S(2)}, u32[]{:S(2)}) collective-permute-start(bf16[272,256]{1,0:T(8,128)(2,1)S(1)} %collective-permute-done.1.refs_1_), channel_id=1, source_target_pairs={{0,2},{1,3},{2,0},{3,1},{4,6},{5,7},{6,4},{7,5},{8,10},{9,11},{10,... | collective-permute-start | bytes 417800 | tf_op jit(solution)/shard_map/ppermute | solution.py:243
  11.6 0.8 %copy-start.2 = (s32[64,128]{1,0:T(8,128)S(1)}, s32[64,128]{1,0:T(8,128)}, u32[]{:S(2)}) copy-start(s32[64,128]{1,0:T(8,128)} %seeds_ref) | copy-start | bytes 98308
  17.1 8.2 %collective-permute-start.12 = (bf16[272,256]{1,0:T(8,128)(2,1)S(1)}, bf16[272,256]{1,0:T(8,128)(2,1)S(1)}, u32[]{:S(2)}, u32[]{:S(2)}) collective-permute-start(bf16[272,256]{1,0:T(8,128)(2,1)S(1)} %collective-permute-done.refs_3_), channel_id=1, source_target_pairs={{0,1},{1,0},{2,3},{3,2},{4,5},{5,4},{6,7},{7,6},{8,9},{9,8},{10,11... | collective-permute-start | bytes 417800 | tf_op jit(solution)/shard_map/ppermute | solution.py:243
  17.2 6.1 %collective-permute-start.8 = (bf16[272,256]{1,0:T(8,128)(2,1)S(1)}, bf16[272,256]{1,0:T(8,128)(2,1)S(1)}, u32[]{:S(2)}, u32[]{:S(2)}) collective-permute-start(bf16[272,256]{1,0:T(8,128)(2,1)S(1)} %collective-permute-done.refs_3_), channel_id=1, source_target_pairs={{0,2},{1,3},{2,0},{3,1},{4,6},{5,7},{6,4},{7,5},{8,10},{9,11},{10,... | collective-permute-start | bytes 417800 | tf_op jit(solution)/shard_map/ppermute | solution.py:243
  17.8 5.7 %collective-permute-start.7 = (bf16[272,256]{1,0:T(8,128)(2,1)S(1)}, bf16[272,256]{1,0:T(8,128)(2,1)S(1)}, u32[]{:S(2)}, u32[]{:S(2)}) collective-permute-start(bf16[272,256]{1,0:T(8,128)(2,1)S(1)} %collective-permute-done.refs_3_), channel_id=1, source_target_pairs={{0,4},{1,5},{2,6},{3,7},{4,0},{5,1},{6,2},{7,3},{8,12},{9,13},{10,... | collective-permute-start | bytes 417800 | tf_op jit(solution)/shard_map/ppermute | solution.py:243
  18.9 6.4 %collective-permute-start.13 = (bf16[272,256]{1,0:T(8,128)(2,1)S(1)}, bf16[272,256]{1,0:T(8,128)(2,1)S(1)}, u32[]{:S(2)}, u32[]{:S(2)}) collective-permute-start(bf16[272,256]{1,0:T(8,128)(2,1)S(1)} %collective-permute-done.2.refs_4_), channel_id=1, source_target_pairs={{0,1},{1,0},{2,3},{3,2},{4,5},{5,4},{6,7},{7,6},{8,9},{9,8},{10,11... | collective-permute-start | bytes 417800 | tf_op jit(solution)/shard_map/ppermute | solution.py:243
  23.5 4.7 %collective-permute-start.10 = (bf16[272,256]{1,0:T(8,128)(2,1)S(1)}, bf16[272,256]{1,0:T(8,128)(2,1)S(1)}, u32[]{:S(2)}, u32[]{:S(2)}) collective-permute-start(bf16[272,256]{1,0:T(8,128)(2,1)S(1)} %collective-permute-done.7.refs_0_), channel_id=1, source_target_pairs={{0,1},{1,0},{2,3},{3,2},{4,5},{5,4},{6,7},{7,6},{8,9},{9,8},{10,11... | collective-permute-start | bytes 417800 | tf_op jit(solution)/shard_map/ppermute | solution.py:243
  23.5 7.0 %collective-permute-start.9 = (bf16[272,256]{1,0:T(8,128)(2,1)S(1)}, bf16[272,256]{1,0:T(8,128)(2,1)S(1)}, u32[]{:S(2)}, u32[]{:S(2)}) collective-permute-start(bf16[272,256]{1,0:T(8,128)(2,1)S(1)} %collective-permute-done.7.refs_0_), channel_id=1, source_target_pairs={{0,2},{1,3},{2,0},{3,1},{4,6},{5,7},{6,4},{7,5},{8,10},{9,11},{10,... | collective-permute-start | bytes 417800 | tf_op jit(solution)/shard_map/ppermute | solution.py:243
  25.0 3.2 %collective-permute-start.11 = (bf16[272,256]{1,0:T(8,128)(2,1)S(1)}, bf16[272,256]{1,0:T(8,128)(2,1)S(1)}, u32[]{:S(2)}, u32[]{:S(2)}) collective-permute-start(bf16[272,256]{1,0:T(8,128)(2,1)S(1)} %collective-permute-done.8.refs_1_), channel_id=1, source_target_pairs={{0,1},{1,0},{2,3},{3,2},{4,5},{5,4},{6,7},{7,6},{8,9},{9,8},{10,11... | collective-permute-start | bytes 417800 | tf_op jit(solution)/shard_map/ppermute | solution.py:243
  30.5 3.1 %collective-permute-start.14 = (bf16[272,256]{1,0:T(8,128)(2,1)S(1)}, bf16[272,256]{1,0:T(8,128)(2,1)S(1)}, u32[]{:S(2)}, u32[]{:S(2)}) collective-permute-start(bf16[272,256]{1,0:T(8,128)(2,1)S(1)} %collective-permute-done.9.refs_0_), channel_id=1, source_target_pairs={{0,1},{1,0},{2,3},{3,2},{4,5},{5,4},{6,7},{7,6},{8,9},{9,8},{10,11... | collective-permute-start | bytes 417800 | tf_op jit(solution)/shard_map/ppermute | solution.py:243
  35.5 1.8 %collective-permute-start.15 = (bf16[64,2048]{1,0:T(8,128)(2,1)S(1)}, bf16[64,2048]{1,0:T(8,128)(2,1)S(1)}, u32[]{:S(2)}, u32[]{:S(2)}) collective-permute-start(bf16[64,2048]{1,0:T(8,128)(2,1)S(1)} %get-tuple-element.76.mine_ref), channel_id=1, source_target_pairs={{0,1},{1,0},{2,3},{3,2},{4,5},{5,4},{6,7},{7,6},{8,9},{9,8},{10,11... | collective-permute-start | bytes 786440 | tf_op jit(solution)/shard_map/ppermute | solution.py:243
  38.6 1.6 %collective-permute-start.16 = (bf16[64,2048]{1,0:T(8,128)(2,1)S(1)}, bf16[64,2048]{1,0:T(8,128)(2,1)S(1)}, u32[]{:S(2)}, u32[]{:S(2)}) collective-permute-start(bf16[64,2048]{1,0:T(8,128)(2,1)S(1)} %step.1.mine_ref), channel_id=1, source_target_pairs={{0,1},{1,0},{2,3},{3,2},{4,5},{5,4},{6,7},{7,6},{8,9},{9,8},{10,11... | collective-permute-start | bytes 786440 | tf_op jit(solution)/shard_map/ppermute | solution.py:243

commit v3 on v2

--- a/solution.py
+++ b/solution.py
@@ -32,7 +32,7 @@
     return (widened * factor * widened.shape[-1] ** (-0.5)).astype(BF16)
 
 
-ORDER = ((0, 0), (1, 0), (2, 0), (1, 1), (0, 1), (2, 1), (3, 0), (3, 1))
+ORDER = ((0, 0), (1, 0), (2, 0), (0, 1), (1, 1), (2, 1), (3, 0), (3, 1))
 PLACE = {block: place for place, block in enumerate(ORDER)}
 OWN_STAGES = (
     ((0, 0), (1, 0), (0, 1), (2, 0), (1, 1)),
@@ -42,8 +42,8 @@
     (),
 )
 OTHER_STAGES = (
-    ((0, 0), (1, 0), (0, 1)),
-    ((2, 0), (1, 1)),
+    ((0, 0), (1, 0)),
+    ((0, 1), (2, 0), (1, 1)),
     ((3, 0), (2, 1)),
     (),
     ((3, 1),),
@@ -70,9 +70,14 @@
                 for source in blocks[side]:
                     if (target[0], source[1]) in blocks[side]:
                         here.add((PLACE[target], side * 8 + PLACE[source]))
-    new = here - before
-    targets = sorted({target for target, _ in new})
-    return [(one, runs_of([source for target, source in new if target == one])) for one in targets]
+    wanted = {}
+    for target, source in here - before:
+        wanted.setdefault(target, set()).add(source)
+    tasks = []
+    for sources in sorted({tuple(sorted(one)) for one in wanted.values()}):
+        for low, high in runs_of([target for target in wanted if tuple(sorted(wanted[target])) == sources]):
+            tasks.append((low, high, runs_of(sources)))
+    return tasks
 
 
 def dot_nt(lhs, rhs):
@@ -83,14 +88,16 @@
     return lax.dot_general(lhs, rhs, (((1,), (0,)), ((), ())), preferred_element_type=F32)
 
 
-def payload_kernel(count_ref, emb_in, list_in, out_ref, emb_ref, list_ref, sems):
+def payload_kernel(count_ref, emb_in, list_in, seeds_in, out_ref, seeds_ref, emb_ref, list_ref, sems):
     rows = emb_ref.shape[0]
     width = emb_ref.shape[1]
     slots = list_ref.shape[1]
     emb_copy = pltpu.make_async_copy(emb_in, emb_ref, sems.at[0])
     list_copy = pltpu.make_async_copy(list_in, list_ref, sems.at[1])
+    seeds_copy = pltpu.make_async_copy(seeds_in, seeds_ref, sems.at[2])
     emb_copy.start()
     list_copy.start()
+    seeds_copy.start()
     emb_copy.wait()
     list_copy.wait()
     out_ref[0:rows, :] = normalize(emb_ref[...])
@@ -99,6 +106,7 @@
     row_hot = lax.broadcasted_iota(jnp.int32, (width, slots), 0) == list_ref[0:1, :]
     table = dot_nt(col_hot.astype(F32).astype(BF16), row_hot.astype(F32).astype(BF16))
     out_ref[rows : rows + EXTRA_ROWS, :] = table.astype(BF16)
+    seeds_copy.wait()
 
 
 def restart_kernel(me_ref, seeds_ref, out_ref, counts):
@@ -159,8 +167,9 @@
                 ]
     if stage == 0:
         total_ref[...] = jnp.zeros_like(total_ref)
-    for target, spans in stage_tasks(stage):
-        lanes = slice(target * rows, (target + 1) * rows)
+    tasks = stage_tasks(stage)
+    for first, end, spans in tasks:
+        lanes = slice(first * rows, end * rows)
         for low, high in spans:
             inner = dot_nt(units[low * rows : high * rows, :], units[lanes, :])
             for tile in range((high - low) * rows // TILE):
@@ -170,9 +179,13 @@
                 shift = bias[pl.ds(bias_row, 1), lanes]
                 value = jnp.exp2(inner[tile * TILE : (tile + 1) * TILE] * SLOPE + shift)
                 kt_ref[low * rows + tile * TILE : low * rows + (tile + 1) * TILE, lanes] = value.astype(BF16)
+    kept = total_ref.shape[0]
+    for first, end, spans in tasks:
+        lanes = slice(first * rows, end * rows)
         total = total_ref[:, lanes]
         for low, high in spans:
-            total = total + dot_nn(rt_ref[:, low * rows : high * rows], kt_ref[low * rows : high * rows, lanes])
+            sources = slice(low * rows, high * rows)
+            total = total + dot_nn(rt_ref[:, sources], kt_ref[sources, lanes])[0:kept]
         total_ref[:, lanes] = total
     if stage < len(OWN_STAGES) - 1:
         refs[0][...] = jnp.zeros_like(refs[0])
@@ -234,8 +247,12 @@
     return pltpu.CompilerParams(vmem_limit_bytes=20 * 2**20)
 
 
+def in_hbm(array):
+    return pltpu.with_memory_space_constraint(array, pltpu.HBM)
+
+
 def work(micros):
-    return pl.CostEstimate(flops=int(micros * 1e9), bytes_accessed=int(micros * 3e6), transcendentals=0)
+    return pl.CostEstimate(flops=int(micros * 1000), bytes_accessed=int(micros * 100), transcendentals=0)
 
 
 def swap(array, mapping):
@@ -267,25 +284,27 @@
     sessions = rows * 16
     own = rows * 8
     slots = tile_list.shape[3]
-    block = pl.pallas_call(
+    block, seeds = pl.pallas_call(
         payload_kernel,
-        in_specs=[SCALARS, REMAIN, REMAIN],
-        out_specs=WHOLE,
-        out_shape=jax.ShapeDtypeStruct((rows + EXTRA_ROWS, width), BF16),
+        in_specs=[SCALARS] + [REMAIN] * 3,
+        out_specs=[WHOLE] * 2,
+        out_shape=[
+            pltpu.VMEM((rows + EXTRA_ROWS, width), BF16),
+            pltpu.VMEM(seeds.shape, seeds.dtype),
+        ],
         scratch_shapes=[
             pltpu.VMEM((rows, width), BF16),
             pltpu.VMEM((2, slots), jnp.int32),
-            pltpu.SemaphoreType.DMA((2,)),
+            pltpu.SemaphoreType.DMA((3,)),
         ],
         compiler_params=params(),
         name="payload",
-    )(tile_count, embeddings, tile_list.reshape(2, slots))
-
+    )(tile_count, in_hbm(embeddings), in_hbm(tile_list.reshape(2, slots)), in_hbm(seeds))
     state_shapes = [
         pltpu.VMEM((sessions, width), BF16),
         pltpu.VMEM((32, own), F32),
         pltpu.VMEM((sessions, own), BF16),
-        pltpu.VMEM((2 * seed_cols, own), F32),
+        pltpu.VMEM((seed_cols + 8, own), F32),
     ]
     mark = [jax.ShapeDtypeStruct((8, TILE), F32)]
 
@@ -303,14 +322,10 @@
         )(me, rt, *arrivals, *state, *after)
         return outs[:4], outs[4:]
 
+    z1 = swap(block, near)
     z2 = swap(block, far)
-    z1 = swap(block, near)
     x0 = swap(block, across)
     b00 = swap(block, sibling)
-    x1 = swap(z1, across)
-    b10 = swap(z1, sibling)
-    b01 = swap(x0, sibling)
-    seeds, z1, x0 = lax.optimization_barrier((seeds, z1, x0))
     rt = pl.pallas_call(
         restart_kernel,
         in_specs=[SCALARS, WHOLE],
@@ -321,17 +336,21 @@
         cost_estimate=work(2.6),
         name="restart",
     )(me, seeds)
-    z2, x1, b00, b10, b01, rt = lax.optimization_barrier((z2, x1, b00, b10, b01, rt))
+    z1, rt = lax.optimization_barrier((z1, rt))
+    x1 = swap(z1, across)
+    b10 = swap(z1, sibling)
+    x0, z2, b00 = lax.optimization_barrier((x0, z2, b00))
     z3 = swap(z2, near)
     x2 = swap(z2, across)
     b20 = swap(z2, sibling)
+    b01 = swap(x0, sibling)
     b11 = swap(x1, sibling)
-    state, (done,) = run_stage(0, rt, [block, z1, x0, z2, x1, b00, b10, b01], [], mark)
-    z3, x2, done = lax.optimization_barrier((z3, x2, done))
+    state, (done,) = run_stage(0, rt, [block, z1, x0, z2, x1, b00, b10], [], mark)
+    x2, z3, done = lax.optimization_barrier((x2, z3, done))
     x3 = swap(z3, across)
     b30 = swap(z3, sibling)
     b21 = swap(x2, sibling)
-    state, (done,) = run_stage(1, rt, [z3, x2, b20, b11], state, mark, done)
+    state, (done,) = run_stage(1, rt, [z3, x2, b01, b20, b11], state, mark, done)
     state, (done,) = run_stage(2, rt, [b30, b21], state, mark, done)
     x3, done = lax.optimization_barrier((x3, done))
     b31 = swap(x3, sibling)

time: 41.6 us -> 36 us (0.87)
  Pallas kernels: 19.1 us -> 16.1 us
  local copies, waits for them, and re-layouts: 2.33 us -> 0 us
    pallas_call x5, Pallas kernels: 12.2 us -> 8.67 us  [run_stage(): pl.pallas_call(functools.partial(stage_kernel, stage), in_specs=[SCALARS]...]
    unnamed x6 -> x0, local copies, waits for them, and re-layouts: 2.33 us -> none
    pallas_call x1, Pallas kernels: 0.31 us -> 1.09 us  [chip_local(): pl.pallas_call(payload_kernel, in_specs=[SCALARS] + [REMAIN] * 3, out_spe...]
    ppermute x17, starting transfers between devices: 12.5 us -> 12.1 us  [swap(): return lax.ppermute(array, ('row', 'col'), pairs)]
  transfers between devices with their start and end apart: 17 -> 17, of which waited for: 5 -> 5; matrix products, arithmetic and copies ran while one was open for 0% -> 0% of each run, Pallas kernels for 35% -> 32%
where the time goes in v3:
time: 36 us; the launch traced here: 35.8 us
  Pallas kernels  16.1 us (45%)
  starting transfers between devices  12.1 us (34%)
  waiting for transfers between devices  6.83 us (19%)
  between operations  0.78 us (2%)
    ppermute x17, starting transfers between devices, swap(): return lax.ppermute(array, ('row', 'col'), pairs)  12.1 us
    pallas_call x5, Pallas kernels, run_stage(): pl.pallas_call(functools.partial(stage_kernel, stage), in_specs=[SCALARS]...  8.67 us
    ppermute x17, waiting for transfers between devices, swap(): return lax.ppermute(array, ('row', 'col'), pairs)  6.83 us
    pallas_call x1, Pallas kernels, chip_local(): pl.pallas_call(restart_kernel, in_specs=[SCALARS, WHOLE], out_specs=WHOLE...  2.7 us
    pallas_call x1, Pallas kernels, chip_local(): pl.pallas_call(step_kernel, in_specs=[WHOLE] * 5, out_specs=WHOLE, out_sh...  1.3 us
    pallas_call x1, Pallas kernels, chip_local(): pl.pallas_call(half_kernel, in_specs=[WHOLE] * 2, out_specs=WHOLE, out_sh...  1.27 us
    pallas_call x1, Pallas kernels, chip_local(): pl.pallas_call(last_kernel, in_specs=[WHOLE] * 5, out_specs=WHOLE, out_sh...  1.09 us
    pallas_call x1, Pallas kernels, chip_local(): pl.pallas_call(payload_kernel, in_specs=[SCALARS] + [REMAIN] * 3, out_spe...  1.09 us
  transfers between devices with their start and end apart: 17, of which 5 were waited for; matrix products, arithmetic and copies ran while one was open for 0% of the time, Pallas kernels for 32%

profile of v3, /device:TPU:0, one launch (start us, length us, event | category | flops | bytes accessed | tf_op | source)
XLA Modules:
  0.0 35.8 jit_solution(589884637373633640)
XLA Ops:
  0.7 1.1 %payload.1 = (bf16[272,256]{1,0:T(8,128)(2,1)S(1)}, s32[64,128]{1,0:T(8,128)S(1)}) custom-call(s32[1,1]{1,0:T(1,128)S(6)} %copy.37.count_ref, bf16[256,256]{1,0:T(8,128)(2,1)} %emb_in.1, s32[2,48]{1,0:T(2,128)} %bitcast.3, s32[64,128]{1,0:T(8,128)} %seeds_in.1), custom_call_target="tpu_custom_call" | custom-call | tf_op jit(solution)/shard_map/payload/pallas_call | solution.py:287
  1.7 3.1 %collective-permute-start = (bf16[272,256]{1,0:T(8,128)(2,1)S(1)}, bf16[272,256]{1,0:T(8,128)(2,1)S(1)}, u32[]{:S(2)}, u32[]{:S(2)}) collective-permute-start(bf16[272,256]{1,0:T(8,128)(2,1)S(1)} %get-tuple-element.39.refs_0_), channel_id=1, source_target_pairs={{0,4},{1,5},{2,6},{3,7},{4,0},{5,1},{6,2},{7,3},{8,12},{9,13},{10,... | collective-permute-start | bytes 417800 | tf_op jit(solution)/shard_map/ppermute | solution.py:260
  4.8 2.6 %collective-permute-start.2 = (bf16[272,256]{1,0:T(8,128)(2,1)S(1)}, bf16[272,256]{1,0:T(8,128)(2,1)S(1)}, u32[]{:S(2)}, u32[]{:S(2)}) collective-permute-start(bf16[272,256]{1,0:T(8,128)(2,1)S(1)} %get-tuple-element.39.refs_0_), channel_id=1, source_target_pairs={{0,8},{1,9},{2,10},{3,11},{4,12},{5,13},{6,14},{7,15},{8,0},{9,1},... | collective-permute-start | bytes 417800 | tf_op jit(solution)/shard_map/ppermute | solution.py:260
  7.4 1.5 %collective-permute-start.1 = (bf16[272,256]{1,0:T(8,128)(2,1)S(1)}, bf16[272,256]{1,0:T(8,128)(2,1)S(1)}, u32[]{:S(2)}, u32[]{:S(2)}) collective-permute-start(bf16[272,256]{1,0:T(8,128)(2,1)S(1)} %get-tuple-element.39.refs_0_), channel_id=1, source_target_pairs={{0,2},{1,3},{2,0},{3,1},{4,6},{5,7},{6,4},{7,5},{8,10},{9,11},{10,... | collective-permute-start | bytes 417800 | tf_op jit(solution)/shard_map/ppermute | solution.py:260
  8.9 2.7 %restart.1.rt_ref = bf16[128,4096]{1,0:T(8,128)(2,1)S(1)} custom-call(s32[1]{0:T(128)} %bitcast.1.me_ref, s32[64,128]{1,0:T(8,128)S(1)} %get-tuple-element.40.seeds_ref), custom_call_target="tpu_custom_call" | custom-call | flops 2600 | bytes 260 | tf_op jit(solution)/shard_map/restart/pallas_call | solution.py:329
  11.7 0.6 %collective-permute-start.6 = (bf16[272,256]{1,0:T(8,128)(2,1)S(1)}, bf16[272,256]{1,0:T(8,128)(2,1)S(1)}, u32[]{:S(2)}, u32[]{:S(2)}) collective-permute-start(bf16[272,256]{1,0:T(8,128)(2,1)S(1)} %collective-permute-done.refs_1_), channel_id=1, source_target_pairs={{0,2},{1,3},{2,0},{3,1},{4,6},{5,7},{6,4},{7,5},{8,10},{9,11},{10,... | collective-permute-start | bytes 417800 | tf_op jit(solution)/shard_map/ppermute | solution.py:260
  12.3 2.5 %collective-permute-done.2.refs_3_ = bf16[272,256]{1,0:T(8,128)(2,1)S(1)} collective-permute-done((bf16[272,256]{1,0:T(8,128)(2,1)S(1)}, bf16[272,256]{1,0:T(8,128)(2,1)S(1)}, u32[]{:S(2)}, u32[]{:S(2)}) %collective-permute-start.2) | collective-permute-done | bytes 139296 | tf_op jit(solution)/shard_map/ppermute | solution.py:260
  14.8 1.5 %collective-permute-start.4 = (bf16[272,256]{1,0:T(8,128)(2,1)S(1)}, bf16[272,256]{1,0:T(8,128)(2,1)S(1)}, u32[]{:S(2)}, u32[]{:S(2)}) collective-permute-start(bf16[272,256]{1,0:T(8,128)(2,1)S(1)} %collective-permute-done.2.refs_3_), channel_id=1, source_target_pairs={{0,2},{1,3},{2,0},{3,1},{4,6},{5,7},{6,4},{7,5},{8,10},{9,11},{10,... | collective-permute-start | bytes 417800 | tf_op jit(solution)/shard_map/ppermute | solution.py:260
  16.3 0.5 %collective-permute-start.12 = (bf16[272,256]{1,0:T(8,128)(2,1)S(1)}, bf16[272,256]{1,0:T(8,128)(2,1)S(1)}, u32[]{:S(2)}, u32[]{:S(2)}) collective-permute-start(bf16[272,256]{1,0:T(8,128)(2,1)S(1)} %collective-permute-done.2.refs_3_), channel_id=1, source_target_pairs={{0,1},{1,0},{2,3},{3,2},{4,5},{5,4},{6,7},{7,6},{8,9},{9,8},{10,11... | collective-permute-start | bytes 417800 | tf_op jit(solution)/shard_map/ppermute | solution.py:260
  16.8 1.4 %collective-permute-done.6.refs_4_ = bf16[272,256]{1,0:T(8,128)(2,1)S(1)} collective-permute-done((bf16[272,256]{1,0:T(8,128)(2,1)S(1)}, bf16[272,256]{1,0:T(8,128)(2,1)S(1)}, u32[]{:S(2)}, u32[]{:S(2)}) %collective-permute-start.6) | collective-permute-done | bytes 139296 | tf_op jit(solution)/shard_map/ppermute | solution.py:260
  18.3 1.9 %stage0.1 = (bf16[4096,256]{1,0:T(8,128)(2,1)S(1)}, f32[32,2048]{1,0:T(8,128)S(1)}, bf16[4096,2048]{1,0:T(8,128)(2,1)S(1)}, f32[72,2048]{1,0:T(8,128)S(1)}, f32[8,128]{1,0:T(8,128)S(1)}) custom-call(s32[1]{0:T(128)} %bitcast.1.me_ref, bf16[128,4096]{1,0:T(8,128)(2,1)S(1)} %restart.1.rt_ref, bf16[272,256]{1,0:T(8,128)(2,1)S(1)} %get-tuple-element.39.refs_0_, ...), custom_call_target="tpu_custom_call" | custom-call | flops 2500 | bytes 250 | tf_op jit(solution)/shard_map/stage0/pallas_call | solution.py:313
  20.2 0.6 %collective-permute-done.4.refs_1_ = bf16[272,256]{1,0:T(8,128)(2,1)S(1)} collective-permute-done((bf16[272,256]{1,0:T(8,128)(2,1)S(1)}, bf16[272,256]{1,0:T(8,128)(2,1)S(1)}, u32[]{:S(2)}, u32[]{:S(2)}) %collective-permute-start.4) | collective-permute-done | bytes 139296 | tf_op jit(solution)/shard_map/ppermute | solution.py:260
  20.8 0.5 %collective-permute-start.9 = (bf16[272,256]{1,0:T(8,128)(2,1)S(1)}, bf16[272,256]{1,0:T(8,128)(2,1)S(1)}, u32[]{:S(2)}, u32[]{:S(2)}) collective-permute-start(bf16[272,256]{1,0:T(8,128)(2,1)S(1)} %collective-permute-done.5.refs_0_), channel_id=1, source_target_pairs={{0,1},{1,0},{2,3},{3,2},{4,5},{5,4},{6,7},{7,6},{8,9},{9,8},{10,11... | collective-permute-start | bytes 417800 | tf_op jit(solution)/shard_map/ppermute | solution.py:260
  21.3 0.8 %collective-permute-start.8 = (bf16[272,256]{1,0:T(8,128)(2,1)S(1)}, bf16[272,256]{1,0:T(8,128)(2,1)S(1)}, u32[]{:S(2)}, u32[]{:S(2)}) collective-permute-start(bf16[272,256]{1,0:T(8,128)(2,1)S(1)} %collective-permute-done.5.refs_0_), channel_id=1, source_target_pairs={{0,2},{1,3},{2,0},{3,1},{4,6},{5,7},{6,4},{7,5},{8,10},{9,11},{10,... | collective-permute-start | bytes 417800 | tf_op jit(solution)/shard_map/ppermute | solution.py:260
  22.1 2.4 %stage1.1 = (bf16[4096,256]{1,0:T(8,128)(2,1)S(1)}, f32[32,2048]{1,0:T(8,128)S(1)}, bf16[4096,2048]{1,0:T(8,128)(2,1)S(1)}, f32[72,2048]{1,0:T(8,128)S(1)}, f32[8,128]{1,0:T(8,128)S(1)}) custom-call(s32[1]{0:T(128)} %bitcast.1.me_ref, bf16[128,4096]{1,0:T(8,128)(2,1)S(1)} %restart.1.rt_ref, ...), custom_call_target="tpu_custom_call", output_to_operand_aliasing={{0}: (7, {}), {1}: (8, {}), {2}: (9, {}), {3}: (10, {})} | custom-call | flops 2500 | bytes 250 | tf_op jit(solution)/shard_map/stage1/pallas_call | solution.py:313
  24.6 1.3 %stage2.1 = (bf16[4096,256]{1,0:T(8,128)(2,1)S(1)}, f32[32,2048]{1,0:T(8,128)S(1)}, bf16[4096,2048]{1,0:T(8,128)(2,1)S(1)}, f32[72,2048]{1,0:T(8,128)S(1)}, f32[8,128]{1,0:T(8,128)S(1)}) custom-call(s32[1]{0:T(128)} %bitcast.1.me_ref, bf16[128,4096]{1,0:T(8,128)(2,1)S(1)} %restart.1.rt_ref, ...), custom_call_target="tpu_custom_call", output_to_operand_aliasing={{0}: (4, {}), {1}: (5, {}), {2}: (6, {}), {3}: (7, {})} | custom-call | flops 2500 | bytes 250 | tf_op jit(solution)/shard_map/stage2/pallas_call | solution.py:313
  25.9 1.0 %collective-permute-done.8.refs_0_ = bf16[272,256]{1,0:T(8,128)(2,1)S(1)} collective-permute-done((bf16[272,256]{1,0:T(8,128)(2,1)S(1)}, bf16[272,256]{1,0:T(8,128)(2,1)S(1)}, u32[]{:S(2)}, u32[]{:S(2)}) %collective-permute-start.8) | collective-permute-done | bytes 139296 | tf_op jit(solution)/shard_map/ppermute | solution.py:260
  26.9 2.0 %stage3.1 = (bf16[4096,256]{1,0:T(8,128)(2,1)S(1)}, f32[32,2048]{1,0:T(8,128)S(1)}, bf16[4096,2048]{1,0:T(8,128)(2,1)S(1)}, f32[72,2048]{1,0:T(8,128)S(1)}, f32[8,128]{1,0:T(8,128)}) custom-call(s32[1]{0:T(128)} %bitcast.1.me_ref, bf16[128,4096]{1,0:T(8,128)(2,1)S(1)} %restart.1.rt_ref, ...), custom_call_target="tpu_custom_call", output_to_operand_aliasing={{0}: (3, {}), {1}: (4, {}), {2}: (5, {}), {3}: (6, {})} | custom-call | flops 2500 | bytes 250 | tf_op jit(solution)/shard_map/stage3/pallas_call | solution.py:313
  28.9 1.0 %stage4.1 = (bf16[4096,256]{1,0:T(8,128)(2,1)S(1)}, f32[32,2048]{1,0:T(8,128)S(1)}, bf16[4096,2048]{1,0:T(8,128)(2,1)S(1)}, f32[72,2048]{1,0:T(8,128)S(1)}, bf16...) custom-call(s32[1]{0:T(128)} %bitcast.1.me_ref, ...), custom_call_target="tpu_custom_call", output_to_operand_aliasing={{0}: (3, {}), {1}: (4, {}), {2}: (5, {}), {3}: (6, {})} | custom-call | flops 2500 | bytes 250 | tf_op jit(solution)/shard_map/stage4/pallas_call | solution.py:313
  29.9 0.6 %collective-permute-start.15 = (bf16[64,2048]{1,0:T(8,128)(2,1)S(1)}, bf16[64,2048]{1,0:T(8,128)(2,1)S(1)}, u32[]{:S(2)}, u32[]{:S(2)}) collective-permute-start(bf16[64,2048]{1,0:T(8,128)(2,1)S(1)} %get-tuple-element.72.mine_ref), channel_id=1, source_target_pairs={{0,1},{1,0},{2,3},{3,2},{4,5},{5,4},{6,7},{7,6},{8,9},{9,8},{10,11... | collective-permute-start | bytes 786440 | tf_op jit(solution)/shard_map/ppermute | solution.py:260
  30.5 1.3 %half.1.half_ref = f32[64,2048]{1,0:T(8,128)S(1)} custom-call(bf16[4096,2048]{1,0:T(8,128)(2,1)S(1)} %get-tuple-element.70.kt_ref, bf16[64,2048]{1,0:T(8,128)(2,1)S(1)} %get-tuple-element.72.mine_ref), custom_call_target="tpu_custom_call" | custom-call | flops 1500 | bytes 150 | tf_op jit(solution)/shard_map/half/pallas_call | solution.py:367
  31.8 1.3 %step.1.mine_ref = bf16[64,2048]{1,0:T(8,128)(2,1)S(1)} custom-call(bf16[128,4096]{1,0:T(8,128)(2,1)S(1)} %restart.1.rt_ref, bf16[4096,2048]{1,0:T(8,128)(2,1)S(1)} %get-tuple-element.70.kt_ref, f32[8,2048]{1,0:T(8,128)S(1)} %get-tuple-element.71.gain_ref, f32[64,2048]{1,0:T(8,128)S(1)} %half.1.half_ref, bf16[64,2048]{1,0:T(8,128)(2,1)S(1)} %collective-permute-done.15.other_ref), custom_call_target="tpu_custom_call" | custom-call | flops 1500 | bytes 150 | tf_op jit(solution)/shard_map/step/pallas_call | solution.py:376
  33.4 1.3 %collective-permute-done.16.other_ref = bf16[64,2048]{1,0:T(8,128)(2,1)S(1)} collective-permute-done((bf16[64,2048]{1,0:T(8,128)(2,1)S(1)}, bf16[64,2048]{1,0:T(8,128)(2,1)S(1)}, u32[]{:S(2)}, u32[]{:S(2)}) %collective-permute-start.16) | collective-permute-done | bytes 262176 | tf_op jit(solution)/shard_map/ppermute | solution.py:260
  34.7 1.1 %last.1 = f32[64,256]{1,0:T(8,128)} custom-call(bf16[128,4096]{1,0:T(8,128)(2,1)S(1)} %restart.1.rt_ref, bf16[4096,2048]{1,0:T(8,128)(2,1)S(1)} %get-tuple-element.70.kt_ref, f32[8,2048]{1,0:T(8,128)S(1)} %get-tuple-element.71.gain_ref, bf16[64,2048]{1,0:T(8,128)(2,1)S(1)} %step.1.mine_ref, bf16[64,2048]{1,0:T(8,128)(2,1)S(1)} %collective-permute-done.16.other_ref), custom_call_target="tpu_custom_call" | custom-call | flops 500 | bytes 50 | tf_op jit(solution)/shard_map/last/pallas_call | solution.py:385
  (20 shorter events, 0.4 us)
Async XLA Ops:
  1.7 9.9 %collective-permute-start = (bf16[272,256]{1,0:T(8,128)(2,1)S(1)}, bf16[272,256]{1,0:T(8,128)(2,1)S(1)}, u32[]{:S(2)}, u32[]{:S(2)}) collective-permute-start(bf16[272,256]{1,0:T(8,128)(2,1)S(1)} %get-tuple-element.39.refs_0_), channel_id=1, source_target_pairs={{0,4},{1,5},{2,6},{3,7},{4,0},{5,1},{6,2},{7,3},{8,12},{9,13},{10,... | collective-permute-start | bytes 417800 | tf_op jit(solution)/shard_map/ppermute | solution.py:260
  4.8 7.5 %collective-permute-start.3 = (bf16[272,256]{1,0:T(8,128)(2,1)S(1)}, bf16[272,256]{1,0:T(8,128)(2,1)S(1)}, u32[]{:S(2)}, u32[]{:S(2)}) collective-permute-start(bf16[272,256]{1,0:T(8,128)(2,1)S(1)} %get-tuple-element.39.refs_0_), channel_id=1, source_target_pairs={{0,1},{1,0},{2,3},{3,2},{4,5},{5,4},{6,7},{7,6},{8,9},{9,8},{10,11... | collective-permute-start | bytes 417800 | tf_op jit(solution)/shard_map/ppermute | solution.py:260
  4.8 10.0 %collective-permute-start.2 = (bf16[272,256]{1,0:T(8,128)(2,1)S(1)}, bf16[272,256]{1,0:T(8,128)(2,1)S(1)}, u32[]{:S(2)}, u32[]{:S(2)}) collective-permute-start(bf16[272,256]{1,0:T(8,128)(2,1)S(1)} %get-tuple-element.39.refs_0_), channel_id=1, source_target_pairs={{0,8},{1,9},{2,10},{3,11},{4,12},{5,13},{6,14},{7,15},{8,0},{9,1},... | collective-permute-start | bytes 417800 | tf_op jit(solution)/shard_map/ppermute | solution.py:260
  7.4 7.4 %collective-permute-start.1 = (bf16[272,256]{1,0:T(8,128)(2,1)S(1)}, bf16[272,256]{1,0:T(8,128)(2,1)S(1)}, u32[]{:S(2)}, u32[]{:S(2)}) collective-permute-start(bf16[272,256]{1,0:T(8,128)(2,1)S(1)} %get-tuple-element.39.refs_0_), channel_id=1, source_target_pairs={{0,2},{1,3},{2,0},{3,1},{4,6},{5,7},{6,4},{7,5},{8,10},{9,11},{10,... | collective-permute-start | bytes 417800 | tf_op jit(solution)/shard_map/ppermute | solution.py:260
  11.6 4.7 %collective-permute-start.7 = (bf16[272,256]{1,0:T(8,128)(2,1)S(1)}, bf16[272,256]{1,0:T(8,128)(2,1)S(1)}, u32[]{:S(2)}, u32[]{:S(2)}) collective-permute-start(bf16[272,256]{1,0:T(8,128)(2,1)S(1)} %collective-permute-done.refs_1_), channel_id=1, source_target_pairs={{0,1},{1,0},{2,3},{3,2},{4,5},{5,4},{6,7},{7,6},{8,9},{9,8},{10,11... | collective-permute-start | bytes 417800 | tf_op jit(solution)/shard_map/ppermute | solution.py:260
  11.7 6.5 %collective-permute-start.6 = (bf16[272,256]{1,0:T(8,128)(2,1)S(1)}, bf16[272,256]{1,0:T(8,128)(2,1)S(1)}, u32[]{:S(2)}, u32[]{:S(2)}) collective-permute-start(bf16[272,256]{1,0:T(8,128)(2,1)S(1)} %collective-permute-done.refs_1_), channel_id=1, source_target_pairs={{0,2},{1,3},{2,0},{3,1},{4,6},{5,7},{6,4},{7,5},{8,10},{9,11},{10,... | collective-permute-start | bytes 417800 | tf_op jit(solution)/shard_map/ppermute | solution.py:260
  14.8 5.4 %collective-permute-start.5 = (bf16[272,256]{1,0:T(8,128)(2,1)S(1)}, bf16[272,256]{1,0:T(8,128)(2,1)S(1)}, u32[]{:S(2)}, u32[]{:S(2)}) collective-permute-start(bf16[272,256]{1,0:T(8,128)(2,1)S(1)} %collective-permute-done.2.refs_3_), channel_id=1, source_target_pairs={{0,4},{1,5},{2,6},{3,7},{4,0},{5,1},{6,2},{7,3},{8,12},{9,13},{10,... | collective-permute-start | bytes 417800 | tf_op jit(solution)/shard_map/ppermute | solution.py:260
  14.8 6.0 %collective-permute-start.4 = (bf16[272,256]{1,0:T(8,128)(2,1)S(1)}, bf16[272,256]{1,0:T(8,128)(2,1)S(1)}, u32[]{:S(2)}, u32[]{:S(2)}) collective-permute-start(bf16[272,256]{1,0:T(8,128)(2,1)S(1)} %collective-permute-done.2.refs_3_), channel_id=1, source_target_pairs={{0,2},{1,3},{2,0},{3,1},{4,6},{5,7},{6,4},{7,5},{8,10},{9,11},{10,... | collective-permute-start | bytes 417800 | tf_op jit(solution)/shard_map/ppermute | solution.py:260
  16.3 5.0 %collective-permute-start.11 = (bf16[272,256]{1,0:T(8,128)(2,1)S(1)}, bf16[272,256]{1,0:T(8,128)(2,1)S(1)}, u32[]{:S(2)}, u32[]{:S(2)}) collective-permute-start(bf16[272,256]{1,0:T(8,128)(2,1)S(1)} %collective-permute-done.1.refs_2_), channel_id=1, source_target_pairs={{0,1},{1,0},{2,3},{3,2},{4,5},{5,4},{6,7},{7,6},{8,9},{9,8},{10,11... | collective-permute-start | bytes 417800 | tf_op jit(solution)/shard_map/ppermute | solution.py:260
  16.3 5.8 %collective-permute-start.12 = (bf16[272,256]{1,0:T(8,128)(2,1)S(1)}, bf16[272,256]{1,0:T(8,128)(2,1)S(1)}, u32[]{:S(2)}, u32[]{:S(2)}) collective-permute-start(bf16[272,256]{1,0:T(8,128)(2,1)S(1)} %collective-permute-done.2.refs_3_), channel_id=1, source_target_pairs={{0,1},{1,0},{2,3},{3,2},{4,5},{5,4},{6,7},{7,6},{8,9},{9,8},{10,11... | collective-permute-start | bytes 417800 | tf_op jit(solution)/shard_map/ppermute | solution.py:260
  18.3 3.9 %collective-permute-start.13 = (bf16[272,256]{1,0:T(8,128)(2,1)S(1)}, bf16[272,256]{1,0:T(8,128)(2,1)S(1)}, u32[]{:S(2)}, u32[]{:S(2)}) collective-permute-start(bf16[272,256]{1,0:T(8,128)(2,1)S(1)} %collective-permute-done.6.refs_4_), channel_id=1, source_target_pairs={{0,1},{1,0},{2,3},{3,2},{4,5},{5,4},{6,7},{7,6},{8,9},{9,8},{10,11... | collective-permute-start | bytes 417800 | tf_op jit(solution)/shard_map/ppermute | solution.py:260
  20.8 3.8 %collective-permute-start.10 = (bf16[272,256]{1,0:T(8,128)(2,1)S(1)}, bf16[272,256]{1,0:T(8,128)(2,1)S(1)}, u32[]{:S(2)}, u32[]{:S(2)}) collective-permute-start(bf16[272,256]{1,0:T(8,128)(2,1)S(1)} %collective-permute-done.4.refs_1_), channel_id=1, source_target_pairs={{0,1},{1,0},{2,3},{3,2},{4,5},{5,4},{6,7},{7,6},{8,9},{9,8},{10,11... | collective-permute-start | bytes 417800 | tf_op jit(solution)/shard_map/ppermute | solution.py:260
  20.8 3.8 %collective-permute-start.9 = (bf16[272,256]{1,0:T(8,128)(2,1)S(1)}, bf16[272,256]{1,0:T(8,128)(2,1)S(1)}, u32[]{:S(2)}, u32[]{:S(2)}) collective-permute-start(bf16[272,256]{1,0:T(8,128)(2,1)S(1)} %collective-permute-done.5.refs_0_), channel_id=1, source_target_pairs={{0,1},{1,0},{2,3},{3,2},{4,5},{5,4},{6,7},{7,6},{8,9},{9,8},{10,11... | collective-permute-start | bytes 417800 | tf_op jit(solution)/shard_map/ppermute | solution.py:260
  21.3 5.6 %collective-permute-start.8 = (bf16[272,256]{1,0:T(8,128)(2,1)S(1)}, bf16[272,256]{1,0:T(8,128)(2,1)S(1)}, u32[]{:S(2)}, u32[]{:S(2)}) collective-permute-start(bf16[272,256]{1,0:T(8,128)(2,1)S(1)} %collective-permute-done.5.refs_0_), channel_id=1, source_target_pairs={{0,2},{1,3},{2,0},{3,1},{4,6},{5,7},{6,4},{7,5},{8,10},{9,11},{10,... | collective-permute-start | bytes 417800 | tf_op jit(solution)/shard_map/ppermute | solution.py:260
  26.9 2.0 %collective-permute-start.14 = (bf16[272,256]{1,0:T(8,128)(2,1)S(1)}, bf16[272,256]{1,0:T(8,128)(2,1)S(1)}, u32[]{:S(2)}, u32[]{:S(2)}) collective-permute-start(bf16[272,256]{1,0:T(8,128)(2,1)S(1)} %collective-permute-done.8.refs_0_), channel_id=1, source_target_pairs={{0,1},{1,0},{2,3},{3,2},{4,5},{5,4},{6,7},{7,6},{8,9},{9,8},{10,11... | collective-permute-start | bytes 417800 | tf_op jit(solution)/shard_map/ppermute | solution.py:260
  29.9 1.9 %collective-permute-start.15 = (bf16[64,2048]{1,0:T(8,128)(2,1)S(1)}, bf16[64,2048]{1,0:T(8,128)(2,1)S(1)}, u32[]{:S(2)}, u32[]{:S(2)}) collective-permute-start(bf16[64,2048]{1,0:T(8,128)(2,1)S(1)} %get-tuple-element.72.mine_ref), channel_id=1, source_target_pairs={{0,1},{1,0},{2,3},{3,2},{4,5},{5,4},{6,7},{7,6},{8,9},{9,8},{10,11... | collective-permute-start | bytes 786440 | tf_op jit(solution)/shard_map/ppermute | solution.py:260
  33.1 1.6 %collective-permute-start.16 = (bf16[64,2048]{1,0:T(8,128)(2,1)S(1)}, bf16[64,2048]{1,0:T(8,128)(2,1)S(1)}, u32[]{:S(2)}, u32[]{:S(2)}) collective-permute-start(bf16[64,2048]{1,0:T(8,128)(2,1)S(1)} %step.1.mine_ref), channel_id=1, source_target_pairs={{0,1},{1,0},{2,3},{3,2},{4,5},{5,4},{6,7},{7,6},{8,9},{9,8},{10,11... | collective-permute-start | bytes 786440 | tf_op jit(solution)/shard_map/ppermute | solution.py:260

commit v4 on v3

--- a/solution.py
+++ b/solution.py
@@ -35,18 +35,18 @@
 ORDER = ((0, 0), (1, 0), (2, 0), (0, 1), (1, 1), (2, 1), (3, 0), (3, 1))
 PLACE = {block: place for place, block in enumerate(ORDER)}
 OWN_STAGES = (
-    ((0, 0), (1, 0), (0, 1), (2, 0), (1, 1)),
+    ((0, 0), (1, 0), (0, 1)),
+    ((2, 0), (1, 1)),
     ((3, 0), (2, 1)),
-    (),
     ((3, 1),),
     (),
 )
 OTHER_STAGES = (
-    ((0, 0), (1, 0)),
-    ((0, 1), (2, 0), (1, 1)),
-    ((3, 0), (2, 1)),
     (),
-    ((3, 1),),
+    ((0, 0), (1, 0), (0, 1)),
+    (),
+    ((2, 0), (1, 1)),
+    ((3, 0), (2, 1), (3, 1)),
 )
 
 
@@ -70,6 +70,8 @@
                 for source in blocks[side]:
                     if (target[0], source[1]) in blocks[side]:
                         here.add((PLACE[target], side * 8 + PLACE[source]))
+        if (0, 0) in blocks[1]:
+            here.update((8, PLACE[source]) for source in blocks[0] if (0, source[1]) in blocks[0])
     wanted = {}
     for target, source in here - before:
         wanted.setdefault(target, set()).add(source)
@@ -109,7 +111,7 @@
     seeds_copy.wait()
 
 
-def restart_kernel(me_ref, seeds_ref, out_ref, counts):
+def restart_kernel(me_ref, seeds_ref, out_ref, pick_ref, counts):
     seed_cols = seeds_ref.shape[0]
     tiles = counts.shape[1]
     me = me_ref[0]
@@ -119,6 +121,12 @@
         offset = offset + jnp.where((spot // 2) % 8 == place, 4 * z + 2 * x, 0)
     tile_ids = (me ^ offset) * 2 + spot % 2
     lows = lax.broadcasted_iota(jnp.int32, (TILE, TILE), 0)
+    core, x_pos = me % 2, (me // 2) % 2
+    pick_row = lax.broadcasted_iota(jnp.int32, pick_ref.shape, 0)
+    pick_col = lax.broadcasted_iota(jnp.int32, pick_ref.shape, 1) // TILE
+    sib = pick_col // 4
+    wanted = 4 * (x_pos ^ ((pick_col // 2) % 2)) + 2 * (core ^ sib) + pick_col % 2
+    pick_ref[...] = (pick_row == wanted).astype(F32).astype(BF16)
 
     @pl.loop(0, seed_cols, unroll=16)
     def _(k):
@@ -134,7 +142,7 @@
     out_ref[seed_cols:, :] = first.astype(F32).astype(BF16)
 
 
-def stage_kernel(stage, me_ref, rt_ref, *refs):
+def stage_kernel(stage, me_ref, rt_ref, pick_ref, *refs):
     own_names, other_names = OWN_STAGES[stage], OTHER_STAGES[stage]
     count = len(own_names) + len(other_names)
     arrivals, refs = refs[:count], refs[count:]
@@ -143,27 +151,27 @@
     units, bias, kt_ref, total_ref = refs[:4]
     refs = refs[4:]
     me = me_ref[0]
-    core, x_pos, z_pos = me % 2, (me // 2) % 2, me // 4
+    z_pos = me // 4
     rows = units.shape[0] // 16
     names = [(0, one) for one in own_names] + [(1, one) for one in other_names]
     for (side, one), ref in zip(names, arrivals):
         place = side * 8 + PLACE[one]
         units[place * rows : (place + 1) * rows] = ref[0:rows]
     if names:
-        pick_row = lax.broadcasted_iota(jnp.int32, (TILE, 4 * TILE), 0)
-        pick_col = lax.broadcasted_iota(jnp.int32, (TILE, 4 * TILE), 1) // TILE
-        wanted = 4 * (x_pos ^ (pick_col // 2)) + 2 * core + pick_col % 2
-        pick = (pick_row == wanted).astype(F32).astype(BF16)
         tables = jnp.concatenate(
             [ref[rows : rows + EXTRA_ROWS, 0:TILE] for ref in arrivals], axis=0
         )
-        live = jnp.where(dot_nn(tables, pick) > 0.5, -SLOPE, DEAD)
+        live = jnp.where(dot_nn(tables, pick_ref[...]) > 0.5, -SLOPE, DEAD)
         for at, (side, (z, x)) in enumerate(names):
             group = (side * 2 + x) * 8
             for xs in range(2):
                 lane = PLACE[(z, xs)] * rows
                 bias[group : group + 8, lane : lane + rows] = live[
                     at * EXTRA_ROWS : at * EXTRA_ROWS + 8, xs * rows : (xs + 1) * rows
+                ]
+            if side == 0 and z == 0:
+                bias[group : group + 8, 8 * rows : 9 * rows] = live[
+                    at * EXTRA_ROWS : at * EXTRA_ROWS + 8, 2 * rows : 3 * rows
                 ]
     if stage == 0:
         total_ref[...] = jnp.zeros_like(total_ref)
@@ -181,7 +189,9 @@
                 kt_ref[low * rows + tile * TILE : low * rows + (tile + 1) * TILE, lanes] = value.astype(BF16)
     kept = total_ref.shape[0]
     for first, end, spans in tasks:
-        lanes = slice(first * rows, end * rows)
+        if first == 8:
+            continue
+        lanes = slice(first * rows, min(end, 8) * rows)
         total = total_ref[:, lanes]
         for low, high in spans:
             sources = slice(low * rows, high * rows)
@@ -215,27 +225,26 @@
         out_ref[:, lanes] = dot_nn(mine, kt_ref[0:own, lanes])[0:seed_cols]
 
 
-def step_kernel(rt_ref, kt_ref, gain_ref, half_ref, other_ref, out_ref):
-    seed_cols, own = out_ref.shape
+def step_kernel(rt_ref, kt_ref, gain_ref, half_ref, other_ref, mine_ref, sent_ref, ranks):
+    seed_cols, rows = mine_ref.shape
+    own = half_ref.shape[1]
     other = padded(other_ref[...])
     chunk = 512
     for c in range(own // chunk):
         lanes = slice(c * chunk, (c + 1) * chunk)
         total = half_ref[:, lanes] + dot_nn(other, kt_ref[own:, lanes])[0:seed_cols]
-        out_ref[:, lanes] = (
+        ranks[0:seed_cols, lanes] = (
             (1.0 - DAMPING) * rt_ref[0:seed_cols, lanes].astype(F32) + total * gain_ref[0:1, lanes]
         ).astype(BF16)
-
-
-def last_kernel(rt_ref, kt_ref, gain_ref, mine_ref, other_ref, out_ref):
+    ranks[seed_cols:, :] = jnp.zeros((ranks.shape[0] - seed_cols, own), BF16)
+    sent_ref[...] = dot_nn(ranks[...], kt_ref[0:own, own : own + rows])[0:seed_cols]
+    mine_ref[...] = dot_nn(ranks[...], kt_ref[0:own, 0:rows])[0:seed_cols]
+
+
+def last_kernel(rt_ref, gain_ref, mine_ref, other_ref, out_ref):
     seed_cols, rows = out_ref.shape
-    own = mine_ref.shape[1]
-    total = dot_nn(padded(mine_ref[...]), kt_ref[0:own, 0:rows]) + dot_nn(
-        padded(other_ref[...]), kt_ref[own:, 0:rows]
-    )
-    out_ref[...] = (1.0 - DAMPING) * rt_ref[0:seed_cols, 0:rows].astype(F32) + total[
-        0:seed_cols
-    ] * gain_ref[0:1, 0:rows]
+    total = mine_ref[...] + other_ref[...]
+    out_ref[...] = (1.0 - DAMPING) * rt_ref[0:seed_cols, 0:rows].astype(F32) + total * gain_ref[0:1, 0:rows]
 
 
 WHOLE = pl.BlockSpec(memory_space=pltpu.VMEM)
@@ -270,6 +279,10 @@
 
 def across(device):
     return device ^ 2
+
+
+def diagonal(device):
+    return device ^ 6
 
 
 def sibling(device):
@@ -302,95 +315,99 @@
     )(tile_count, in_hbm(embeddings), in_hbm(tile_list.reshape(2, slots)), in_hbm(seeds))
     state_shapes = [
         pltpu.VMEM((sessions, width), BF16),
-        pltpu.VMEM((32, own), F32),
-        pltpu.VMEM((sessions, own), BF16),
+        pltpu.VMEM((32, own + rows), F32),
+        pltpu.VMEM((sessions, own + rows), BF16),
         pltpu.VMEM((seed_cols + 8, own), F32),
     ]
     mark = [jax.ShapeDtypeStruct((8, TILE), F32)]
 
     def run_stage(stage, rt, arrivals, state, extra, *after):
-        first_state = 2 + len(arrivals)
+        first_state = 3 + len(arrivals)
         outs = pl.pallas_call(
             functools.partial(stage_kernel, stage),
-            in_specs=[SCALARS] + [WHOLE] * (1 + len(arrivals) + len(state)) + [REMAIN] * len(after),
+            in_specs=[SCALARS] + [WHOLE] * (2 + len(arrivals) + len(state)) + [REMAIN] * len(after),
             out_specs=[WHOLE] * (4 + len(extra)),
             out_shape=state_shapes + extra,
             input_output_aliases={first_state + k: k for k in range(len(state))},
             compiler_params=params(),
             cost_estimate=work(2.5),
             name=f"stage{stage}",
-        )(me, rt, *arrivals, *state, *after)
+        )(me, rt, pick, *arrivals, *state, *after)
         return outs[:4], outs[4:]
 
     z1 = swap(block, near)
     z2 = swap(block, far)
     x0 = swap(block, across)
     b00 = swap(block, sibling)
-    rt = pl.pallas_call(
+    rt, pick = pl.pallas_call(
         restart_kernel,
         in_specs=[SCALARS, WHOLE],
-        out_specs=WHOLE,
-        out_shape=jax.ShapeDtypeStruct((2 * seed_cols, sessions), BF16),
+        out_specs=[WHOLE] * 2,
+        out_shape=[
+            jax.ShapeDtypeStruct((2 * seed_cols, sessions), BF16),
+            jax.ShapeDtypeStruct((TILE, 6 * TILE), BF16),
+        ],
         scratch_shapes=[pltpu.VMEM((seed_cols, sessions // TILE, TILE), F32)],
         compiler_params=params(),
         cost_estimate=work(2.6),
         name="restart",
     )(me, seeds)
-    z1, rt = lax.optimization_barrier((z1, rt))
+    z1, x0, rt = lax.optimization_barrier((z1, x0, rt))
     x1 = swap(z1, across)
     b10 = swap(z1, sibling)
-    x0, z2, b00 = lax.optimization_barrier((x0, z2, b00))
+    b01 = swap(x0, sibling)
+    state, (done,) = run_stage(0, rt, [block, z1, x0], [], mark)
+    z2, b00, done = lax.optimization_barrier((z2, b00, done))
     z3 = swap(z2, near)
     x2 = swap(z2, across)
+    x3 = swap(z2, diagonal)
+    state, (done,) = run_stage(1, rt, [z2, x1, b00, b10, b01], state, mark, done)
+    z2, x1, done = lax.optimization_barrier((z2, x1, done))
     b20 = swap(z2, sibling)
-    b01 = swap(x0, sibling)
     b11 = swap(x1, sibling)
-    state, (done,) = run_stage(0, rt, [block, z1, x0, z2, x1, b00, b10], [], mark)
     x2, z3, done = lax.optimization_barrier((x2, z3, done))
-    x3 = swap(z3, across)
+    state, (done,) = run_stage(2, rt, [z3, x2], state, mark, done)
+    x2, z3, done = lax.optimization_barrier((x2, z3, done))
     b30 = swap(z3, sibling)
     b21 = swap(x2, sibling)
-    state, (done,) = run_stage(1, rt, [z3, x2, b01, b20, b11], state, mark, done)
-    state, (done,) = run_stage(2, rt, [b30, b21], state, mark, done)
-    x3, done = lax.optimization_barrier((x3, done))
     b31 = swap(x3, sibling)
-    state, (done,) = run_stage(3, rt, [x3], state, mark, done)
+    state, (done,) = run_stage(3, rt, [x3, b20, b11], state, mark, done)
     state, (ranks, gain) = run_stage(
         4,
         rt,
-        [b31],
+        [b30, b21, b31],
         state,
         [jax.ShapeDtypeStruct((seed_cols, own), BF16), jax.ShapeDtypeStruct((8, own), F32)],
     )
     kt = state[2]
-    for sweep in range(ITERS - 2):
-        half = pl.pallas_call(
-            half_kernel,
-            in_specs=[WHOLE] * 2,
-            out_specs=WHOLE,
-            out_shape=jax.ShapeDtypeStruct((seed_cols, own), F32),
-            compiler_params=params(),
-            cost_estimate=work(1.5),
-            name="half",
-        )(kt, ranks)
-        ranks = pl.pallas_call(
-            step_kernel,
-            in_specs=[WHOLE] * 5,
-            out_specs=WHOLE,
-            out_shape=jax.ShapeDtypeStruct((seed_cols, own), BF16),
-            compiler_params=params(),
-            cost_estimate=work(1.5),
-            name="step",
-        )(rt, kt, gain, half, swap(ranks, sibling))
+    half = pl.pallas_call(
+        half_kernel,
+        in_specs=[WHOLE] * 2,
+        out_specs=WHOLE,
+        out_shape=jax.ShapeDtypeStruct((seed_cols, own), F32),
+        compiler_params=params(),
+        cost_estimate=work(1.5),
+        name="half",
+    )(kt, ranks)
+    mine, sent = pl.pallas_call(
+        step_kernel,
+        in_specs=[WHOLE] * 5,
+        out_specs=[WHOLE] * 2,
+        out_shape=[jax.ShapeDtypeStruct((seed_cols, rows), F32)] * 2,
+        scratch_shapes=[pltpu.VMEM((2 * seed_cols, own), BF16)],
+        compiler_params=params(),
+        cost_estimate=work(1.5),
+        name="step",
+    )(rt, kt, gain, half, swap(ranks, sibling))
     result = pl.pallas_call(
         last_kernel,
-        in_specs=[WHOLE] * 5,
+        in_specs=[WHOLE] * 4,
         out_specs=WHOLE,
         out_shape=jax.ShapeDtypeStruct((seed_cols, rows), F32),
         compiler_params=params(),
         cost_estimate=work(0.5),
         name="last",
-    )(rt, kt, gain, ranks, swap(ranks, sibling))
+    )(rt, gain, mine, swap(sent, sibling))
     return result.T
 
 

time: 36 us -> 35 us (0.972)
  starting transfers between devices: 12.1 us -> 11.4 us
    ppermute x17, starting transfers between devices: 12.1 us -> 11.4 us  [swap(): return lax.ppermute(array, ('row', 'col'), pairs)]
  transfers between devices with their start and end apart: 17 -> 17, of which waited for: 5 -> 6; matrix products, arithmetic and copies ran while one was open for 0% -> 0% of each run, Pallas kernels for 32% -> 30%
where the time goes in v4:
time: 35 us; the launch traced here: 34.8 us
  Pallas kernels  16.1 us (46%)
  starting transfers between devices  11.4 us (33%)
  waiting for transfers between devices  6.54 us (19%)
  between operations  0.77 us (2%)
    ppermute x17, starting transfers between devices, swap(): return lax.ppermute(array, ('row', 'col'), pairs)  11.4 us
    pallas_call x5, Pallas kernels, run_stage(): pl.pallas_call(functools.partial(stage_kernel, stage), in_specs=[SCALARS]...  8.73 us
    ppermute x17, waiting for transfers between devices, swap(): return lax.ppermute(array, ('row', 'col'), pairs)  6.54 us
    pallas_call x1, Pallas kernels, chip_local(): pl.pallas_call(restart_kernel, in_specs=[SCALARS, WHOLE], out_specs=[WHOL...  2.74 us
    pallas_call x1, Pallas kernels, chip_local(): pl.pallas_call(step_kernel, in_specs=[WHOLE] * 5, out_specs=[WHOLE] * 2,...  1.59 us
    pallas_call x1, Pallas kernels, chip_local(): pl.pallas_call(half_kernel, in_specs=[WHOLE] * 2, out_specs=WHOLE, out_sh...  1.26 us
    pallas_call x1, Pallas kernels, chip_local(): pl.pallas_call(payload_kernel, in_specs=[SCALARS] + [REMAIN] * 3, out_spe...  1.09 us
  transfers between devices with their start and end apart: 17, of which 6 were waited for; matrix products, arithmetic and copies ran while one was open for 0% of the time, Pallas kernels for 30%

profile of v4, /device:TPU:0, one launch (start us, length us, event | category | flops | bytes accessed | tf_op | source)
XLA Modules:
  0.0 34.8 jit_solution(16081066269072414124)
XLA Ops:
  0.7 1.1 %payload.1 = (bf16[272,256]{1,0:T(8,128)(2,1)S(1)}, s32[64,128]{1,0:T(8,128)S(1)}) custom-call(s32[1,1]{1,0:T(1,128)S(6)} %copy.37.count_ref, bf16[256,256]{1,0:T(8,128)(2,1)} %emb_in.1, s32[2,48]{1,0:T(2,128)} %bitcast.3, s32[64,128]{1,0:T(8,128)} %seeds_in.1), custom_call_target="tpu_custom_call" | custom-call | tf_op jit(solution)/shard_map/payload/pallas_call | solution.py:300
  1.7 3.1 %collective-permute-start = (bf16[272,256]{1,0:T(8,128)(2,1)S(1)}, bf16[272,256]{1,0:T(8,128)(2,1)S(1)}, u32[]{:S(2)}, u32[]{:S(2)}) collective-permute-start(bf16[272,256]{1,0:T(8,128)(2,1)S(1)} %get-tuple-element.48.refs_0_), channel_id=1, source_target_pairs={{0,4},{1,5},{2,6},{3,7},{4,0},{5,1},{6,2},{7,3},{8,12},{9,13},{10,... | collective-permute-start | bytes 417800 | tf_op jit(solution)/shard_map/ppermute | solution.py:269
  4.8 1.5 %collective-permute-start.1 = (bf16[272,256]{1,0:T(8,128)(2,1)S(1)}, bf16[272,256]{1,0:T(8,128)(2,1)S(1)}, u32[]{:S(2)}, u32[]{:S(2)}) collective-permute-start(bf16[272,256]{1,0:T(8,128)(2,1)S(1)} %get-tuple-element.48.refs_0_), channel_id=1, source_target_pairs={{0,2},{1,3},{2,0},{3,1},{4,6},{5,7},{6,4},{7,5},{8,10},{9,11},{10,... | collective-permute-start | bytes 417800 | tf_op jit(solution)/shard_map/ppermute | solution.py:269
  6.3 2.6 %collective-permute-start.2 = (bf16[272,256]{1,0:T(8,128)(2,1)S(1)}, bf16[272,256]{1,0:T(8,128)(2,1)S(1)}, u32[]{:S(2)}, u32[]{:S(2)}) collective-permute-start(bf16[272,256]{1,0:T(8,128)(2,1)S(1)} %get-tuple-element.48.refs_0_), channel_id=1, source_target_pairs={{0,8},{1,9},{2,10},{3,11},{4,12},{5,13},{6,14},{7,15},{8,0},{9,1},... | collective-permute-start | bytes 417800 | tf_op jit(solution)/shard_map/ppermute | solution.py:269
  8.9 2.7 %restart.1 = (bf16[128,4096]{1,0:T(8,128)(2,1)S(1)}, bf16[128,768]{1,0:T(8,128)(2,1)S(1)}) custom-call(s32[1]{0:T(128)} %bitcast.1.me_ref, s32[64,128]{1,0:T(8,128)S(1)} %get-tuple-element.49.seeds_ref), custom_call_target="tpu_custom_call" | custom-call | flops 2600 | bytes 260 | tf_op jit(solution)/shard_map/restart/pallas_call | solution.py:342
  11.7 0.6 %collective-permute-start.6 = (bf16[272,256]{1,0:T(8,128)(2,1)S(1)}, bf16[272,256]{1,0:T(8,128)(2,1)S(1)}, u32[]{:S(2)}, u32[]{:S(2)}) collective-permute-start(bf16[272,256]{1,0:T(8,128)(2,1)S(1)} %collective-permute-done.refs_1_), channel_id=1, source_target_pairs={{0,2},{1,3},{2,0},{3,1},{4,6},{5,7},{6,4},{7,5},{8,10},{9,11},{10,... | collective-permute-start | bytes 417800 | tf_op jit(solution)/shard_map/ppermute | solution.py:269
  12.8 0.7 %stage0.1 = (bf16[4096,256]{1,0:T(8,128)(2,1)S(1)}, f32[32,2304]{1,0:T(8,128)S(1)}, bf16[4096,2304]{1,0:T(8,128)(2,1)S(1)}, f32[72,2048]{1,0:T(8,128)S(1)}, f32[8,128]{1,0:T(8,128)S(1)}) custom-call(s32[1]{0:T(128)} %bitcast.1.me_ref, bf16[128,4096]{1,0:T(8,128)(2,1)S(1)} %get-tuple-element.51.rt_ref, bf16[128,768]{1,0:T(8,128)(2,1)S(1)} %get-tuple-element.52.pick_ref, ...), custom_call_target="tpu_custom_call" | custom-call | flops 2500 | bytes 250 | tf_op jit(solution)/shard_map/stage0/pallas_call | solution.py:326
  13.5 1.5 %collective-permute-done.2.refs_0_ = bf16[272,256]{1,0:T(8,128)(2,1)S(1)} collective-permute-done((bf16[272,256]{1,0:T(8,128)(2,1)S(1)}, bf16[272,256]{1,0:T(8,128)(2,1)S(1)}, u32[]{:S(2)}, u32[]{:S(2)}) %collective-permute-start.2) | collective-permute-done | bytes 139296 | tf_op jit(solution)/shard_map/ppermute | solution.py:269
  15.1 0.6 %collective-permute-start.4 = (bf16[272,256]{1,0:T(8,128)(2,1)S(1)}, bf16[272,256]{1,0:T(8,128)(2,1)S(1)}, u32[]{:S(2)}, u32[]{:S(2)}) collective-permute-start(bf16[272,256]{1,0:T(8,128)(2,1)S(1)} %collective-permute-done.2.refs_0_), channel_id=1, source_target_pairs={{0,2},{1,3},{2,0},{3,1},{4,6},{5,7},{6,4},{7,5},{8,10},{9,11},{10,... | collective-permute-start | bytes 417800 | tf_op jit(solution)/shard_map/ppermute | solution.py:269
  15.8 2.4 %collective-permute-done.6.refs_1_ = bf16[272,256]{1,0:T(8,128)(2,1)S(1)} collective-permute-done((bf16[272,256]{1,0:T(8,128)(2,1)S(1)}, bf16[272,256]{1,0:T(8,128)(2,1)S(1)}, u32[]{:S(2)}, u32[]{:S(2)}) %collective-permute-start.6) | collective-permute-done | bytes 139296 | tf_op jit(solution)/shard_map/ppermute | solution.py:269
  18.7 1.7 %stage1.1 = (bf16[4096,256]{1,0:T(8,128)(2,1)S(1)}, f32[32,2304]{1,0:T(8,128)S(1)}, bf16[4096,2304]{1,0:T(8,128)(2,1)S(1)}, f32[72,2048]{1,0:T(8,128)S(1)}, f32[8,128]{1,0:T(8,128)S(1)}) custom-call(s32[1]{0:T(128)} %bitcast.1.me_ref, ...), custom_call_target="tpu_custom_call", output_to_operand_aliasing={{0}: (8, {}), {1}: (9, {}), {2}: (10, {}), {3}: (11, {})} | custom-call | flops 2500 | bytes 250 | tf_op jit(solution)/shard_map/stage1/pallas_call | solution.py:326
  20.4 0.4 %collective-permute-done.4.refs_1_ = bf16[272,256]{1,0:T(8,128)(2,1)S(1)} collective-permute-done((bf16[272,256]{1,0:T(8,128)(2,1)S(1)}, bf16[272,256]{1,0:T(8,128)(2,1)S(1)}, u32[]{:S(2)}, u32[]{:S(2)}) %collective-permute-start.4) | collective-permute-done | bytes 139296 | tf_op jit(solution)/shard_map/ppermute | solution.py:269
  20.8 0.5 %collective-permute-done.5.refs_0_ = bf16[272,256]{1,0:T(8,128)(2,1)S(1)} collective-permute-done((bf16[272,256]{1,0:T(8,128)(2,1)S(1)}, bf16[272,256]{1,0:T(8,128)(2,1)S(1)}, u32[]{:S(2)}, u32[]{:S(2)}) %collective-permute-start.5) | collective-permute-done | bytes 139296 | tf_op jit(solution)/shard_map/ppermute | solution.py:269
  21.3 0.5 %collective-permute-start.14 = (bf16[272,256]{1,0:T(8,128)(2,1)S(1)}, bf16[272,256]{1,0:T(8,128)(2,1)S(1)}, u32[]{:S(2)}, u32[]{:S(2)}) collective-permute-start(bf16[272,256]{1,0:T(8,128)(2,1)S(1)} %collective-permute-done.6.refs_1_), channel_id=1, source_target_pairs={{0,1},{1,0},{2,3},{3,2},{4,5},{5,4},{6,7},{7,6},{8,9},{9,8},{10,11... | collective-permute-start | bytes 417800 | tf_op jit(solution)/shard_map/ppermute | solution.py:269
  21.8 1.5 %stage2.1 = (bf16[4096,256]{1,0:T(8,128)(2,1)S(1)}, f32[32,2304]{1,0:T(8,128)S(1)}, bf16[4096,2304]{1,0:T(8,128)(2,1)S(1)}, f32[72,2048]{1,0:T(8,128)S(1)}, f32[8,128]{1,0:T(8,128)S(1)}) custom-call(s32[1]{0:T(128)} %bitcast.1.me_ref, ...), custom_call_target="tpu_custom_call", output_to_operand_aliasing={{0}: (5, {}), {1}: (6, {}), {2}: (7, {}), {3}: (8, {})} | custom-call | flops 2500 | bytes 250 | tf_op jit(solution)/shard_map/stage2/pallas_call | solution.py:326
  23.4 0.5 %collective-permute-start.9 = (bf16[272,256]{1,0:T(8,128)(2,1)S(1)}, bf16[272,256]{1,0:T(8,128)(2,1)S(1)}, u32[]{:S(2)}, u32[]{:S(2)}) collective-permute-start(bf16[272,256]{1,0:T(8,128)(2,1)S(1)} %collective-permute-done.5.refs_0_), channel_id=1, source_target_pairs={{0,1},{1,0},{2,3},{3,2},{4,5},{5,4},{6,7},{7,6},{8,9},{9,8},{10,11... | collective-permute-start | bytes 417800 | tf_op jit(solution)/shard_map/ppermute | solution.py:269
  23.9 0.7 %collective-permute-done.11.refs_0_ = bf16[272,256]{1,0:T(8,128)(2,1)S(1)} collective-permute-done((bf16[272,256]{1,0:T(8,128)(2,1)S(1)}, bf16[272,256]{1,0:T(8,128)(2,1)S(1)}, u32[]{:S(2)}, u32[]{:S(2)}) %collective-permute-start.11) | collective-permute-done | bytes 139296 | tf_op jit(solution)/shard_map/ppermute | solution.py:269
  24.6 2.5 %stage3.1 = (bf16[4096,256]{1,0:T(8,128)(2,1)S(1)}, f32[32,2304]{1,0:T(8,128)S(1)}, bf16[4096,2304]{1,0:T(8,128)(2,1)S(1)}, f32[72,2048]{1,0:T(8,128)S(1)}, f32[8,128]{1,0:T(8,128)}) custom-call(s32[1]{0:T(128)} %bitcast.1.me_ref, ...), custom_call_target="tpu_custom_call", output_to_operand_aliasing={{0}: (6, {}), {1}: (7, {}), {2}: (8, {}), {3}: (9, {})} | custom-call | flops 2500 | bytes 250 | tf_op jit(solution)/shard_map/stage3/pallas_call | solution.py:326
  27.1 2.3 %stage4.1 = (bf16[4096,256]{1,0:T(8,128)(2,1)S(1)}, f32[32,2304]{1,0:T(8,128)S(1)}, bf16[4096,2304]{1,0:T(8,128)(2,1)S(1)}, f32[72,2048]{1,0:T(8,128)S(1)}, bf16...) custom-call(s32[1]{0:T(128)} %bitcast.1.me_ref, ...), custom_call_target="tpu_custom_call", output_to_operand_aliasing={{0}: (6, {}), {1}: (7, {}), {2}: (8, {}), {3}: (9, {})} | custom-call | flops 2500 | bytes 250 | tf_op jit(solution)/shard_map/stage4/pallas_call | solution.py:326
  29.4 0.6 %collective-permute-start.15 = (bf16[64,2048]{1,0:T(8,128)(2,1)S(1)}, bf16[64,2048]{1,0:T(8,128)(2,1)S(1)}, u32[]{:S(2)}, u32[]{:S(2)}) collective-permute-start(bf16[64,2048]{1,0:T(8,128)(2,1)S(1)} %get-tuple-element.88.mine_ref), channel_id=1, source_target_pairs={{0,1},{1,0},{2,3},{3,2},{4,5},{5,4},{6,7},{7,6},{8,9},{9,8},{10,11... | collective-permute-start | bytes 786440 | tf_op jit(solution)/shard_map/ppermute | solution.py:269
  30.0 1.3 %half.1.half_ref = f32[64,2048]{1,0:T(8,128)S(1)} custom-call(bf16[4096,2304]{1,0:T(8,128)(2,1)S(1)} %get-tuple-element.87.kt_ref, bf16[64,2048]{1,0:T(8,128)(2,1)S(1)} %get-tuple-element.88.mine_ref), custom_call_target="tpu_custom_call" | custom-call | flops 1500 | bytes 150 | tf_op jit(solution)/shard_map/half/pallas_call | solution.py:383
  31.2 1.6 %step.1 = (f32[64,256]{1,0:T(8,128)S(1)}, f32[64,256]{1,0:T(8,128)S(1)}) custom-call(bf16[128,4096]{1,0:T(8,128)(2,1)S(1)} %get-tuple-element.51.rt_ref, bf16[4096,2304]{1,0:T(8,128)(2,1)S(1)} %get-tuple-element.87.kt_ref, f32[8,2048]{1,0:T(8,128)S(1)} %get-tuple-element.86.gain_ref, f32[64,2048]{1,0:T(8,128)S(1)} %half.1.half_ref, ...), custom_call_target="tpu_custom_call" | custom-call | flops 1500 | bytes 150 | tf_op jit(solution)/shard_map/step/pallas_call | solution.py:392
  33.2 1.0 %collective-permute-done.16.other_ref = f32[64,256]{1,0:T(8,128)S(1)} collective-permute-done((f32[64,256]{1,0:T(8,128)S(1)}, f32[64,256]{1,0:T(8,128)S(1)}, u32[]{:S(2)}, u32[]{:S(2)}) %collective-permute-start.16) | collective-permute-done | bytes 65568 | tf_op jit(solution)/shard_map/ppermute | solution.py:269
  34.2 0.6 %last.1 = f32[64,256]{1,0:T(8,128)} custom-call(bf16[128,4096]{1,0:T(8,128)(2,1)S(1)} %get-tuple-element.51.rt_ref, f32[8,2048]{1,0:T(8,128)S(1)} %get-tuple-element.86.gain_ref, f32[64,256]{1,0:T(8,128)S(1)} %get-tuple-element.89.mine_ref, f32[64,256]{1,0:T(8,128)S(1)} %collective-permute-done.16.other_ref), custom_call_target="tpu_custom_call" | custom-call | flops 500 | bytes 50 | tf_op jit(solution)/shard_map/last/pallas_call | solution.py:402
  (20 shorter events, 1.5 us)
Async XLA Ops:
  1.7 9.9 %collective-permute-start = (bf16[272,256]{1,0:T(8,128)(2,1)S(1)}, bf16[272,256]{1,0:T(8,128)(2,1)S(1)}, u32[]{:S(2)}, u32[]{:S(2)}) collective-permute-start(bf16[272,256]{1,0:T(8,128)(2,1)S(1)} %get-tuple-element.48.refs_0_), channel_id=1, source_target_pairs={{0,4},{1,5},{2,6},{3,7},{4,0},{5,1},{6,2},{7,3},{8,12},{9,13},{10,... | collective-permute-start | bytes 417800 | tf_op jit(solution)/shard_map/ppermute | solution.py:269
  4.8 6.8 %collective-permute-start.1 = (bf16[272,256]{1,0:T(8,128)(2,1)S(1)}, bf16[272,256]{1,0:T(8,128)(2,1)S(1)}, u32[]{:S(2)}, u32[]{:S(2)}) collective-permute-start(bf16[272,256]{1,0:T(8,128)(2,1)S(1)} %get-tuple-element.48.refs_0_), channel_id=1, source_target_pairs={{0,2},{1,3},{2,0},{3,1},{4,6},{5,7},{6,4},{7,5},{8,10},{9,11},{10,... | collective-permute-start | bytes 417800 | tf_op jit(solution)/shard_map/ppermute | solution.py:269
  6.3 8.7 %collective-permute-start.2 = (bf16[272,256]{1,0:T(8,128)(2,1)S(1)}, bf16[272,256]{1,0:T(8,128)(2,1)S(1)}, u32[]{:S(2)}, u32[]{:S(2)}) collective-permute-start(bf16[272,256]{1,0:T(8,128)(2,1)S(1)} %get-tuple-element.48.refs_0_), channel_id=1, source_target_pairs={{0,8},{1,9},{2,10},{3,11},{4,12},{5,13},{6,14},{7,15},{8,0},{9,1},... | collective-permute-start | bytes 417800 | tf_op jit(solution)/shard_map/ppermute | solution.py:269
  8.9 6.1 %collective-permute-start.3 = (bf16[272,256]{1,0:T(8,128)(2,1)S(1)}, bf16[272,256]{1,0:T(8,128)(2,1)S(1)}, u32[]{:S(2)}, u32[]{:S(2)}) collective-permute-start(bf16[272,256]{1,0:T(8,128)(2,1)S(1)} %get-tuple-element.48.refs_0_), channel_id=1, source_target_pairs={{0,1},{1,0},{2,3},{3,2},{4,5},{5,4},{6,7},{7,6},{8,9},{9,8},{10,11... | collective-permute-start | bytes 417800 | tf_op jit(solution)/shard_map/ppermute | solution.py:269
  11.7 6.5 %collective-permute-start.6 = (bf16[272,256]{1,0:T(8,128)(2,1)S(1)}, bf16[272,256]{1,0:T(8,128)(2,1)S(1)}, u32[]{:S(2)}, u32[]{:S(2)}) collective-permute-start(bf16[272,256]{1,0:T(8,128)(2,1)S(1)} %collective-permute-done.refs_1_), channel_id=1, source_target_pairs={{0,2},{1,3},{2,0},{3,1},{4,6},{5,7},{6,4},{7,5},{8,10},{9,11},{10,... | collective-permute-start | bytes 417800 | tf_op jit(solution)/shard_map/ppermute | solution.py:269
  12.3 6.4 %collective-permute-start.7 = (bf16[272,256]{1,0:T(8,128)(2,1)S(1)}, bf16[272,256]{1,0:T(8,128)(2,1)S(1)}, u32[]{:S(2)}, u32[]{:S(2)}) collective-permute-start(bf16[272,256]{1,0:T(8,128)(2,1)S(1)} %collective-permute-done.refs_1_), channel_id=1, source_target_pairs={{0,1},{1,0},{2,3},{3,2},{4,5},{5,4},{6,7},{7,6},{8,9},{9,8},{10,11... | collective-permute-start | bytes 417800 | tf_op jit(solution)/shard_map/ppermute | solution.py:269
  12.5 6.1 %collective-permute-start.8 = (bf16[272,256]{1,0:T(8,128)(2,1)S(1)}, bf16[272,256]{1,0:T(8,128)(2,1)S(1)}, u32[]{:S(2)}, u32[]{:S(2)}) collective-permute-start(bf16[272,256]{1,0:T(8,128)(2,1)S(1)} %collective-permute-done.1.refs_2_), channel_id=1, source_target_pairs={{0,1},{1,0},{2,3},{3,2},{4,5},{5,4},{6,7},{7,6},{8,9},{9,8},{10,11... | collective-permute-start | bytes 417800 | tf_op jit(solution)/shard_map/ppermute | solution.py:269
  15.1 5.8 %collective-permute-start.4 = (bf16[272,256]{1,0:T(8,128)(2,1)S(1)}, bf16[272,256]{1,0:T(8,128)(2,1)S(1)}, u32[]{:S(2)}, u32[]{:S(2)}) collective-permute-start(bf16[272,256]{1,0:T(8,128)(2,1)S(1)} %collective-permute-done.2.refs_0_), channel_id=1, source_target_pairs={{0,2},{1,3},{2,0},{3,1},{4,6},{5,7},{6,4},{7,5},{8,10},{9,11},{10,... | collective-permute-start | bytes 417800 | tf_op jit(solution)/shard_map/ppermute | solution.py:269
  15.7 5.7 %collective-permute-start.5 = (bf16[272,256]{1,0:T(8,128)(2,1)S(1)}, bf16[272,256]{1,0:T(8,128)(2,1)S(1)}, u32[]{:S(2)}, u32[]{:S(2)}) collective-permute-start(bf16[272,256]{1,0:T(8,128)(2,1)S(1)} %collective-permute-done.2.refs_0_), channel_id=1, source_target_pairs={{0,4},{1,5},{2,6},{3,7},{4,0},{5,1},{6,2},{7,3},{8,12},{9,13},{10,... | collective-permute-start | bytes 417800 | tf_op jit(solution)/shard_map/ppermute | solution.py:269
  18.2 6.3 %collective-permute-start.11 = (bf16[272,256]{1,0:T(8,128)(2,1)S(1)}, bf16[272,256]{1,0:T(8,128)(2,1)S(1)}, u32[]{:S(2)}, u32[]{:S(2)}) collective-permute-start(bf16[272,256]{1,0:T(8,128)(2,1)S(1)} %collective-permute-done.2.refs_0_), channel_id=1, source_target_pairs={{0,6},{1,7},{2,4},{3,5},{4,2},{5,3},{6,0},{7,1},{8,14},{9,15},{10,... | collective-permute-start | bytes 417800 | tf_op jit(solution)/shard_map/ppermute | solution.py:269
  21.3 3.3 %collective-permute-start.13 = (bf16[272,256]{1,0:T(8,128)(2,1)S(1)}, bf16[272,256]{1,0:T(8,128)(2,1)S(1)}, u32[]{:S(2)}, u32[]{:S(2)}) collective-permute-start(bf16[272,256]{1,0:T(8,128)(2,1)S(1)} %collective-permute-done.2.refs_0_), channel_id=1, source_target_pairs={{0,1},{1,0},{2,3},{3,2},{4,5},{5,4},{6,7},{7,6},{8,9},{9,8},{10,11... | collective-permute-start | bytes 417800 | tf_op jit(solution)/shard_map/ppermute | solution.py:269
  21.3 3.3 %collective-permute-start.14 = (bf16[272,256]{1,0:T(8,128)(2,1)S(1)}, bf16[272,256]{1,0:T(8,128)(2,1)S(1)}, u32[]{:S(2)}, u32[]{:S(2)}) collective-permute-start(bf16[272,256]{1,0:T(8,128)(2,1)S(1)} %collective-permute-done.6.refs_1_), channel_id=1, source_target_pairs={{0,1},{1,0},{2,3},{3,2},{4,5},{5,4},{6,7},{7,6},{8,9},{9,8},{10,11... | collective-permute-start | bytes 417800 | tf_op jit(solution)/shard_map/ppermute | solution.py:269
  23.3 3.8 %collective-permute-start.10 = (bf16[272,256]{1,0:T(8,128)(2,1)S(1)}, bf16[272,256]{1,0:T(8,128)(2,1)S(1)}, u32[]{:S(2)}, u32[]{:S(2)}) collective-permute-start(bf16[272,256]{1,0:T(8,128)(2,1)S(1)} %collective-permute-done.4.refs_1_), channel_id=1, source_target_pairs={{0,1},{1,0},{2,3},{3,2},{4,5},{5,4},{6,7},{7,6},{8,9},{9,8},{10,11... | collective-permute-start | bytes 417800 | tf_op jit(solution)/shard_map/ppermute | solution.py:269
  23.4 3.7 %collective-permute-start.9 = (bf16[272,256]{1,0:T(8,128)(2,1)S(1)}, bf16[272,256]{1,0:T(8,128)(2,1)S(1)}, u32[]{:S(2)}, u32[]{:S(2)}) collective-permute-start(bf16[272,256]{1,0:T(8,128)(2,1)S(1)} %collective-permute-done.5.refs_0_), channel_id=1, source_target_pairs={{0,1},{1,0},{2,3},{3,2},{4,5},{5,4},{6,7},{7,6},{8,9},{9,8},{10,11... | collective-permute-start | bytes 417800 | tf_op jit(solution)/shard_map/ppermute | solution.py:269
  24.6 2.6 %collective-permute-start.12 = (bf16[272,256]{1,0:T(8,128)(2,1)S(1)}, bf16[272,256]{1,0:T(8,128)(2,1)S(1)}, u32[]{:S(2)}, u32[]{:S(2)}) collective-permute-start(bf16[272,256]{1,0:T(8,128)(2,1)S(1)} %collective-permute-done.11.refs_0_), channel_id=1, source_target_pairs={{0,1},{1,0},{2,3},{3,2},{4,5},{5,4},{6,7},{7,6},{8,9},{9,8},{10,11... | collective-permute-start | bytes 417800 | tf_op jit(solution)/shard_map/ppermute | solution.py:269
  29.4 1.8 %collective-permute-start.15 = (bf16[64,2048]{1,0:T(8,128)(2,1)S(1)}, bf16[64,2048]{1,0:T(8,128)(2,1)S(1)}, u32[]{:S(2)}, u32[]{:S(2)}) collective-permute-start(bf16[64,2048]{1,0:T(8,128)(2,1)S(1)} %get-tuple-element.88.mine_ref), channel_id=1, source_target_pairs={{0,1},{1,0},{2,3},{3,2},{4,5},{5,4},{6,7},{7,6},{8,9},{9,8},{10,11... | collective-permute-start | bytes 786440 | tf_op jit(solution)/shard_map/ppermute | solution.py:269
  32.8 1.3 %collective-permute-start.16 = (f32[64,256]{1,0:T(8,128)S(1)}, f32[64,256]{1,0:T(8,128)S(1)}, u32[]{:S(2)}, u32[]{:S(2)}) collective-permute-start(f32[64,256]{1,0:T(8,128)S(1)} %get-tuple-element.90), channel_id=1, source_target_pairs={{0,1},{1,0},{2,3},{3,2},{4,5},{5,4},{6,7},{7,6},{8,9},{9,8},{10,11... | collective-permute-start | bytes 196616 | tf_op jit(solution)/shard_map/ppermute | solution.py:269

commit v5 on v4

--- a/solution.py
+++ b/solution.py
@@ -32,21 +32,23 @@
     return (widened * factor * widened.shape[-1] ** (-0.5)).astype(BF16)
 
 
-ORDER = ((0, 0), (1, 0), (2, 0), (0, 1), (1, 1), (2, 1), (3, 0), (3, 1))
+ORDER = ((0, 0), (0, 1), (1, 1), (1, 0), (2, 0), (2, 1), (3, 0), (3, 1))
 PLACE = {block: place for place, block in enumerate(ORDER)}
 OWN_STAGES = (
     ((0, 0), (1, 0), (0, 1)),
-    ((2, 0), (1, 1)),
+    ((2, 0),),
+    ((1, 1),),
     ((3, 0), (2, 1)),
     ((3, 1),),
     (),
 )
 OTHER_STAGES = (
     (),
-    ((0, 0), (1, 0), (0, 1)),
-    (),
+    ((0, 0),),
+    ((1, 0), (0, 1)),
     ((2, 0), (1, 1)),
-    ((3, 0), (2, 1), (3, 1)),
+    ((3, 0), (2, 1)),
+    ((3, 1),),
 )
 
 
@@ -192,13 +194,12 @@
         if first == 8:
             continue
         lanes = slice(first * rows, min(end, 8) * rows)
-        total = total_ref[:, lanes]
-        for low, high in spans:
-            sources = slice(low * rows, high * rows)
-            total = total + dot_nn(rt_ref[:, sources], kt_ref[sources, lanes])[0:kept]
-        total_ref[:, lanes] = total
+        scores = jnp.concatenate([rt_ref[:, low * rows : high * rows] for low, high in spans], axis=1)
+        values = jnp.concatenate([kt_ref[low * rows : high * rows, lanes] for low, high in spans], axis=0)
+        total_ref[:, lanes] = total_ref[:, lanes] + dot_nn(scores, values)[0:kept]
     if stage < len(OWN_STAGES) - 1:
-        refs[0][...] = jnp.zeros_like(refs[0])
+        if refs:
+            refs[0][...] = jnp.zeros_like(refs[0])
         return
     next_ref, gain_ref = refs
     seed_cols = next_ref.shape[0]
@@ -360,22 +361,23 @@
     z2, b00, done = lax.optimization_barrier((z2, b00, done))
     z3 = swap(z2, near)
     x2 = swap(z2, across)
+    state, (done,) = run_stage(1, rt, [z2, b00], state, mark, done)
+    z2, done = lax.optimization_barrier((z2, done))
     x3 = swap(z2, diagonal)
-    state, (done,) = run_stage(1, rt, [z2, x1, b00, b10, b01], state, mark, done)
-    z2, x1, done = lax.optimization_barrier((z2, x1, done))
     b20 = swap(z2, sibling)
     b11 = swap(x1, sibling)
-    x2, z3, done = lax.optimization_barrier((x2, z3, done))
-    state, (done,) = run_stage(2, rt, [z3, x2], state, mark, done)
+    state, (done,) = run_stage(2, rt, [x1, b10, b01], state, mark, done)
     x2, z3, done = lax.optimization_barrier((x2, z3, done))
     b30 = swap(z3, sibling)
     b21 = swap(x2, sibling)
+    state, (done,) = run_stage(3, rt, [z3, x2, b20, b11], state, mark, done)
+    x3, done = lax.optimization_barrier((x3, done))
     b31 = swap(x3, sibling)
-    state, (done,) = run_stage(3, rt, [x3, b20, b11], state, mark, done)
+    state, _ = run_stage(4, rt, [x3, b30, b21], state, [], done)
     state, (ranks, gain) = run_stage(
-        4,
+        5,
         rt,
-        [b30, b21, b31],
+        [b31],
         state,
         [jax.ShapeDtypeStruct((seed_cols, own), BF16), jax.ShapeDtypeStruct((8, own), F32)],
     )

time: 35 us -> 34.3 us (0.980)
  waiting for transfers between devices: 6.54 us -> 5.34 us
  starting transfers between devices: 11.4 us -> 12.3 us
    ppermute x17, waiting for transfers between devices: 6.54 us -> 5.34 us  [swap(): return lax.ppermute(array, ('row', 'col'), pairs)]
    ppermute x17, starting transfers between devices: 11.4 us -> 12.3 us  [swap(): return lax.ppermute(array, ('row', 'col'), pairs)]
    pallas_call x5 -> x6, Pallas kernels: 8.73 us -> 8.44 us  [run_stage(): pl.pallas_call(functools.partial(stage_kernel, stage), in_specs=[SCALARS]...]
  transfers between devices with their start and end apart: 17 -> 17, of which waited for: 6 -> 4; matrix products, arithmetic and copies ran while one was open for 0% -> 0% of each run, Pallas kernels for 30% -> 34%
where the time goes in v5:
time: 34.3 us; the launch traced here: 34.2 us
  Pallas kernels  15.8 us (46%)
  starting transfers between devices  12.3 us (36%)
  waiting for transfers between devices  5.34 us (16%)
  between operations  0.8 us (2%)
    ppermute x17, starting transfers between devices, swap(): return lax.ppermute(array, ('row', 'col'), pairs)  12.3 us
    pallas_call x6, Pallas kernels, run_stage(): pl.pallas_call(functools.partial(stage_kernel, stage), in_specs=[SCALARS]...  8.44 us
    ppermute x17, waiting for transfers between devices, swap(): return lax.ppermute(array, ('row', 'col'), pairs)  5.34 us
    pallas_call x1, Pallas kernels, chip_local(): pl.pallas_call(restart_kernel, in_specs=[SCALARS, WHOLE], out_specs=[WHOL...  2.74 us
    pallas_call x1, Pallas kernels, chip_local(): pl.pallas_call(step_kernel, in_specs=[WHOLE] * 5, out_specs=[WHOLE] * 2,...  1.59 us
    pallas_call x1, Pallas kernels, chip_local(): pl.pallas_call(half_kernel, in_specs=[WHOLE] * 2, out_specs=WHOLE, out_sh...  1.26 us
    pallas_call x1, Pallas kernels, chip_local(): pl.pallas_call(payload_kernel, in_specs=[SCALARS] + [REMAIN] * 3, out_spe...  1.09 us
  transfers between devices with their start and end apart: 17, of which 4 were waited for; matrix products, arithmetic and copies ran while one was open for 0% of the time, Pallas kernels for 34%

profile of v5, /device:TPU:0, one launch (start us, length us, event | category | flops | bytes accessed | tf_op | source)
XLA Modules:
  0.0 34.2 jit_solution(2111025955818613760)
XLA Ops:
  0.7 1.1 %payload.1 = (bf16[272,256]{1,0:T(8,128)(2,1)S(1)}, s32[64,128]{1,0:T(8,128)S(1)}) custom-call(s32[1,1]{1,0:T(1,128)S(6)} %copy.45.count_ref, bf16[256,256]{1,0:T(8,128)(2,1)} %emb_in.1, s32[2,48]{1,0:T(2,128)} %bitcast.3, s32[64,128]{1,0:T(8,128)} %seeds_in.1), custom_call_target="tpu_custom_call" | custom-call | tf_op jit(solution)/shard_map/payload/pallas_call | solution.py:301
  1.7 3.1 %collective-permute-start = (bf16[272,256]{1,0:T(8,128)(2,1)S(1)}, bf16[272,256]{1,0:T(8,128)(2,1)S(1)}, u32[]{:S(2)}, u32[]{:S(2)}) collective-permute-start(bf16[272,256]{1,0:T(8,128)(2,1)S(1)} %get-tuple-element.51.refs_0_), channel_id=1, source_target_pairs={{0,4},{1,5},{2,6},{3,7},{4,0},{5,1},{6,2},{7,3},{8,12},{9,13},{10,... | collective-permute-start | bytes 417800 | tf_op jit(solution)/shard_map/ppermute | solution.py:270
  4.8 1.5 %collective-permute-start.1 = (bf16[272,256]{1,0:T(8,128)(2,1)S(1)}, bf16[272,256]{1,0:T(8,128)(2,1)S(1)}, u32[]{:S(2)}, u32[]{:S(2)}) collective-permute-start(bf16[272,256]{1,0:T(8,128)(2,1)S(1)} %get-tuple-element.51.refs_0_), channel_id=1, source_target_pairs={{0,2},{1,3},{2,0},{3,1},{4,6},{5,7},{6,4},{7,5},{8,10},{9,11},{10,... | collective-permute-start | bytes 417800 | tf_op jit(solution)/shard_map/ppermute | solution.py:270
  6.3 2.6 %collective-permute-start.2 = (bf16[272,256]{1,0:T(8,128)(2,1)S(1)}, bf16[272,256]{1,0:T(8,128)(2,1)S(1)}, u32[]{:S(2)}, u32[]{:S(2)}) collective-permute-start(bf16[272,256]{1,0:T(8,128)(2,1)S(1)} %get-tuple-element.51.refs_0_), channel_id=1, source_target_pairs={{0,8},{1,9},{2,10},{3,11},{4,12},{5,13},{6,14},{7,15},{8,0},{9,1},... | collective-permute-start | bytes 417800 | tf_op jit(solution)/shard_map/ppermute | solution.py:270
  8.9 2.7 %restart.1 = (bf16[128,4096]{1,0:T(8,128)(2,1)S(1)}, bf16[128,768]{1,0:T(8,128)(2,1)S(1)}) custom-call(s32[1]{0:T(128)} %bitcast.1.me_ref, s32[64,128]{1,0:T(8,128)S(1)} %get-tuple-element.52.seeds_ref), custom_call_target="tpu_custom_call" | custom-call | flops 2600 | bytes 260 | tf_op jit(solution)/shard_map/restart/pallas_call | solution.py:343
  11.7 0.6 %collective-permute-start.7 = (bf16[272,256]{1,0:T(8,128)(2,1)S(1)}, bf16[272,256]{1,0:T(8,128)(2,1)S(1)}, u32[]{:S(2)}, u32[]{:S(2)}) collective-permute-start(bf16[272,256]{1,0:T(8,128)(2,1)S(1)} %collective-permute-done.refs_1_), channel_id=1, source_target_pairs={{0,2},{1,3},{2,0},{3,1},{4,6},{5,7},{6,4},{7,5},{8,10},{9,11},{10,... | collective-permute-start | bytes 417800 | tf_op jit(solution)/shard_map/ppermute | solution.py:270
  12.8 0.7 %stage0.1 = (bf16[4096,256]{1,0:T(8,128)(2,1)S(1)}, f32[32,2304]{1,0:T(8,128)S(1)}, bf16[4096,2304]{1,0:T(8,128)(2,1)S(1)}, f32[72,2048]{1,0:T(8,128)S(1)}, f32[8,128]{1,0:T(8,128)S(1)}) custom-call(s32[1]{0:T(128)} %bitcast.1.me_ref, bf16[128,4096]{1,0:T(8,128)(2,1)S(1)} %get-tuple-element.54.rt_ref, bf16[128,768]{1,0:T(8,128)(2,1)S(1)} %get-tuple-element.55.pick_ref, ...), custom_call_target="tpu_custom_call" | custom-call | flops 2500 | bytes 250 | tf_op jit(solution)/shard_map/stage0/pallas_call | solution.py:327
  13.5 1.6 %collective-permute-done.2.refs_0_ = bf16[272,256]{1,0:T(8,128)(2,1)S(1)} collective-permute-done((bf16[272,256]{1,0:T(8,128)(2,1)S(1)}, bf16[272,256]{1,0:T(8,128)(2,1)S(1)}, u32[]{:S(2)}, u32[]{:S(2)}) %collective-permute-start.2) | collective-permute-done | bytes 139296 | tf_op jit(solution)/shard_map/ppermute | solution.py:270
  15.1 0.6 %collective-permute-start.5 = (bf16[272,256]{1,0:T(8,128)(2,1)S(1)}, bf16[272,256]{1,0:T(8,128)(2,1)S(1)}, u32[]{:S(2)}, u32[]{:S(2)}) collective-permute-start(bf16[272,256]{1,0:T(8,128)(2,1)S(1)} %collective-permute-done.2.refs_0_), channel_id=1, source_target_pairs={{0,2},{1,3},{2,0},{3,1},{4,6},{5,7},{6,4},{7,5},{8,10},{9,11},{10,... | collective-permute-start | bytes 417800 | tf_op jit(solution)/shard_map/ppermute | solution.py:270
  15.8 0.8 %stage1.1 = (bf16[4096,256]{1,0:T(8,128)(2,1)S(1)}, f32[32,2304]{1,0:T(8,128)S(1)}, bf16[4096,2304]{1,0:T(8,128)(2,1)S(1)}, f32[72,2048]{1,0:T(8,128)S(1)}, f32[8,128]{1,0:T(8,128)S(1)}) custom-call(s32[1]{0:T(128)} %bitcast.1.me_ref, ...), custom_call_target="tpu_custom_call", output_to_operand_aliasing={{0}: (5, {}), {1}: (6, {}), {2}: (7, {}), {3}: (8, {})} | custom-call | flops 2500 | bytes 250 | tf_op jit(solution)/shard_map/stage1/pallas_call | solution.py:327
  16.7 1.5 %collective-permute-done.7.refs_0_ = bf16[272,256]{1,0:T(8,128)(2,1)S(1)} collective-permute-done((bf16[272,256]{1,0:T(8,128)(2,1)S(1)}, bf16[272,256]{1,0:T(8,128)(2,1)S(1)}, u32[]{:S(2)}, u32[]{:S(2)}) %collective-permute-start.7) | collective-permute-done | bytes 139296 | tf_op jit(solution)/shard_map/ppermute | solution.py:270
  18.2 0.5 %collective-permute-start.11 = (bf16[272,256]{1,0:T(8,128)(2,1)S(1)}, bf16[272,256]{1,0:T(8,128)(2,1)S(1)}, u32[]{:S(2)}, u32[]{:S(2)}) collective-permute-start(bf16[272,256]{1,0:T(8,128)(2,1)S(1)} %collective-permute-done.7.refs_0_), channel_id=1, source_target_pairs={{0,1},{1,0},{2,3},{3,2},{4,5},{5,4},{6,7},{7,6},{8,9},{9,8},{10,11... | collective-permute-start | bytes 417800 | tf_op jit(solution)/shard_map/ppermute | solution.py:270
  18.7 1.2 %collective-permute-start.4 = (bf16[272,256]{1,0:T(8,128)(2,1)S(1)}, bf16[272,256]{1,0:T(8,128)(2,1)S(1)}, u32[]{:S(2)}, u32[]{:S(2)}) collective-permute-start(bf16[272,256]{1,0:T(8,128)(2,1)S(1)} %collective-permute-done.2.refs_0_), channel_id=1, source_target_pairs={{0,6},{1,7},{2,4},{3,5},{4,2},{5,3},{6,0},{7,1},{8,14},{9,15},{10,... | collective-permute-start | bytes 417800 | tf_op jit(solution)/shard_map/ppermute | solution.py:270
  20.0 1.1 %stage2.1 = (bf16[4096,256]{1,0:T(8,128)(2,1)S(1)}, f32[32,2304]{1,0:T(8,128)S(1)}, bf16[4096,2304]{1,0:T(8,128)(2,1)S(1)}, f32[72,2048]{1,0:T(8,128)S(1)}, f32[8,128]{1,0:T(8,128)S(1)}) custom-call(s32[1]{0:T(128)} %bitcast.1.me_ref, ...), custom_call_target="tpu_custom_call", output_to_operand_aliasing={{0}: (6, {}), {1}: (7, {}), {2}: (8, {}), {3}: (9, {})} | custom-call | flops 2500 | bytes 250 | tf_op jit(solution)/shard_map/stage2/pallas_call | solution.py:327
  21.2 0.5 %collective-permute-start.14 = (bf16[272,256]{1,0:T(8,128)(2,1)S(1)}, bf16[272,256]{1,0:T(8,128)(2,1)S(1)}, u32[]{:S(2)}, u32[]{:S(2)}) collective-permute-start(bf16[272,256]{1,0:T(8,128)(2,1)S(1)} %collective-permute-done.5.refs_1_), channel_id=1, source_target_pairs={{0,1},{1,0},{2,3},{3,2},{4,5},{5,4},{6,7},{7,6},{8,9},{9,8},{10,11... | collective-permute-start | bytes 417800 | tf_op jit(solution)/shard_map/ppermute | solution.py:270
  21.7 2.3 %stage3.1 = (bf16[4096,256]{1,0:T(8,128)(2,1)S(1)}, f32[32,2304]{1,0:T(8,128)S(1)}, bf16[4096,2304]{1,0:T(8,128)(2,1)S(1)}, f32[72,2048]{1,0:T(8,128)S(1)}, f32[8,128]{1,0:T(8,128)S(1)}) custom-call(s32[1]{0:T(128)} %bitcast.1.me_ref, ...), custom_call_target="tpu_custom_call", output_to_operand_aliasing={{0}: (7, {}), {1}: (8, {}), {2}: (9, {}), {3}: (10, {})} | custom-call | flops 2500 | bytes 250 | tf_op jit(solution)/shard_map/stage3/pallas_call | solution.py:327
  24.1 1.2 %collective-permute-done.4.refs_0_ = bf16[272,256]{1,0:T(8,128)(2,1)S(1)} collective-permute-done((bf16[272,256]{1,0:T(8,128)(2,1)S(1)}, bf16[272,256]{1,0:T(8,128)(2,1)S(1)}, u32[]{:S(2)}, u32[]{:S(2)}) %collective-permute-start.4) | collective-permute-done | bytes 139296 | tf_op jit(solution)/shard_map/ppermute | solution.py:270
  25.3 2.5 %stage4.1 = (bf16[4096,256]{1,0:T(8,128)(2,1)S(1)}, f32[32,2304]{1,0:T(8,128)S(1)}, bf16[4096,2304]{1,0:T(8,128)(2,1)S(1)}, f32[72,2048]{1,0:T(8,128)S(1)}) custom-call(s32[1]{0:T(128)} %bitcast.1.me_ref, bf16[128,4096]{1,0:T(8,128)(2,1)S(1)} %get-tuple-element.54.rt_ref, ...), custom_call_target="tpu_custom_call", output_to_operand_aliasing={{0}: (6, {}), {1}: (7, {}), {2}: (8, {}), {3}: (9, {})} | custom-call | flops 2500 | bytes 250 | tf_op jit(solution)/shard_map/stage4/pallas_call | solution.py:327
  27.8 1.0 %stage5.1 = (bf16[4096,256]{1,0:T(8,128)(2,1)S(1)}, f32[32,2304]{1,0:T(8,128)S(1)}, bf16[4096,2304]{1,0:T(8,128)(2,1)S(1)}, f32[72,2048]{1,0:T(8,128)S(1)}, bf16...) custom-call(s32[1]{0:T(128)} %bitcast.1.me_ref, ...), custom_call_target="tpu_custom_call", output_to_operand_aliasing={{0}: (4, {}), {1}: (5, {}), {2}: (6, {}), {3}: (7, {})} | custom-call | flops 2500 | bytes 250 | tf_op jit(solution)/shard_map/stage5/pallas_call | solution.py:327
  28.8 0.6 %collective-permute-start.15 = (bf16[64,2048]{1,0:T(8,128)(2,1)S(1)}, bf16[64,2048]{1,0:T(8,128)(2,1)S(1)}, u32[]{:S(2)}, u32[]{:S(2)}) collective-permute-start(bf16[64,2048]{1,0:T(8,128)(2,1)S(1)} %get-tuple-element.94.mine_ref), channel_id=1, source_target_pairs={{0,1},{1,0},{2,3},{3,2},{4,5},{5,4},{6,7},{7,6},{8,9},{9,8},{10,11... | collective-permute-start | bytes 786440 | tf_op jit(solution)/shard_map/ppermute | solution.py:270
  29.3 1.3 %half.1.half_ref = f32[64,2048]{1,0:T(8,128)S(1)} custom-call(bf16[4096,2304]{1,0:T(8,128)(2,1)S(1)} %get-tuple-element.93.kt_ref, bf16[64,2048]{1,0:T(8,128)(2,1)S(1)} %get-tuple-element.94.mine_ref), custom_call_target="tpu_custom_call" | custom-call | flops 1500 | bytes 150 | tf_op jit(solution)/shard_map/half/pallas_call | solution.py:385
  30.6 1.6 %step.1 = (f32[64,256]{1,0:T(8,128)S(1)}, f32[64,256]{1,0:T(8,128)S(1)}) custom-call(bf16[128,4096]{1,0:T(8,128)(2,1)S(1)} %get-tuple-element.54.rt_ref, bf16[4096,2304]{1,0:T(8,128)(2,1)S(1)} %get-tuple-element.93.kt_ref, f32[8,2048]{1,0:T(8,128)S(1)} %get-tuple-element.92.gain_ref, f32[64,2048]{1,0:T(8,128)S(1)} %half.1.half_ref, ...), custom_call_target="tpu_custom_call" | custom-call | flops 1500 | bytes 150 | tf_op jit(solution)/shard_map/step/pallas_call | solution.py:394
  32.5 1.0 %collective-permute-done.16.other_ref = f32[64,256]{1,0:T(8,128)S(1)} collective-permute-done((f32[64,256]{1,0:T(8,128)S(1)}, f32[64,256]{1,0:T(8,128)S(1)}, u32[]{:S(2)}, u32[]{:S(2)}) %collective-permute-start.16) | collective-permute-done | bytes 65568 | tf_op jit(solution)/shard_map/ppermute | solution.py:270
  33.5 0.6 %last.1 = f32[64,256]{1,0:T(8,128)} custom-call(bf16[128,4096]{1,0:T(8,128)(2,1)S(1)} %get-tuple-element.54.rt_ref, f32[8,2048]{1,0:T(8,128)S(1)} %get-tuple-element.92.gain_ref, f32[64,256]{1,0:T(8,128)S(1)} %get-tuple-element.95.mine_ref, f32[64,256]{1,0:T(8,128)S(1)} %collective-permute-done.16.other_ref), custom_call_target="tpu_custom_call" | custom-call | flops 500 | bytes 50 | tf_op jit(solution)/shard_map/last/pallas_call | solution.py:404
  (21 shorter events, 1.1 us)
Async XLA Ops:
  1.7 9.9 %collective-permute-start = (bf16[272,256]{1,0:T(8,128)(2,1)S(1)}, bf16[272,256]{1,0:T(8,128)(2,1)S(1)}, u32[]{:S(2)}, u32[]{:S(2)}) collective-permute-start(bf16[272,256]{1,0:T(8,128)(2,1)S(1)} %get-tuple-element.51.refs_0_), channel_id=1, source_target_pairs={{0,4},{1,5},{2,6},{3,7},{4,0},{5,1},{6,2},{7,3},{8,12},{9,13},{10,... | collective-permute-start | bytes 417800 | tf_op jit(solution)/shard_map/ppermute | solution.py:270
  4.8 6.8 %collective-permute-start.1 = (bf16[272,256]{1,0:T(8,128)(2,1)S(1)}, bf16[272,256]{1,0:T(8,128)(2,1)S(1)}, u32[]{:S(2)}, u32[]{:S(2)}) collective-permute-start(bf16[272,256]{1,0:T(8,128)(2,1)S(1)} %get-tuple-element.51.refs_0_), channel_id=1, source_target_pairs={{0,2},{1,3},{2,0},{3,1},{4,6},{5,7},{6,4},{7,5},{8,10},{9,11},{10,... | collective-permute-start | bytes 417800 | tf_op jit(solution)/shard_map/ppermute | solution.py:270
  6.3 8.7 %collective-permute-start.2 = (bf16[272,256]{1,0:T(8,128)(2,1)S(1)}, bf16[272,256]{1,0:T(8,128)(2,1)S(1)}, u32[]{:S(2)}, u32[]{:S(2)}) collective-permute-start(bf16[272,256]{1,0:T(8,128)(2,1)S(1)} %get-tuple-element.51.refs_0_), channel_id=1, source_target_pairs={{0,8},{1,9},{2,10},{3,11},{4,12},{5,13},{6,14},{7,15},{8,0},{9,1},... | collective-permute-start | bytes 417800 | tf_op jit(solution)/shard_map/ppermute | solution.py:270
  8.9 6.1 %collective-permute-start.3 = (bf16[272,256]{1,0:T(8,128)(2,1)S(1)}, bf16[272,256]{1,0:T(8,128)(2,1)S(1)}, u32[]{:S(2)}, u32[]{:S(2)}) collective-permute-start(bf16[272,256]{1,0:T(8,128)(2,1)S(1)} %get-tuple-element.51.refs_0_), channel_id=1, source_target_pairs={{0,1},{1,0},{2,3},{3,2},{4,5},{5,4},{6,7},{7,6},{8,9},{9,8},{10,11... | collective-permute-start | bytes 417800 | tf_op jit(solution)/shard_map/ppermute | solution.py:270
  11.7 6.5 %collective-permute-start.7 = (bf16[272,256]{1,0:T(8,128)(2,1)S(1)}, bf16[272,256]{1,0:T(8,128)(2,1)S(1)}, u32[]{:S(2)}, u32[]{:S(2)}) collective-permute-start(bf16[272,256]{1,0:T(8,128)(2,1)S(1)} %collective-permute-done.refs_1_), channel_id=1, source_target_pairs={{0,2},{1,3},{2,0},{3,1},{4,6},{5,7},{6,4},{7,5},{8,10},{9,11},{10,... | collective-permute-start | bytes 417800 | tf_op jit(solution)/shard_map/ppermute | solution.py:270
  12.3 5.9 %collective-permute-start.8 = (bf16[272,256]{1,0:T(8,128)(2,1)S(1)}, bf16[272,256]{1,0:T(8,128)(2,1)S(1)}, u32[]{:S(2)}, u32[]{:S(2)}) collective-permute-start(bf16[272,256]{1,0:T(8,128)(2,1)S(1)} %collective-permute-done.refs_1_), channel_id=1, source_target_pairs={{0,1},{1,0},{2,3},{3,2},{4,5},{5,4},{6,7},{7,6},{8,9},{9,8},{10,11... | collective-permute-start | bytes 417800 | tf_op jit(solution)/shard_map/ppermute | solution.py:270
  12.5 6.2 %collective-permute-start.9 = (bf16[272,256]{1,0:T(8,128)(2,1)S(1)}, bf16[272,256]{1,0:T(8,128)(2,1)S(1)}, u32[]{:S(2)}, u32[]{:S(2)}) collective-permute-start(bf16[272,256]{1,0:T(8,128)(2,1)S(1)} %collective-permute-done.1.refs_2_), channel_id=1, source_target_pairs={{0,1},{1,0},{2,3},{3,2},{4,5},{5,4},{6,7},{7,6},{8,9},{9,8},{10,11... | collective-permute-start | bytes 417800 | tf_op jit(solution)/shard_map/ppermute | solution.py:270
  15.1 6.1 %collective-permute-start.5 = (bf16[272,256]{1,0:T(8,128)(2,1)S(1)}, bf16[272,256]{1,0:T(8,128)(2,1)S(1)}, u32[]{:S(2)}, u32[]{:S(2)}) collective-permute-start(bf16[272,256]{1,0:T(8,128)(2,1)S(1)} %collective-permute-done.2.refs_0_), channel_id=1, source_target_pairs={{0,2},{1,3},{2,0},{3,1},{4,6},{5,7},{6,4},{7,5},{8,10},{9,11},{10,... | collective-permute-start | bytes 417800 | tf_op jit(solution)/shard_map/ppermute | solution.py:270
  15.7 5.5 %collective-permute-start.6 = (bf16[272,256]{1,0:T(8,128)(2,1)S(1)}, bf16[272,256]{1,0:T(8,128)(2,1)S(1)}, u32[]{:S(2)}, u32[]{:S(2)}) collective-permute-start(bf16[272,256]{1,0:T(8,128)(2,1)S(1)} %collective-permute-done.2.refs_0_), channel_id=1, source_target_pairs={{0,4},{1,5},{2,6},{3,7},{4,0},{5,1},{6,2},{7,3},{8,12},{9,13},{10,... | collective-permute-start | bytes 417800 | tf_op jit(solution)/shard_map/ppermute | solution.py:270
  18.2 3.5 %collective-permute-start.10 = (bf16[272,256]{1,0:T(8,128)(2,1)S(1)}, bf16[272,256]{1,0:T(8,128)(2,1)S(1)}, u32[]{:S(2)}, u32[]{:S(2)}) collective-permute-start(bf16[272,256]{1,0:T(8,128)(2,1)S(1)} %collective-permute-done.2.refs_0_), channel_id=1, source_target_pairs={{0,1},{1,0},{2,3},{3,2},{4,5},{5,4},{6,7},{7,6},{8,9},{9,8},{10,11... | collective-permute-start | bytes 417800 | tf_op jit(solution)/shard_map/ppermute | solution.py:270
  18.2 3.5 %collective-permute-start.11 = (bf16[272,256]{1,0:T(8,128)(2,1)S(1)}, bf16[272,256]{1,0:T(8,128)(2,1)S(1)}, u32[]{:S(2)}, u32[]{:S(2)}) collective-permute-start(bf16[272,256]{1,0:T(8,128)(2,1)S(1)} %collective-permute-done.7.refs_0_), channel_id=1, source_target_pairs={{0,1},{1,0},{2,3},{3,2},{4,5},{5,4},{6,7},{7,6},{8,9},{9,8},{10,11... | collective-permute-start | bytes 417800 | tf_op jit(solution)/shard_map/ppermute | solution.py:270
  18.7 6.5 %collective-permute-start.4 = (bf16[272,256]{1,0:T(8,128)(2,1)S(1)}, bf16[272,256]{1,0:T(8,128)(2,1)S(1)}, u32[]{:S(2)}, u32[]{:S(2)}) collective-permute-start(bf16[272,256]{1,0:T(8,128)(2,1)S(1)} %collective-permute-done.2.refs_0_), channel_id=1, source_target_pairs={{0,6},{1,7},{2,4},{3,5},{4,2},{5,3},{6,0},{7,1},{8,14},{9,15},{10,... | collective-permute-start | bytes 417800 | tf_op jit(solution)/shard_map/ppermute | solution.py:270
  21.2 4.1 %collective-permute-start.13 = (bf16[272,256]{1,0:T(8,128)(2,1)S(1)}, bf16[272,256]{1,0:T(8,128)(2,1)S(1)}, u32[]{:S(2)}, u32[]{:S(2)}) collective-permute-start(bf16[272,256]{1,0:T(8,128)(2,1)S(1)} %collective-permute-done.6.refs_0_), channel_id=1, source_target_pairs={{0,1},{1,0},{2,3},{3,2},{4,5},{5,4},{6,7},{7,6},{8,9},{9,8},{10,11... | collective-permute-start | bytes 417800 | tf_op jit(solution)/shard_map/ppermute | solution.py:270
  21.2 4.1 %collective-permute-start.14 = (bf16[272,256]{1,0:T(8,128)(2,1)S(1)}, bf16[272,256]{1,0:T(8,128)(2,1)S(1)}, u32[]{:S(2)}, u32[]{:S(2)}) collective-permute-start(bf16[272,256]{1,0:T(8,128)(2,1)S(1)} %collective-permute-done.5.refs_1_), channel_id=1, source_target_pairs={{0,1},{1,0},{2,3},{3,2},{4,5},{5,4},{6,7},{7,6},{8,9},{9,8},{10,11... | collective-permute-start | bytes 417800 | tf_op jit(solution)/shard_map/ppermute | solution.py:270
  25.3 2.5 %collective-permute-start.12 = (bf16[272,256]{1,0:T(8,128)(2,1)S(1)}, bf16[272,256]{1,0:T(8,128)(2,1)S(1)}, u32[]{:S(2)}, u32[]{:S(2)}) collective-permute-start(bf16[272,256]{1,0:T(8,128)(2,1)S(1)} %collective-permute-done.4.refs_0_), channel_id=1, source_target_pairs={{0,1},{1,0},{2,3},{3,2},{4,5},{5,4},{6,7},{7,6},{8,9},{9,8},{10,11... | collective-permute-start | bytes 417800 | tf_op jit(solution)/shard_map/ppermute | solution.py:270
  28.8 1.8 %collective-permute-start.15 = (bf16[64,2048]{1,0:T(8,128)(2,1)S(1)}, bf16[64,2048]{1,0:T(8,128)(2,1)S(1)}, u32[]{:S(2)}, u32[]{:S(2)}) collective-permute-start(bf16[64,2048]{1,0:T(8,128)(2,1)S(1)} %get-tuple-element.94.mine_ref), channel_id=1, source_target_pairs={{0,1},{1,0},{2,3},{3,2},{4,5},{5,4},{6,7},{7,6},{8,9},{9,8},{10,11... | collective-permute-start | bytes 786440 | tf_op jit(solution)/shard_map/ppermute | solution.py:270
  32.2 1.3 %collective-permute-start.16 = (f32[64,256]{1,0:T(8,128)S(1)}, f32[64,256]{1,0:T(8,128)S(1)}, u32[]{:S(2)}, u32[]{:S(2)}) collective-permute-start(f32[64,256]{1,0:T(8,128)S(1)} %get-tuple-element.96), channel_id=1, source_target_pairs={{0,1},{1,0},{2,3},{3,2},{4,5},{5,4},{6,7},{7,6},{8,9},{9,8},{10,11... | collective-permute-start | bytes 196616 | tf_op jit(solution)/shard_map/ppermute | solution.py:270

commit v6 on v5

--- a/solution.py
+++ b/solution.py
@@ -113,8 +113,11 @@
     seeds_copy.wait()
 
 
-def restart_kernel(me_ref, seeds_ref, out_ref, pick_ref, counts):
+def restart_kernel(first, me_ref, seeds_ref, *refs):
+    out_ref, counts = refs[-3 if first else -2], refs[-1]
     seed_cols = seeds_ref.shape[0]
+    low_col = 0 if first else seed_cols // 2
+    span = seed_cols // 2
     tiles = counts.shape[1]
     me = me_ref[0]
     spot = lax.broadcasted_iota(jnp.int32, (tiles, TILE), 0)
@@ -123,22 +126,26 @@
         offset = offset + jnp.where((spot // 2) % 8 == place, 4 * z + 2 * x, 0)
     tile_ids = (me ^ offset) * 2 + spot % 2
     lows = lax.broadcasted_iota(jnp.int32, (TILE, TILE), 0)
-    core, x_pos = me % 2, (me // 2) % 2
-    pick_row = lax.broadcasted_iota(jnp.int32, pick_ref.shape, 0)
-    pick_col = lax.broadcasted_iota(jnp.int32, pick_ref.shape, 1) // TILE
-    sib = pick_col // 4
-    wanted = 4 * (x_pos ^ ((pick_col // 2) % 2)) + 2 * (core ^ sib) + pick_col % 2
-    pick_ref[...] = (pick_row == wanted).astype(F32).astype(BF16)
-
-    @pl.loop(0, seed_cols, unroll=16)
+    if first:
+        pick_ref = refs[-2]
+        core, x_pos = me % 2, (me // 2) % 2
+        pick_row = lax.broadcasted_iota(jnp.int32, pick_ref.shape, 0)
+        pick_col = lax.broadcasted_iota(jnp.int32, pick_ref.shape, 1) // TILE
+        sib = pick_col // 4
+        wanted = 4 * (x_pos ^ ((pick_col // 2) % 2)) + 2 * (core ^ sib) + pick_col % 2
+        pick_ref[...] = (pick_row == wanted).astype(F32).astype(BF16)
+
+    @pl.loop(0, span, unroll=16)
     def _(k):
-        row = seeds_ref[pl.ds(k, 1), :]
+        row = seeds_ref[pl.ds(low_col + k, 1), :]
         high_hot = (tile_ids == row // TILE).astype(F32).astype(BF16)
         low_hot = (lows == row % TILE).astype(F32).astype(BF16)
         counts[k] = dot_nt(high_hot, low_hot) * float(SEED_SHARE)
 
     for t in range(tiles):
-        out_ref[0:seed_cols, t * TILE : (t + 1) * TILE] = counts[:, t, :].astype(BF16)
+        out_ref[low_col : low_col + span, t * TILE : (t + 1) * TILE] = counts[:, t, :].astype(BF16)
+    if not first:
+        return
     rest = out_ref.shape[0] - seed_cols
     first = lax.broadcasted_iota(jnp.int32, (rest, out_ref.shape[1]), 0) == 0
     out_ref[seed_cols:, :] = first.astype(F32).astype(BF16)
@@ -341,22 +348,34 @@
     x0 = swap(block, across)
     b00 = swap(block, sibling)
     rt, pick = pl.pallas_call(
-        restart_kernel,
+        functools.partial(restart_kernel, True),
         in_specs=[SCALARS, WHOLE],
         out_specs=[WHOLE] * 2,
-        out_shape=[
-            jax.ShapeDtypeStruct((2 * seed_cols, sessions), BF16),
-            jax.ShapeDtypeStruct((TILE, 6 * TILE), BF16),
-        ],
-        scratch_shapes=[pltpu.VMEM((seed_cols, sessions // TILE, TILE), F32)],
+        out_shape=[pltpu.VMEM((2 * seed_cols, sessions), BF16), jax.ShapeDtypeStruct((TILE, 6 * TILE), BF16)],
+        scratch_shapes=[pltpu.VMEM((seed_cols // 2, sessions // TILE, TILE), F32)],
         compiler_params=params(),
-        cost_estimate=work(2.6),
+        cost_estimate=work(1.3),
         name="restart",
     )(me, seeds)
+
+    def more_restart(rt):
+        return pl.pallas_call(
+            functools.partial(restart_kernel, False),
+            in_specs=[SCALARS, WHOLE, WHOLE],
+            out_specs=WHOLE,
+            out_shape=pltpu.VMEM((2 * seed_cols, sessions), BF16),
+            input_output_aliases={2: 0},
+            scratch_shapes=[pltpu.VMEM((seed_cols // 2, sessions // TILE, TILE), F32)],
+            compiler_params=params(),
+            cost_estimate=work(1.3),
+            name="restart2",
+        )(me, seeds, rt)
+
     z1, x0, rt = lax.optimization_barrier((z1, x0, rt))
     x1 = swap(z1, across)
     b10 = swap(z1, sibling)
     b01 = swap(x0, sibling)
+    rt = more_restart(rt)
     state, (done,) = run_stage(0, rt, [block, z1, x0], [], mark)
     z2, b00, done = lax.optimization_barrier((z2, b00, done))
     z3 = swap(z2, near)

time: 34.3 us -> 33.6 us (0.980)
  waiting for transfers between devices: 5.34 us -> 2.02 us
  starting transfers between devices: 12.3 us -> 14.8 us
    ppermute x17, waiting for transfers between devices: 5.34 us -> 2.02 us  [swap(): return lax.ppermute(array, ('row', 'col'), pairs)]
    ppermute x17, starting transfers between devices: 12.3 us -> 14.8 us  [swap(): return lax.ppermute(array, ('row', 'col'), pairs)]
    pallas_call x1 -> x2, Pallas kernels: 2.74 us -> 2.77 us  [the longest x1 1.42 us: chip_local(): pl.pallas_call(functools.partial(restart_kernel, True), in_specs=[SCALARS...]
  transfers between devices with their start and end apart: 17 -> 17, of which waited for: 4 -> 3; matrix products, arithmetic and copies ran while one was open for 0% -> 0% of each run, Pallas kernels for 34% -> 34%
where the time goes in v6:
time: 33.6 us; the launch traced here: 33.4 us
  Pallas kernels  15.8 us (47%)
  starting transfers between devices  14.8 us (44%)
  waiting for transfers between devices  2.02 us (6%)
  between operations  0.83 us (2%)
    ppermute x17, starting transfers between devices, swap(): return lax.ppermute(array, ('row', 'col'), pairs)  14.8 us
    pallas_call x6, Pallas kernels, run_stage(): pl.pallas_call(functools.partial(stage_kernel, stage), in_specs=[SCALARS]...  8.43 us
    ppermute x17, waiting for transfers between devices, swap(): return lax.ppermute(array, ('row', 'col'), pairs)  2.02 us
    pallas_call x1, Pallas kernels, chip_local(): pl.pallas_call(step_kernel, in_specs=[WHOLE] * 5, out_specs=[WHOLE] * 2,...  1.59 us
    pallas_call x1, Pallas kernels, chip_local(): pl.pallas_call(functools.partial(restart_kernel, True), in_specs=[SCALARS...  1.42 us
    pallas_call x1, Pallas kernels, more_restart(): pl.pallas_call(functools.partial(restart_kernel, False), in_specs=[SCALAR...  1.34 us
    pallas_call x1, Pallas kernels, chip_local(): pl.pallas_call(half_kernel, in_specs=[WHOLE] * 2, out_specs=WHOLE, out_sh...  1.26 us
    pallas_call x1, Pallas kernels, chip_local(): pl.pallas_call(payload_kernel, in_specs=[SCALARS] + [REMAIN] * 3, out_spe...  1.09 us
  transfers between devices with their start and end apart: 17, of which 3 were waited for; matrix products, arithmetic and copies ran while one was open for 0% of the time, Pallas kernels for 34%

profile of v6, /device:TPU:0, one launch (start us, length us, event | category | flops | bytes accessed | tf_op | source)
XLA Modules:
  0.0 33.4 jit_solution(8466009708119203899)
XLA Ops:
  0.7 1.1 %payload.1 = (bf16[272,256]{1,0:T(8,128)(2,1)S(1)}, s32[64,128]{1,0:T(8,128)S(1)}) custom-call(s32[1,1]{1,0:T(1,128)S(6)} %copy.47.count_ref, bf16[256,256]{1,0:T(8,128)(2,1)} %emb_in.1, s32[2,48]{1,0:T(2,128)} %bitcast.3, s32[64,128]{1,0:T(8,128)} %seeds_in.1), custom_call_target="tpu_custom_call" | custom-call | tf_op jit(solution)/shard_map/payload/pallas_call | solution.py:308
  1.7 3.1 %collective-permute-start = (bf16[272,256]{1,0:T(8,128)(2,1)S(1)}, bf16[272,256]{1,0:T(8,128)(2,1)S(1)}, u32[]{:S(2)}, u32[]{:S(2)}) collective-permute-start(bf16[272,256]{1,0:T(8,128)(2,1)S(1)} %get-tuple-element.52.refs_0_), channel_id=1, source_target_pairs={{0,4},{1,5},{2,6},{3,7},{4,0},{5,1},{6,2},{7,3},{8,12},{9,13},{10,... | collective-permute-start | bytes 417800 | tf_op jit(solution)/shard_map/ppermute | solution.py:277
  4.8 1.5 %collective-permute-start.1 = (bf16[272,256]{1,0:T(8,128)(2,1)S(1)}, bf16[272,256]{1,0:T(8,128)(2,1)S(1)}, u32[]{:S(2)}, u32[]{:S(2)}) collective-permute-start(bf16[272,256]{1,0:T(8,128)(2,1)S(1)} %get-tuple-element.52.refs_0_), channel_id=1, source_target_pairs={{0,2},{1,3},{2,0},{3,1},{4,6},{5,7},{6,4},{7,5},{8,10},{9,11},{10,... | collective-permute-start | bytes 417800 | tf_op jit(solution)/shard_map/ppermute | solution.py:277
  6.3 2.6 %collective-permute-start.2 = (bf16[272,256]{1,0:T(8,128)(2,1)S(1)}, bf16[272,256]{1,0:T(8,128)(2,1)S(1)}, u32[]{:S(2)}, u32[]{:S(2)}) collective-permute-start(bf16[272,256]{1,0:T(8,128)(2,1)S(1)} %get-tuple-element.52.refs_0_), channel_id=1, source_target_pairs={{0,8},{1,9},{2,10},{3,11},{4,12},{5,13},{6,14},{7,15},{8,0},{9,1},... | collective-permute-start | bytes 417800 | tf_op jit(solution)/shard_map/ppermute | solution.py:277
  8.9 1.4 %restart.1 = (bf16[128,4096]{1,0:T(8,128)(2,1)S(1)}, bf16[128,768]{1,0:T(8,128)(2,1)S(1)}) custom-call(s32[1]{0:T(128)} %bitcast.me_ref, s32[64,128]{1,0:T(8,128)S(1)} %get-tuple-element.51.seeds_ref), custom_call_target="tpu_custom_call" | custom-call | flops 1300 | bytes 130 | tf_op jit(solution)/shard_map/restart/pallas_call | solution.py:350
  10.4 1.6 %collective-permute-start.7 = (bf16[272,256]{1,0:T(8,128)(2,1)S(1)}, bf16[272,256]{1,0:T(8,128)(2,1)S(1)}, u32[]{:S(2)}, u32[]{:S(2)}) collective-permute-start(bf16[272,256]{1,0:T(8,128)(2,1)S(1)} %collective-permute-done.refs_1_), channel_id=1, source_target_pairs={{0,2},{1,3},{2,0},{3,1},{4,6},{5,7},{6,4},{7,5},{8,10},{9,11},{10,... | collective-permute-start | bytes 417800 | tf_op jit(solution)/shard_map/ppermute | solution.py:277
  12.0 0.5 %collective-permute-start.9 = (bf16[272,256]{1,0:T(8,128)(2,1)S(1)}, bf16[272,256]{1,0:T(8,128)(2,1)S(1)}, u32[]{:S(2)}, u32[]{:S(2)}) collective-permute-start(bf16[272,256]{1,0:T(8,128)(2,1)S(1)} %collective-permute-done.1.refs_2_), channel_id=1, source_target_pairs={{0,1},{1,0},{2,3},{3,2},{4,5},{5,4},{6,7},{7,6},{8,9},{9,8},{10,11... | collective-permute-start | bytes 417800 | tf_op jit(solution)/shard_map/ppermute | solution.py:277
  12.5 1.3 %restart2.1.rt_ref = bf16[128,4096]{1,0:T(8,128)(2,1)S(1)} custom-call(s32[1]{0:T(128)} %bitcast.me_ref, s32[64,128]{1,0:T(8,128)S(1)} %get-tuple-element.51.seeds_ref, bf16[128,4096]{1,0:T(8,128)(2,1)S(1)} %get-tuple-element.54.refs_0_), custom_call_target="tpu_custom_call", output_to_operand_aliasing={{}: (2, {})} | custom-call | flops 1300 | bytes 130 | tf_op jit(solution)/shard_map/restart2/pallas_call | solution.py:362
  13.9 0.7 %stage0.1 = (bf16[4096,256]{1,0:T(8,128)(2,1)S(1)}, f32[32,2304]{1,0:T(8,128)S(1)}, bf16[4096,2304]{1,0:T(8,128)(2,1)S(1)}, f32[72,2048]{1,0:T(8,128)S(1)}, f32[8,128]{1,0:T(8,128)S(1)}) custom-call(s32[1]{0:T(128)} %bitcast.me_ref, bf16[128,4096]{1,0:T(8,128)(2,1)S(1)} %restart2.1.rt_ref, bf16[128,768]{1,0:T(8,128)(2,1)S(1)} %get-tuple-element.55.pick_ref, ...), custom_call_target="tpu_custom_call" | custom-call | flops 2500 | bytes 250 | tf_op jit(solution)/shard_map/stage0/pallas_call | solution.py:334
  14.5 0.5 %collective-permute-done.2.refs_0_ = bf16[272,256]{1,0:T(8,128)(2,1)S(1)} collective-permute-done((bf16[272,256]{1,0:T(8,128)(2,1)S(1)}, bf16[272,256]{1,0:T(8,128)(2,1)S(1)}, u32[]{:S(2)}, u32[]{:S(2)}) %collective-permute-start.2) | collective-permute-done | bytes 139296 | tf_op jit(solution)/shard_map/ppermute | solution.py:277
  15.1 0.6 %collective-permute-start.5 = (bf16[272,256]{1,0:T(8,128)(2,1)S(1)}, bf16[272,256]{1,0:T(8,128)(2,1)S(1)}, u32[]{:S(2)}, u32[]{:S(2)}) collective-permute-start(bf16[272,256]{1,0:T(8,128)(2,1)S(1)} %collective-permute-done.2.refs_0_), channel_id=1, source_target_pairs={{0,2},{1,3},{2,0},{3,1},{4,6},{5,7},{6,4},{7,5},{8,10},{9,11},{10,... | collective-permute-start | bytes 417800 | tf_op jit(solution)/shard_map/ppermute | solution.py:277
  15.8 0.8 %stage1.1 = (bf16[4096,256]{1,0:T(8,128)(2,1)S(1)}, f32[32,2304]{1,0:T(8,128)S(1)}, bf16[4096,2304]{1,0:T(8,128)(2,1)S(1)}, f32[72,2048]{1,0:T(8,128)S(1)}, f32[8,128]{1,0:T(8,128)S(1)}) custom-call(s32[1]{0:T(128)} %bitcast.me_ref, bf16[128,4096]{1,0:T(8,128)(2,1)S(1)} %restart2.1.rt_ref, ...), custom_call_target="tpu_custom_call", output_to_operand_aliasing={{0}: (5, {}), {1}: (6, {}), {2}: (7, {}), {3}: (8, {})} | custom-call | flops 2500 | bytes 250 | tf_op jit(solution)/shard_map/stage1/pallas_call | solution.py:334
  16.8 0.5 %collective-permute-start.11 = (bf16[272,256]{1,0:T(8,128)(2,1)S(1)}, bf16[272,256]{1,0:T(8,128)(2,1)S(1)}, u32[]{:S(2)}, u32[]{:S(2)}) collective-permute-start(bf16[272,256]{1,0:T(8,128)(2,1)S(1)} %collective-permute-done.7.refs_0_), channel_id=1, source_target_pairs={{0,1},{1,0},{2,3},{3,2},{4,5},{5,4},{6,7},{7,6},{8,9},{9,8},{10,11... | collective-permute-start | bytes 417800 | tf_op jit(solution)/shard_map/ppermute | solution.py:277
  17.3 2.7 %collective-permute-start.4 = (bf16[272,256]{1,0:T(8,128)(2,1)S(1)}, bf16[272,256]{1,0:T(8,128)(2,1)S(1)}, u32[]{:S(2)}, u32[]{:S(2)}) collective-permute-start(bf16[272,256]{1,0:T(8,128)(2,1)S(1)} %collective-permute-done.2.refs_0_), channel_id=1, source_target_pairs={{0,6},{1,7},{2,4},{3,5},{4,2},{5,3},{6,0},{7,1},{8,14},{9,15},{10,... | collective-permute-start | bytes 417800 | tf_op jit(solution)/shard_map/ppermute | solution.py:277
  20.0 1.1 %stage2.1 = (bf16[4096,256]{1,0:T(8,128)(2,1)S(1)}, f32[32,2304]{1,0:T(8,128)S(1)}, bf16[4096,2304]{1,0:T(8,128)(2,1)S(1)}, f32[72,2048]{1,0:T(8,128)S(1)}, f32[8,128]{1,0:T(8,128)S(1)}) custom-call(s32[1]{0:T(128)} %bitcast.me_ref, bf16[128,4096]{1,0:T(8,128)(2,1)S(1)} %restart2.1.rt_ref, ...), custom_call_target="tpu_custom_call", output_to_operand_aliasing={{0}: (6, {}), {1}: (7, {}), {2}: (8, {}), {3}: (9, {})} | custom-call | flops 2500 | bytes 250 | tf_op jit(solution)/shard_map/stage2/pallas_call | solution.py:334
  21.2 0.5 %collective-permute-start.14 = (bf16[272,256]{1,0:T(8,128)(2,1)S(1)}, bf16[272,256]{1,0:T(8,128)(2,1)S(1)}, u32[]{:S(2)}, u32[]{:S(2)}) collective-permute-start(bf16[272,256]{1,0:T(8,128)(2,1)S(1)} %collective-permute-done.5.refs_1_), channel_id=1, source_target_pairs={{0,1},{1,0},{2,3},{3,2},{4,5},{5,4},{6,7},{7,6},{8,9},{9,8},{10,11... | collective-permute-start | bytes 417800 | tf_op jit(solution)/shard_map/ppermute | solution.py:277
  21.7 2.3 %stage3.1 = (bf16[4096,256]{1,0:T(8,128)(2,1)S(1)}, f32[32,2304]{1,0:T(8,128)S(1)}, bf16[4096,2304]{1,0:T(8,128)(2,1)S(1)}, f32[72,2048]{1,0:T(8,128)S(1)}, f32[8,128]{1,0:T(8,128)S(1)}) custom-call(s32[1]{0:T(128)} %bitcast.me_ref, bf16[128,4096]{1,0:T(8,128)(2,1)S(1)} %restart2.1.rt_ref, ...), custom_call_target="tpu_custom_call", output_to_operand_aliasing={{0}: (7, {}), {1}: (8, {}), {2}: (9, {}), {3}: (10, {})} | custom-call | flops 2500 | bytes 250 | tf_op jit(solution)/shard_map/stage3/pallas_call | solution.py:334
  24.6 2.5 %stage4.1 = (bf16[4096,256]{1,0:T(8,128)(2,1)S(1)}, f32[32,2304]{1,0:T(8,128)S(1)}, bf16[4096,2304]{1,0:T(8,128)(2,1)S(1)}, f32[72,2048]{1,0:T(8,128)S(1)}) custom-call(s32[1]{0:T(128)} %bitcast.me_ref, bf16[128,4096]{1,0:T(8,128)(2,1)S(1)} %restart2.1.rt_ref, ...), custom_call_target="tpu_custom_call", output_to_operand_aliasing={{0}: (6, {}), {1}: (7, {}), {2}: (8, {}), {3}: (9, {})} | custom-call | flops 2500 | bytes 250 | tf_op jit(solution)/shard_map/stage4/pallas_call | solution.py:334
  27.1 1.0 %stage5.1 = (bf16[4096,256]{1,0:T(8,128)(2,1)S(1)}, f32[32,2304]{1,0:T(8,128)S(1)}, bf16[4096,2304]{1,0:T(8,128)(2,1)S(1)}, f32[72,2048]{1,0:T(8,128)S(1)}, bf16...) custom-call(s32[1]{0:T(128)} %bitcast.me_ref, ...), custom_call_target="tpu_custom_call", output_to_operand_aliasing={{0}: (4, {}), {1}: (5, {}), {2}: (6, {}), {3}: (7, {})} | custom-call | flops 2500 | bytes 250 | tf_op jit(solution)/shard_map/stage5/pallas_call | solution.py:334
  28.0 0.6 %collective-permute-start.15 = (bf16[64,2048]{1,0:T(8,128)(2,1)S(1)}, bf16[64,2048]{1,0:T(8,128)(2,1)S(1)}, u32[]{:S(2)}, u32[]{:S(2)}) collective-permute-start(bf16[64,2048]{1,0:T(8,128)(2,1)S(1)} %get-tuple-element.94.mine_ref), channel_id=1, source_target_pairs={{0,1},{1,0},{2,3},{3,2},{4,5},{5,4},{6,7},{7,6},{8,9},{9,8},{10,11... | collective-permute-start | bytes 786440 | tf_op jit(solution)/shard_map/ppermute | solution.py:277
  28.6 1.3 %half.1.half_ref = f32[64,2048]{1,0:T(8,128)S(1)} custom-call(bf16[4096,2304]{1,0:T(8,128)(2,1)S(1)} %get-tuple-element.93.kt_ref, bf16[64,2048]{1,0:T(8,128)(2,1)S(1)} %get-tuple-element.94.mine_ref), custom_call_target="tpu_custom_call" | custom-call | flops 1500 | bytes 150 | tf_op jit(solution)/shard_map/half/pallas_call | solution.py:404
  29.9 1.6 %step.1 = (f32[64,256]{1,0:T(8,128)S(1)}, f32[64,256]{1,0:T(8,128)S(1)}) custom-call(bf16[128,4096]{1,0:T(8,128)(2,1)S(1)} %restart2.1.rt_ref, bf16[4096,2304]{1,0:T(8,128)(2,1)S(1)} %get-tuple-element.93.kt_ref, f32[8,2048]{1,0:T(8,128)S(1)} %get-tuple-element.92.gain_ref, f32[64,2048]{1,0:T(8,128)S(1)} %half.1.half_ref, ...), custom_call_target="tpu_custom_call" | custom-call | flops 1500 | bytes 150 | tf_op jit(solution)/shard_map/step/pallas_call | solution.py:413
  31.8 1.0 %collective-permute-done.16.other_ref = f32[64,256]{1,0:T(8,128)S(1)} collective-permute-done((f32[64,256]{1,0:T(8,128)S(1)}, f32[64,256]{1,0:T(8,128)S(1)}, u32[]{:S(2)}, u32[]{:S(2)}) %collective-permute-start.16) | collective-permute-done | bytes 65568 | tf_op jit(solution)/shard_map/ppermute | solution.py:277
  32.8 0.6 %last.1 = f32[64,256]{1,0:T(8,128)} custom-call(bf16[128,4096]{1,0:T(8,128)(2,1)S(1)} %restart2.1.rt_ref, f32[8,2048]{1,0:T(8,128)S(1)} %get-tuple-element.92.gain_ref, f32[64,256]{1,0:T(8,128)S(1)} %get-tuple-element.95.mine_ref, f32[64,256]{1,0:T(8,128)S(1)} %collective-permute-done.16.other_ref), custom_call_target="tpu_custom_call" | custom-call | flops 500 | bytes 50 | tf_op jit(solution)/shard_map/last/pallas_call | solution.py:423
  (22 shorter events, 1.2 us)
Async XLA Ops:
  1.7 8.6 %collective-permute-start = (bf16[272,256]{1,0:T(8,128)(2,1)S(1)}, bf16[272,256]{1,0:T(8,128)(2,1)S(1)}, u32[]{:S(2)}, u32[]{:S(2)}) collective-permute-start(bf16[272,256]{1,0:T(8,128)(2,1)S(1)} %get-tuple-element.52.refs_0_), channel_id=1, source_target_pairs={{0,4},{1,5},{2,6},{3,7},{4,0},{5,1},{6,2},{7,3},{8,12},{9,13},{10,... | collective-permute-start | bytes 417800 | tf_op jit(solution)/shard_map/ppermute | solution.py:277
  4.8 5.5 %collective-permute-start.1 = (bf16[272,256]{1,0:T(8,128)(2,1)S(1)}, bf16[272,256]{1,0:T(8,128)(2,1)S(1)}, u32[]{:S(2)}, u32[]{:S(2)}) collective-permute-start(bf16[272,256]{1,0:T(8,128)(2,1)S(1)} %get-tuple-element.52.refs_0_), channel_id=1, source_target_pairs={{0,2},{1,3},{2,0},{3,1},{4,6},{5,7},{6,4},{7,5},{8,10},{9,11},{10,... | collective-permute-start | bytes 417800 | tf_op jit(solution)/shard_map/ppermute | solution.py:277
  6.3 8.7 %collective-permute-start.2 = (bf16[272,256]{1,0:T(8,128)(2,1)S(1)}, bf16[272,256]{1,0:T(8,128)(2,1)S(1)}, u32[]{:S(2)}, u32[]{:S(2)}) collective-permute-start(bf16[272,256]{1,0:T(8,128)(2,1)S(1)} %get-tuple-element.52.refs_0_), channel_id=1, source_target_pairs={{0,8},{1,9},{2,10},{3,11},{4,12},{5,13},{6,14},{7,15},{8,0},{9,1},... | collective-permute-start | bytes 417800 | tf_op jit(solution)/shard_map/ppermute | solution.py:277
  8.9 6.1 %collective-permute-start.3 = (bf16[272,256]{1,0:T(8,128)(2,1)S(1)}, bf16[272,256]{1,0:T(8,128)(2,1)S(1)}, u32[]{:S(2)}, u32[]{:S(2)}) collective-permute-start(bf16[272,256]{1,0:T(8,128)(2,1)S(1)} %get-tuple-element.52.refs_0_), channel_id=1, source_target_pairs={{0,1},{1,0},{2,3},{3,2},{4,5},{5,4},{6,7},{7,6},{8,9},{9,8},{10,11... | collective-permute-start | bytes 417800 | tf_op jit(solution)/shard_map/ppermute | solution.py:277
  10.4 6.3 %collective-permute-start.7 = (bf16[272,256]{1,0:T(8,128)(2,1)S(1)}, bf16[272,256]{1,0:T(8,128)(2,1)S(1)}, u32[]{:S(2)}, u32[]{:S(2)}) collective-permute-start(bf16[272,256]{1,0:T(8,128)(2,1)S(1)} %collective-permute-done.refs_1_), channel_id=1, source_target_pairs={{0,2},{1,3},{2,0},{3,1},{4,6},{5,7},{6,4},{7,5},{8,10},{9,11},{10,... | collective-permute-start | bytes 417800 | tf_op jit(solution)/shard_map/ppermute | solution.py:277
  12.0 4.8 %collective-permute-start.8 = (bf16[272,256]{1,0:T(8,128)(2,1)S(1)}, bf16[272,256]{1,0:T(8,128)(2,1)S(1)}, u32[]{:S(2)}, u32[]{:S(2)}) collective-permute-start(bf16[272,256]{1,0:T(8,128)(2,1)S(1)} %collective-permute-done.refs_1_), channel_id=1, source_target_pairs={{0,1},{1,0},{2,3},{3,2},{4,5},{5,4},{6,7},{7,6},{8,9},{9,8},{10,11... | collective-permute-start | bytes 417800 | tf_op jit(solution)/shard_map/ppermute | solution.py:277
  12.0 5.3 %collective-permute-start.9 = (bf16[272,256]{1,0:T(8,128)(2,1)S(1)}, bf16[272,256]{1,0:T(8,128)(2,1)S(1)}, u32[]{:S(2)}, u32[]{:S(2)}) collective-permute-start(bf16[272,256]{1,0:T(8,128)(2,1)S(1)} %collective-permute-done.1.refs_2_), channel_id=1, source_target_pairs={{0,1},{1,0},{2,3},{3,2},{4,5},{5,4},{6,7},{7,6},{8,9},{9,8},{10,11... | collective-permute-start | bytes 417800 | tf_op jit(solution)/shard_map/ppermute | solution.py:277
  15.1 6.1 %collective-permute-start.5 = (bf16[272,256]{1,0:T(8,128)(2,1)S(1)}, bf16[272,256]{1,0:T(8,128)(2,1)S(1)}, u32[]{:S(2)}, u32[]{:S(2)}) collective-permute-start(bf16[272,256]{1,0:T(8,128)(2,1)S(1)} %collective-permute-done.2.refs_0_), channel_id=1, source_target_pairs={{0,2},{1,3},{2,0},{3,1},{4,6},{5,7},{6,4},{7,5},{8,10},{9,11},{10,... | collective-permute-start | bytes 417800 | tf_op jit(solution)/shard_map/ppermute | solution.py:277
  15.7 5.5 %collective-permute-start.6 = (bf16[272,256]{1,0:T(8,128)(2,1)S(1)}, bf16[272,256]{1,0:T(8,128)(2,1)S(1)}, u32[]{:S(2)}, u32[]{:S(2)}) collective-permute-start(bf16[272,256]{1,0:T(8,128)(2,1)S(1)} %collective-permute-done.2.refs_0_), channel_id=1, source_target_pairs={{0,4},{1,5},{2,6},{3,7},{4,0},{5,1},{6,2},{7,3},{8,12},{9,13},{10,... | collective-permute-start | bytes 417800 | tf_op jit(solution)/shard_map/ppermute | solution.py:277
  16.7 5.1 %collective-permute-start.10 = (bf16[272,256]{1,0:T(8,128)(2,1)S(1)}, bf16[272,256]{1,0:T(8,128)(2,1)S(1)}, u32[]{:S(2)}, u32[]{:S(2)}) collective-permute-start(bf16[272,256]{1,0:T(8,128)(2,1)S(1)} %collective-permute-done.2.refs_0_), channel_id=1, source_target_pairs={{0,1},{1,0},{2,3},{3,2},{4,5},{5,4},{6,7},{7,6},{8,9},{9,8},{10,11... | collective-permute-start | bytes 417800 | tf_op jit(solution)/shard_map/ppermute | solution.py:277
  16.8 5.0 %collective-permute-start.11 = (bf16[272,256]{1,0:T(8,128)(2,1)S(1)}, bf16[272,256]{1,0:T(8,128)(2,1)S(1)}, u32[]{:S(2)}, u32[]{:S(2)}) collective-permute-start(bf16[272,256]{1,0:T(8,128)(2,1)S(1)} %collective-permute-done.7.refs_0_), channel_id=1, source_target_pairs={{0,1},{1,0},{2,3},{3,2},{4,5},{5,4},{6,7},{7,6},{8,9},{9,8},{10,11... | collective-permute-start | bytes 417800 | tf_op jit(solution)/shard_map/ppermute | solution.py:277
  17.3 7.3 %collective-permute-start.4 = (bf16[272,256]{1,0:T(8,128)(2,1)S(1)}, bf16[272,256]{1,0:T(8,128)(2,1)S(1)}, u32[]{:S(2)}, u32[]{:S(2)}) collective-permute-start(bf16[272,256]{1,0:T(8,128)(2,1)S(1)} %collective-permute-done.2.refs_0_), channel_id=1, source_target_pairs={{0,6},{1,7},{2,4},{3,5},{4,2},{5,3},{6,0},{7,1},{8,14},{9,15},{10,... | collective-permute-start | bytes 417800 | tf_op jit(solution)/shard_map/ppermute | solution.py:277
  21.2 3.4 %collective-permute-start.13 = (bf16[272,256]{1,0:T(8,128)(2,1)S(1)}, bf16[272,256]{1,0:T(8,128)(2,1)S(1)}, u32[]{:S(2)}, u32[]{:S(2)}) collective-permute-start(bf16[272,256]{1,0:T(8,128)(2,1)S(1)} %collective-permute-done.6.refs_0_), channel_id=1, source_target_pairs={{0,1},{1,0},{2,3},{3,2},{4,5},{5,4},{6,7},{7,6},{8,9},{9,8},{10,11... | collective-permute-start | bytes 417800 | tf_op jit(solution)/shard_map/ppermute | solution.py:277
  21.2 3.3 %collective-permute-start.14 = (bf16[272,256]{1,0:T(8,128)(2,1)S(1)}, bf16[272,256]{1,0:T(8,128)(2,1)S(1)}, u32[]{:S(2)}, u32[]{:S(2)}) collective-permute-start(bf16[272,256]{1,0:T(8,128)(2,1)S(1)} %collective-permute-done.5.refs_1_), channel_id=1, source_target_pairs={{0,1},{1,0},{2,3},{3,2},{4,5},{5,4},{6,7},{7,6},{8,9},{9,8},{10,11... | collective-permute-start | bytes 417800 | tf_op jit(solution)/shard_map/ppermute | solution.py:277
  24.6 2.5 %collective-permute-start.12 = (bf16[272,256]{1,0:T(8,128)(2,1)S(1)}, bf16[272,256]{1,0:T(8,128)(2,1)S(1)}, u32[]{:S(2)}, u32[]{:S(2)}) collective-permute-start(bf16[272,256]{1,0:T(8,128)(2,1)S(1)} %collective-permute-done.4.refs_0_), channel_id=1, source_target_pairs={{0,1},{1,0},{2,3},{3,2},{4,5},{5,4},{6,7},{7,6},{8,9},{9,8},{10,11... | collective-permute-start | bytes 417800 | tf_op jit(solution)/shard_map/ppermute | solution.py:277
  28.0 1.8 %collective-permute-start.15 = (bf16[64,2048]{1,0:T(8,128)(2,1)S(1)}, bf16[64,2048]{1,0:T(8,128)(2,1)S(1)}, u32[]{:S(2)}, u32[]{:S(2)}) collective-permute-start(bf16[64,2048]{1,0:T(8,128)(2,1)S(1)} %get-tuple-element.94.mine_ref), channel_id=1, source_target_pairs={{0,1},{1,0},{2,3},{3,2},{4,5},{5,4},{6,7},{7,6},{8,9},{9,8},{10,11... | collective-permute-start | bytes 786440 | tf_op jit(solution)/shard_map/ppermute | solution.py:277
  31.5 1.3 %collective-permute-start.16 = (f32[64,256]{1,0:T(8,128)S(1)}, f32[64,256]{1,0:T(8,128)S(1)}, u32[]{:S(2)}, u32[]{:S(2)}) collective-permute-start(f32[64,256]{1,0:T(8,128)S(1)} %get-tuple-element.96), channel_id=1, source_target_pairs={{0,1},{1,0},{2,3},{3,2},{4,5},{5,4},{6,7},{7,6},{8,9},{9,8},{10,11... | collective-permute-start | bytes 196616 | tf_op jit(solution)/shard_map/ppermute | solution.py:277

commit v7 on v6

--- a/solution.py
+++ b/solution.py
@@ -135,7 +135,7 @@
         wanted = 4 * (x_pos ^ ((pick_col // 2) % 2)) + 2 * (core ^ sib) + pick_col % 2
         pick_ref[...] = (pick_row == wanted).astype(F32).astype(BF16)
 
-    @pl.loop(0, span, unroll=16)
+    @pl.loop(0, span, unroll=32)
     def _(k):
         row = seeds_ref[pl.ds(low_col + k, 1), :]
         high_hot = (tile_ids == row // TILE).astype(F32).astype(BF16)

time: 33.6 us -> 33.6 us (level)
  Pallas kernels: 15.8 us -> 15 us
  waiting for transfers between devices: 2.02 us -> 2.43 us
  starting transfers between devices: 14.8 us -> 15.2 us
    ppermute x17, waiting for transfers between devices: 2.02 us -> 2.43 us  [swap(): return lax.ppermute(array, ('row', 'col'), pairs)]
    pallas_call x1, Pallas kernels: 1.34 us -> 0.94 us  [more_restart(): pl.pallas_call(functools.partial(restart_kernel, False), in_specs=[SCALAR...]
    ppermute x17, starting transfers between devices: 14.8 us -> 15.2 us  [swap(): return lax.ppermute(array, ('row', 'col'), pairs)]
    pallas_call x1, Pallas kernels: 1.42 us -> 1.05 us  [chip_local(): pl.pallas_call(functools.partial(restart_kernel, True), in_specs=[SCALARS...]
  transfers between devices with their start and end apart: 17 -> 17, of which waited for: 3 -> 3; matrix products, arithmetic and copies ran while one was open for 0% -> 0% of each run, Pallas kernels for 34% -> 32%
where the time goes in v7:
time: 33.6 us; the launch traced here: 33.4 us
  starting transfers between devices  15.2 us (45%)
  Pallas kernels  15 us (45%)
  waiting for transfers between devices  2.43 us (7%)
  between operations  0.83 us (2%)
    ppermute x17, starting transfers between devices, swap(): return lax.ppermute(array, ('row', 'col'), pairs)  15.2 us
    pallas_call x6, Pallas kernels, run_stage(): pl.pallas_call(functools.partial(stage_kernel, stage), in_specs=[SCALARS]...  8.43 us
    ppermute x17, waiting for transfers between devices, swap(): return lax.ppermute(array, ('row', 'col'), pairs)  2.43 us
    pallas_call x1, Pallas kernels, chip_local(): pl.pallas_call(step_kernel, in_specs=[WHOLE] * 5, out_specs=[WHOLE] * 2,...  1.59 us
    pallas_call x1, Pallas kernels, chip_local(): pl.pallas_call(half_kernel, in_specs=[WHOLE] * 2, out_specs=WHOLE, out_sh...  1.26 us
    pallas_call x1, Pallas kernels, chip_local(): pl.pallas_call(payload_kernel, in_specs=[SCALARS] + [REMAIN] * 3, out_spe...  1.09 us
    pallas_call x1, Pallas kernels, chip_local(): pl.pallas_call(functools.partial(restart_kernel, True), in_specs=[SCALARS...  1.05 us
    pallas_call x1, Pallas kernels, more_restart(): pl.pallas_call(functools.partial(restart_kernel, False), in_specs=[SCALAR...  0.94 us
  transfers between devices with their start and end apart: 17, of which 3 were waited for; matrix products, arithmetic and copies ran while one was open for 0% of the time, Pallas kernels for 32%

profile of v7, /device:TPU:0, one launch (start us, length us, event | category | flops | bytes accessed | tf_op | source)
XLA Modules:
  0.0 33.4 jit_solution(15886224795042398316)
XLA Ops:
  0.7 1.1 %payload.1 = (bf16[272,256]{1,0:T(8,128)(2,1)S(1)}, s32[64,128]{1,0:T(8,128)S(1)}) custom-call(s32[1,1]{1,0:T(1,128)S(6)} %copy.47.count_ref, bf16[256,256]{1,0:T(8,128)(2,1)} %emb_in.1, s32[2,48]{1,0:T(2,128)} %bitcast.3, s32[64,128]{1,0:T(8,128)} %seeds_in.1), custom_call_target="tpu_custom_call" | custom-call | tf_op jit(solution)/shard_map/payload/pallas_call | solution.py:308
  1.7 3.1 %collective-permute-start = (bf16[272,256]{1,0:T(8,128)(2,1)S(1)}, bf16[272,256]{1,0:T(8,128)(2,1)S(1)}, u32[]{:S(2)}, u32[]{:S(2)}) collective-permute-start(bf16[272,256]{1,0:T(8,128)(2,1)S(1)} %get-tuple-element.52.refs_0_), channel_id=1, source_target_pairs={{0,4},{1,5},{2,6},{3,7},{4,0},{5,1},{6,2},{7,3},{8,12},{9,13},{10,... | collective-permute-start | bytes 417800 | tf_op jit(solution)/shard_map/ppermute | solution.py:277
  4.8 1.5 %collective-permute-start.1 = (bf16[272,256]{1,0:T(8,128)(2,1)S(1)}, bf16[272,256]{1,0:T(8,128)(2,1)S(1)}, u32[]{:S(2)}, u32[]{:S(2)}) collective-permute-start(bf16[272,256]{1,0:T(8,128)(2,1)S(1)} %get-tuple-element.52.refs_0_), channel_id=1, source_target_pairs={{0,2},{1,3},{2,0},{3,1},{4,6},{5,7},{6,4},{7,5},{8,10},{9,11},{10,... | collective-permute-start | bytes 417800 | tf_op jit(solution)/shard_map/ppermute | solution.py:277
  6.3 2.6 %collective-permute-start.2 = (bf16[272,256]{1,0:T(8,128)(2,1)S(1)}, bf16[272,256]{1,0:T(8,128)(2,1)S(1)}, u32[]{:S(2)}, u32[]{:S(2)}) collective-permute-start(bf16[272,256]{1,0:T(8,128)(2,1)S(1)} %get-tuple-element.52.refs_0_), channel_id=1, source_target_pairs={{0,8},{1,9},{2,10},{3,11},{4,12},{5,13},{6,14},{7,15},{8,0},{9,1},... | collective-permute-start | bytes 417800 | tf_op jit(solution)/shard_map/ppermute | solution.py:277
  8.9 1.1 %restart.1 = (bf16[128,4096]{1,0:T(8,128)(2,1)S(1)}, bf16[128,768]{1,0:T(8,128)(2,1)S(1)}) custom-call(s32[1]{0:T(128)} %bitcast.me_ref, s32[64,128]{1,0:T(8,128)S(1)} %get-tuple-element.51.seeds_ref), custom_call_target="tpu_custom_call" | custom-call | flops 1300 | bytes 130 | tf_op jit(solution)/shard_map/restart/pallas_call | solution.py:350
  10.0 2.0 %collective-permute-start.7 = (bf16[272,256]{1,0:T(8,128)(2,1)S(1)}, bf16[272,256]{1,0:T(8,128)(2,1)S(1)}, u32[]{:S(2)}, u32[]{:S(2)}) collective-permute-start(bf16[272,256]{1,0:T(8,128)(2,1)S(1)} %collective-permute-done.refs_1_), channel_id=1, source_target_pairs={{0,2},{1,3},{2,0},{3,1},{4,6},{5,7},{6,4},{7,5},{8,10},{9,11},{10,... | collective-permute-start | bytes 417800 | tf_op jit(solution)/shard_map/ppermute | solution.py:277
  12.0 0.5 %collective-permute-start.9 = (bf16[272,256]{1,0:T(8,128)(2,1)S(1)}, bf16[272,256]{1,0:T(8,128)(2,1)S(1)}, u32[]{:S(2)}, u32[]{:S(2)}) collective-permute-start(bf16[272,256]{1,0:T(8,128)(2,1)S(1)} %collective-permute-done.1.refs_2_), channel_id=1, source_target_pairs={{0,1},{1,0},{2,3},{3,2},{4,5},{5,4},{6,7},{7,6},{8,9},{9,8},{10,11... | collective-permute-start | bytes 417800 | tf_op jit(solution)/shard_map/ppermute | solution.py:277
  12.5 0.9 %restart2.1.rt_ref = bf16[128,4096]{1,0:T(8,128)(2,1)S(1)} custom-call(s32[1]{0:T(128)} %bitcast.me_ref, s32[64,128]{1,0:T(8,128)S(1)} %get-tuple-element.51.seeds_ref, bf16[128,4096]{1,0:T(8,128)(2,1)S(1)} %get-tuple-element.54.refs_0_), custom_call_target="tpu_custom_call", output_to_operand_aliasing={{}: (2, {})} | custom-call | flops 1300 | bytes 130 | tf_op jit(solution)/shard_map/restart2/pallas_call | solution.py:362
  13.5 0.7 %stage0.1 = (bf16[4096,256]{1,0:T(8,128)(2,1)S(1)}, f32[32,2304]{1,0:T(8,128)S(1)}, bf16[4096,2304]{1,0:T(8,128)(2,1)S(1)}, f32[72,2048]{1,0:T(8,128)S(1)}, f32[8,128]{1,0:T(8,128)S(1)}) custom-call(s32[1]{0:T(128)} %bitcast.me_ref, bf16[128,4096]{1,0:T(8,128)(2,1)S(1)} %restart2.1.rt_ref, bf16[128,768]{1,0:T(8,128)(2,1)S(1)} %get-tuple-element.55.pick_ref, ...), custom_call_target="tpu_custom_call" | custom-call | flops 2500 | bytes 250 | tf_op jit(solution)/shard_map/stage0/pallas_call | solution.py:334
  14.1 0.9 %collective-permute-done.2.refs_0_ = bf16[272,256]{1,0:T(8,128)(2,1)S(1)} collective-permute-done((bf16[272,256]{1,0:T(8,128)(2,1)S(1)}, bf16[272,256]{1,0:T(8,128)(2,1)S(1)}, u32[]{:S(2)}, u32[]{:S(2)}) %collective-permute-start.2) | collective-permute-done | bytes 139296 | tf_op jit(solution)/shard_map/ppermute | solution.py:277
  15.1 0.6 %collective-permute-start.5 = (bf16[272,256]{1,0:T(8,128)(2,1)S(1)}, bf16[272,256]{1,0:T(8,128)(2,1)S(1)}, u32[]{:S(2)}, u32[]{:S(2)}) collective-permute-start(bf16[272,256]{1,0:T(8,128)(2,1)S(1)} %collective-permute-done.2.refs_0_), channel_id=1, source_target_pairs={{0,2},{1,3},{2,0},{3,1},{4,6},{5,7},{6,4},{7,5},{8,10},{9,11},{10,... | collective-permute-start | bytes 417800 | tf_op jit(solution)/shard_map/ppermute | solution.py:277
  15.8 0.8 %stage1.1 = (bf16[4096,256]{1,0:T(8,128)(2,1)S(1)}, f32[32,2304]{1,0:T(8,128)S(1)}, bf16[4096,2304]{1,0:T(8,128)(2,1)S(1)}, f32[72,2048]{1,0:T(8,128)S(1)}, f32[8,128]{1,0:T(8,128)S(1)}) custom-call(s32[1]{0:T(128)} %bitcast.me_ref, bf16[128,4096]{1,0:T(8,128)(2,1)S(1)} %restart2.1.rt_ref, ...), custom_call_target="tpu_custom_call", output_to_operand_aliasing={{0}: (5, {}), {1}: (6, {}), {2}: (7, {}), {3}: (8, {})} | custom-call | flops 2500 | bytes 250 | tf_op jit(solution)/shard_map/stage1/pallas_call | solution.py:334
  16.8 0.5 %collective-permute-start.11 = (bf16[272,256]{1,0:T(8,128)(2,1)S(1)}, bf16[272,256]{1,0:T(8,128)(2,1)S(1)}, u32[]{:S(2)}, u32[]{:S(2)}) collective-permute-start(bf16[272,256]{1,0:T(8,128)(2,1)S(1)} %collective-permute-done.7.refs_0_), channel_id=1, source_target_pairs={{0,1},{1,0},{2,3},{3,2},{4,5},{5,4},{6,7},{7,6},{8,9},{9,8},{10,11... | collective-permute-start | bytes 417800 | tf_op jit(solution)/shard_map/ppermute | solution.py:277
  17.3 2.7 %collective-permute-start.4 = (bf16[272,256]{1,0:T(8,128)(2,1)S(1)}, bf16[272,256]{1,0:T(8,128)(2,1)S(1)}, u32[]{:S(2)}, u32[]{:S(2)}) collective-permute-start(bf16[272,256]{1,0:T(8,128)(2,1)S(1)} %collective-permute-done.2.refs_0_), channel_id=1, source_target_pairs={{0,6},{1,7},{2,4},{3,5},{4,2},{5,3},{6,0},{7,1},{8,14},{9,15},{10,... | collective-permute-start | bytes 417800 | tf_op jit(solution)/shard_map/ppermute | solution.py:277
  20.0 1.1 %stage2.1 = (bf16[4096,256]{1,0:T(8,128)(2,1)S(1)}, f32[32,2304]{1,0:T(8,128)S(1)}, bf16[4096,2304]{1,0:T(8,128)(2,1)S(1)}, f32[72,2048]{1,0:T(8,128)S(1)}, f32[8,128]{1,0:T(8,128)S(1)}) custom-call(s32[1]{0:T(128)} %bitcast.me_ref, bf16[128,4096]{1,0:T(8,128)(2,1)S(1)} %restart2.1.rt_ref, ...), custom_call_target="tpu_custom_call", output_to_operand_aliasing={{0}: (6, {}), {1}: (7, {}), {2}: (8, {}), {3}: (9, {})} | custom-call | flops 2500 | bytes 250 | tf_op jit(solution)/shard_map/stage2/pallas_call | solution.py:334
  21.2 0.5 %collective-permute-start.14 = (bf16[272,256]{1,0:T(8,128)(2,1)S(1)}, bf16[272,256]{1,0:T(8,128)(2,1)S(1)}, u32[]{:S(2)}, u32[]{:S(2)}) collective-permute-start(bf16[272,256]{1,0:T(8,128)(2,1)S(1)} %collective-permute-done.5.refs_1_), channel_id=1, source_target_pairs={{0,1},{1,0},{2,3},{3,2},{4,5},{5,4},{6,7},{7,6},{8,9},{9,8},{10,11... | collective-permute-start | bytes 417800 | tf_op jit(solution)/shard_map/ppermute | solution.py:277
  21.7 2.3 %stage3.1 = (bf16[4096,256]{1,0:T(8,128)(2,1)S(1)}, f32[32,2304]{1,0:T(8,128)S(1)}, bf16[4096,2304]{1,0:T(8,128)(2,1)S(1)}, f32[72,2048]{1,0:T(8,128)S(1)}, f32[8,128]{1,0:T(8,128)S(1)}) custom-call(s32[1]{0:T(128)} %bitcast.me_ref, bf16[128,4096]{1,0:T(8,128)(2,1)S(1)} %restart2.1.rt_ref, ...), custom_call_target="tpu_custom_call", output_to_operand_aliasing={{0}: (7, {}), {1}: (8, {}), {2}: (9, {}), {3}: (10, {})} | custom-call | flops 2500 | bytes 250 | tf_op jit(solution)/shard_map/stage3/pallas_call | solution.py:334
  24.6 2.5 %stage4.1 = (bf16[4096,256]{1,0:T(8,128)(2,1)S(1)}, f32[32,2304]{1,0:T(8,128)S(1)}, bf16[4096,2304]{1,0:T(8,128)(2,1)S(1)}, f32[72,2048]{1,0:T(8,128)S(1)}) custom-call(s32[1]{0:T(128)} %bitcast.me_ref, bf16[128,4096]{1,0:T(8,128)(2,1)S(1)} %restart2.1.rt_ref, ...), custom_call_target="tpu_custom_call", output_to_operand_aliasing={{0}: (6, {}), {1}: (7, {}), {2}: (8, {}), {3}: (9, {})} | custom-call | flops 2500 | bytes 250 | tf_op jit(solution)/shard_map/stage4/pallas_call | solution.py:334
  27.1 1.0 %stage5.1 = (bf16[4096,256]{1,0:T(8,128)(2,1)S(1)}, f32[32,2304]{1,0:T(8,128)S(1)}, bf16[4096,2304]{1,0:T(8,128)(2,1)S(1)}, f32[72,2048]{1,0:T(8,128)S(1)}, bf16...) custom-call(s32[1]{0:T(128)} %bitcast.me_ref, ...), custom_call_target="tpu_custom_call", output_to_operand_aliasing={{0}: (4, {}), {1}: (5, {}), {2}: (6, {}), {3}: (7, {})} | custom-call | flops 2500 | bytes 250 | tf_op jit(solution)/shard_map/stage5/pallas_call | solution.py:334
  28.0 0.6 %collective-permute-start.15 = (bf16[64,2048]{1,0:T(8,128)(2,1)S(1)}, bf16[64,2048]{1,0:T(8,128)(2,1)S(1)}, u32[]{:S(2)}, u32[]{:S(2)}) collective-permute-start(bf16[64,2048]{1,0:T(8,128)(2,1)S(1)} %get-tuple-element.94.mine_ref), channel_id=1, source_target_pairs={{0,1},{1,0},{2,3},{3,2},{4,5},{5,4},{6,7},{7,6},{8,9},{9,8},{10,11... | collective-permute-start | bytes 786440 | tf_op jit(solution)/shard_map/ppermute | solution.py:277
  28.6 1.3 %half.1.half_ref = f32[64,2048]{1,0:T(8,128)S(1)} custom-call(bf16[4096,2304]{1,0:T(8,128)(2,1)S(1)} %get-tuple-element.93.kt_ref, bf16[64,2048]{1,0:T(8,128)(2,1)S(1)} %get-tuple-element.94.mine_ref), custom_call_target="tpu_custom_call" | custom-call | flops 1500 | bytes 150 | tf_op jit(solution)/shard_map/half/pallas_call | solution.py:404
  29.9 1.6 %step.1 = (f32[64,256]{1,0:T(8,128)S(1)}, f32[64,256]{1,0:T(8,128)S(1)}) custom-call(bf16[128,4096]{1,0:T(8,128)(2,1)S(1)} %restart2.1.rt_ref, bf16[4096,2304]{1,0:T(8,128)(2,1)S(1)} %get-tuple-element.93.kt_ref, f32[8,2048]{1,0:T(8,128)S(1)} %get-tuple-element.92.gain_ref, f32[64,2048]{1,0:T(8,128)S(1)} %half.1.half_ref, ...), custom_call_target="tpu_custom_call" | custom-call | flops 1500 | bytes 150 | tf_op jit(solution)/shard_map/step/pallas_call | solution.py:413
  31.8 1.0 %collective-permute-done.16.other_ref = f32[64,256]{1,0:T(8,128)S(1)} collective-permute-done((f32[64,256]{1,0:T(8,128)S(1)}, f32[64,256]{1,0:T(8,128)S(1)}, u32[]{:S(2)}, u32[]{:S(2)}) %collective-permute-start.16) | collective-permute-done | bytes 65568 | tf_op jit(solution)/shard_map/ppermute | solution.py:277
  32.8 0.6 %last.1 = f32[64,256]{1,0:T(8,128)} custom-call(bf16[128,4096]{1,0:T(8,128)(2,1)S(1)} %restart2.1.rt_ref, f32[8,2048]{1,0:T(8,128)S(1)} %get-tuple-element.92.gain_ref, f32[64,256]{1,0:T(8,128)S(1)} %get-tuple-element.95.mine_ref, f32[64,256]{1,0:T(8,128)S(1)} %collective-permute-done.16.other_ref), custom_call_target="tpu_custom_call" | custom-call | flops 500 | bytes 50 | tf_op jit(solution)/shard_map/last/pallas_call | solution.py:423
  (22 shorter events, 1.2 us)
Async XLA Ops:
  1.7 8.2 %collective-permute-start = (bf16[272,256]{1,0:T(8,128)(2,1)S(1)}, bf16[272,256]{1,0:T(8,128)(2,1)S(1)}, u32[]{:S(2)}, u32[]{:S(2)}) collective-permute-start(bf16[272,256]{1,0:T(8,128)(2,1)S(1)} %get-tuple-element.52.refs_0_), channel_id=1, source_target_pairs={{0,4},{1,5},{2,6},{3,7},{4,0},{5,1},{6,2},{7,3},{8,12},{9,13},{10,... | collective-permute-start | bytes 417800 | tf_op jit(solution)/shard_map/ppermute | solution.py:277
  4.8 5.2 %collective-permute-start.1 = (bf16[272,256]{1,0:T(8,128)(2,1)S(1)}, bf16[272,256]{1,0:T(8,128)(2,1)S(1)}, u32[]{:S(2)}, u32[]{:S(2)}) collective-permute-start(bf16[272,256]{1,0:T(8,128)(2,1)S(1)} %get-tuple-element.52.refs_0_), channel_id=1, source_target_pairs={{0,2},{1,3},{2,0},{3,1},{4,6},{5,7},{6,4},{7,5},{8,10},{9,11},{10,... | collective-permute-start | bytes 417800 | tf_op jit(solution)/shard_map/ppermute | solution.py:277
  6.3 8.7 %collective-permute-start.2 = (bf16[272,256]{1,0:T(8,128)(2,1)S(1)}, bf16[272,256]{1,0:T(8,128)(2,1)S(1)}, u32[]{:S(2)}, u32[]{:S(2)}) collective-permute-start(bf16[272,256]{1,0:T(8,128)(2,1)S(1)} %get-tuple-element.52.refs_0_), channel_id=1, source_target_pairs={{0,8},{1,9},{2,10},{3,11},{4,12},{5,13},{6,14},{7,15},{8,0},{9,1},... | collective-permute-start | bytes 417800 | tf_op jit(solution)/shard_map/ppermute | solution.py:277
  8.9 6.1 %collective-permute-start.3 = (bf16[272,256]{1,0:T(8,128)(2,1)S(1)}, bf16[272,256]{1,0:T(8,128)(2,1)S(1)}, u32[]{:S(2)}, u32[]{:S(2)}) collective-permute-start(bf16[272,256]{1,0:T(8,128)(2,1)S(1)} %get-tuple-element.52.refs_0_), channel_id=1, source_target_pairs={{0,1},{1,0},{2,3},{3,2},{4,5},{5,4},{6,7},{7,6},{8,9},{9,8},{10,11... | collective-permute-start | bytes 417800 | tf_op jit(solution)/shard_map/ppermute | solution.py:277
  10.0 6.7 %collective-permute-start.7 = (bf16[272,256]{1,0:T(8,128)(2,1)S(1)}, bf16[272,256]{1,0:T(8,128)(2,1)S(1)}, u32[]{:S(2)}, u32[]{:S(2)}) collective-permute-start(bf16[272,256]{1,0:T(8,128)(2,1)S(1)} %collective-permute-done.refs_1_), channel_id=1, source_target_pairs={{0,2},{1,3},{2,0},{3,1},{4,6},{5,7},{6,4},{7,5},{8,10},{9,11},{10,... | collective-permute-start | bytes 417800 | tf_op jit(solution)/shard_map/ppermute | solution.py:277
  12.0 4.8 %collective-permute-start.8 = (bf16[272,256]{1,0:T(8,128)(2,1)S(1)}, bf16[272,256]{1,0:T(8,128)(2,1)S(1)}, u32[]{:S(2)}, u32[]{:S(2)}) collective-permute-start(bf16[272,256]{1,0:T(8,128)(2,1)S(1)} %collective-permute-done.refs_1_), channel_id=1, source_target_pairs={{0,1},{1,0},{2,3},{3,2},{4,5},{5,4},{6,7},{7,6},{8,9},{9,8},{10,11... | collective-permute-start | bytes 417800 | tf_op jit(solution)/shard_map/ppermute | solution.py:277
  12.0 5.3 %collective-permute-start.9 = (bf16[272,256]{1,0:T(8,128)(2,1)S(1)}, bf16[272,256]{1,0:T(8,128)(2,1)S(1)}, u32[]{:S(2)}, u32[]{:S(2)}) collective-permute-start(bf16[272,256]{1,0:T(8,128)(2,1)S(1)} %collective-permute-done.1.refs_2_), channel_id=1, source_target_pairs={{0,1},{1,0},{2,3},{3,2},{4,5},{5,4},{6,7},{7,6},{8,9},{9,8},{10,11... | collective-permute-start | bytes 417800 | tf_op jit(solution)/shard_map/ppermute | solution.py:277
  15.1 6.1 %collective-permute-start.5 = (bf16[272,256]{1,0:T(8,128)(2,1)S(1)}, bf16[272,256]{1,0:T(8,128)(2,1)S(1)}, u32[]{:S(2)}, u32[]{:S(2)}) collective-permute-start(bf16[272,256]{1,0:T(8,128)(2,1)S(1)} %collective-permute-done.2.refs_0_), channel_id=1, source_target_pairs={{0,2},{1,3},{2,0},{3,1},{4,6},{5,7},{6,4},{7,5},{8,10},{9,11},{10,... | collective-permute-start | bytes 417800 | tf_op jit(solution)/shard_map/ppermute | solution.py:277
  15.7 5.5 %collective-permute-start.6 = (bf16[272,256]{1,0:T(8,128)(2,1)S(1)}, bf16[272,256]{1,0:T(8,128)(2,1)S(1)}, u32[]{:S(2)}, u32[]{:S(2)}) collective-permute-start(bf16[272,256]{1,0:T(8,128)(2,1)S(1)} %collective-permute-done.2.refs_0_), channel_id=1, source_target_pairs={{0,4},{1,5},{2,6},{3,7},{4,0},{5,1},{6,2},{7,3},{8,12},{9,13},{10,... | collective-permute-start | bytes 417800 | tf_op jit(solution)/shard_map/ppermute | solution.py:277
  16.7 5.1 %collective-permute-start.10 = (bf16[272,256]{1,0:T(8,128)(2,1)S(1)}, bf16[272,256]{1,0:T(8,128)(2,1)S(1)}, u32[]{:S(2)}, u32[]{:S(2)}) collective-permute-start(bf16[272,256]{1,0:T(8,128)(2,1)S(1)} %collective-permute-done.2.refs_0_), channel_id=1, source_target_pairs={{0,1},{1,0},{2,3},{3,2},{4,5},{5,4},{6,7},{7,6},{8,9},{9,8},{10,11... | collective-permute-start | bytes 417800 | tf_op jit(solution)/shard_map/ppermute | solution.py:277
  16.8 5.0 %collective-permute-start.11 = (bf16[272,256]{1,0:T(8,128)(2,1)S(1)}, bf16[272,256]{1,0:T(8,128)(2,1)S(1)}, u32[]{:S(2)}, u32[]{:S(2)}) collective-permute-start(bf16[272,256]{1,0:T(8,128)(2,1)S(1)} %collective-permute-done.7.refs_0_), channel_id=1, source_target_pairs={{0,1},{1,0},{2,3},{3,2},{4,5},{5,4},{6,7},{7,6},{8,9},{9,8},{10,11... | collective-permute-start | bytes 417800 | tf_op jit(solution)/shard_map/ppermute | solution.py:277
  17.3 7.3 %collective-permute-start.4 = (bf16[272,256]{1,0:T(8,128)(2,1)S(1)}, bf16[272,256]{1,0:T(8,128)(2,1)S(1)}, u32[]{:S(2)}, u32[]{:S(2)}) collective-permute-start(bf16[272,256]{1,0:T(8,128)(2,1)S(1)} %collective-permute-done.2.refs_0_), channel_id=1, source_target_pairs={{0,6},{1,7},{2,4},{3,5},{4,2},{5,3},{6,0},{7,1},{8,14},{9,15},{10,... | collective-permute-start | bytes 417800 | tf_op jit(solution)/shard_map/ppermute | solution.py:277
  21.2 3.4 %collective-permute-start.13 = (bf16[272,256]{1,0:T(8,128)(2,1)S(1)}, bf16[272,256]{1,0:T(8,128)(2,1)S(1)}, u32[]{:S(2)}, u32[]{:S(2)}) collective-permute-start(bf16[272,256]{1,0:T(8,128)(2,1)S(1)} %collective-permute-done.6.refs_0_), channel_id=1, source_target_pairs={{0,1},{1,0},{2,3},{3,2},{4,5},{5,4},{6,7},{7,6},{8,9},{9,8},{10,11... | collective-permute-start | bytes 417800 | tf_op jit(solution)/shard_map/ppermute | solution.py:277
  21.2 3.3 %collective-permute-start.14 = (bf16[272,256]{1,0:T(8,128)(2,1)S(1)}, bf16[272,256]{1,0:T(8,128)(2,1)S(1)}, u32[]{:S(2)}, u32[]{:S(2)}) collective-permute-start(bf16[272,256]{1,0:T(8,128)(2,1)S(1)} %collective-permute-done.5.refs_1_), channel_id=1, source_target_pairs={{0,1},{1,0},{2,3},{3,2},{4,5},{5,4},{6,7},{7,6},{8,9},{9,8},{10,11... | collective-permute-start | bytes 417800 | tf_op jit(solution)/shard_map/ppermute | solution.py:277
  24.6 2.5 %collective-permute-start.12 = (bf16[272,256]{1,0:T(8,128)(2,1)S(1)}, bf16[272,256]{1,0:T(8,128)(2,1)S(1)}, u32[]{:S(2)}, u32[]{:S(2)}) collective-permute-start(bf16[272,256]{1,0:T(8,128)(2,1)S(1)} %collective-permute-done.4.refs_0_), channel_id=1, source_target_pairs={{0,1},{1,0},{2,3},{3,2},{4,5},{5,4},{6,7},{7,6},{8,9},{9,8},{10,11... | collective-permute-start | bytes 417800 | tf_op jit(solution)/shard_map/ppermute | solution.py:277
  28.0 1.8 %collective-permute-start.15 = (bf16[64,2048]{1,0:T(8,128)(2,1)S(1)}, bf16[64,2048]{1,0:T(8,128)(2,1)S(1)}, u32[]{:S(2)}, u32[]{:S(2)}) collective-permute-start(bf16[64,2048]{1,0:T(8,128)(2,1)S(1)} %get-tuple-element.94.mine_ref), channel_id=1, source_target_pairs={{0,1},{1,0},{2,3},{3,2},{4,5},{5,4},{6,7},{7,6},{8,9},{9,8},{10,11... | collective-permute-start | bytes 786440 | tf_op jit(solution)/shard_map/ppermute | solution.py:277
  31.5 1.3 %collective-permute-start.16 = (f32[64,256]{1,0:T(8,128)S(1)}, f32[64,256]{1,0:T(8,128)S(1)}, u32[]{:S(2)}, u32[]{:S(2)}) collective-permute-start(f32[64,256]{1,0:T(8,128)S(1)} %get-tuple-element.96), channel_id=1, source_target_pairs={{0,1},{1,0},{2,3},{3,2},{4,5},{5,4},{6,7},{7,6},{8,9},{9,8},{10,11... | collective-permute-start | bytes 196616 | tf_op jit(solution)/shard_map/ppermute | solution.py:277

commit v8 on v7

--- a/solution.py
+++ b/solution.py
@@ -386,7 +386,7 @@
     b20 = swap(z2, sibling)
     b11 = swap(x1, sibling)
     state, (done,) = run_stage(2, rt, [x1, b10, b01], state, mark, done)
-    x2, z3, done = lax.optimization_barrier((x2, z3, done))
+    z3, x2, done = lax.optimization_barrier((z3, x2, done))
     b30 = swap(z3, sibling)
     b21 = swap(x2, sibling)
     state, (done,) = run_stage(3, rt, [z3, x2, b20, b11], state, mark, done)

time: 33.6 us -> 33.2 us (0.988)
  waiting for transfers between devices: 2.43 us -> 1.95 us
    ppermute x17, waiting for transfers between devices: 2.43 us -> 1.95 us  [swap(): return lax.ppermute(array, ('row', 'col'), pairs)]
  transfers between devices with their start and end apart: 17 -> 17, of which waited for: 3 -> 2; matrix products, arithmetic and copies ran while one was open for 0% -> 0% of each run, Pallas kernels for 32% -> 32%
where the time goes in v8:
time: 33.2 us; the launch traced here: 33.1 us
  starting transfers between devices  15.3 us (46%)
  Pallas kernels  15 us (45%)
  waiting for transfers between devices  1.95 us (6%)
  between operations  0.83 us (2%)
    ppermute x17, starting transfers between devices, swap(): return lax.ppermute(array, ('row', 'col'), pairs)  15.3 us
    pallas_call x6, Pallas kernels, run_stage(): pl.pallas_call(functools.partial(stage_kernel, stage), in_specs=[SCALARS]...  8.43 us
    ppermute x17, waiting for transfers between devices, swap(): return lax.ppermute(array, ('row', 'col'), pairs)  1.95 us
    pallas_call x1, Pallas kernels, chip_local(): pl.pallas_call(step_kernel, in_specs=[WHOLE] * 5, out_specs=[WHOLE] * 2,...  1.59 us
    pallas_call x1, Pallas kernels, chip_local(): pl.pallas_call(half_kernel, in_specs=[WHOLE] * 2, out_specs=WHOLE, out_sh...  1.26 us
    pallas_call x1, Pallas kernels, chip_local(): pl.pallas_call(payload_kernel, in_specs=[SCALARS] + [REMAIN] * 3, out_spe...  1.09 us
    pallas_call x1, Pallas kernels, chip_local(): pl.pallas_call(functools.partial(restart_kernel, True), in_specs=[SCALARS...  1.05 us
    pallas_call x1, Pallas kernels, more_restart(): pl.pallas_call(functools.partial(restart_kernel, False), in_specs=[SCALAR...  0.94 us
  transfers between devices with their start and end apart: 17, of which 2 were waited for; matrix products, arithmetic and copies ran while one was open for 0% of the time, Pallas kernels for 32%

profile of v8, /device:TPU:0, one launch (start us, length us, event | category | flops | bytes accessed | tf_op | source)
XLA Modules:
  0.0 33.1 jit_solution(15133857585881119341)
XLA Ops:
  0.7 1.1 %payload.1 = (bf16[272,256]{1,0:T(8,128)(2,1)S(1)}, s32[64,128]{1,0:T(8,128)S(1)}) custom-call(s32[1,1]{1,0:T(1,128)S(6)} %copy.47.count_ref, bf16[256,256]{1,0:T(8,128)(2,1)} %emb_in.1, s32[2,48]{1,0:T(2,128)} %bitcast.3, s32[64,128]{1,0:T(8,128)} %seeds_in.1), custom_call_target="tpu_custom_call" | custom-call | tf_op jit(solution)/shard_map/payload/pallas_call | solution.py:308
  1.7 3.1 %collective-permute-start = (bf16[272,256]{1,0:T(8,128)(2,1)S(1)}, bf16[272,256]{1,0:T(8,128)(2,1)S(1)}, u32[]{:S(2)}, u32[]{:S(2)}) collective-permute-start(bf16[272,256]{1,0:T(8,128)(2,1)S(1)} %get-tuple-element.52.refs_0_), channel_id=1, source_target_pairs={{0,4},{1,5},{2,6},{3,7},{4,0},{5,1},{6,2},{7,3},{8,12},{9,13},{10,... | collective-permute-start | bytes 417800 | tf_op jit(solution)/shard_map/ppermute | solution.py:277
  4.8 1.5 %collective-permute-start.1 = (bf16[272,256]{1,0:T(8,128)(2,1)S(1)}, bf16[272,256]{1,0:T(8,128)(2,1)S(1)}, u32[]{:S(2)}, u32[]{:S(2)}) collective-permute-start(bf16[272,256]{1,0:T(8,128)(2,1)S(1)} %get-tuple-element.52.refs_0_), channel_id=1, source_target_pairs={{0,2},{1,3},{2,0},{3,1},{4,6},{5,7},{6,4},{7,5},{8,10},{9,11},{10,... | collective-permute-start | bytes 417800 | tf_op jit(solution)/shard_map/ppermute | solution.py:277
  6.3 2.6 %collective-permute-start.2 = (bf16[272,256]{1,0:T(8,128)(2,1)S(1)}, bf16[272,256]{1,0:T(8,128)(2,1)S(1)}, u32[]{:S(2)}, u32[]{:S(2)}) collective-permute-start(bf16[272,256]{1,0:T(8,128)(2,1)S(1)} %get-tuple-element.52.refs_0_), channel_id=1, source_target_pairs={{0,8},{1,9},{2,10},{3,11},{4,12},{5,13},{6,14},{7,15},{8,0},{9,1},... | collective-permute-start | bytes 417800 | tf_op jit(solution)/shard_map/ppermute | solution.py:277
  8.9 1.1 %restart.1 = (bf16[128,4096]{1,0:T(8,128)(2,1)S(1)}, bf16[128,768]{1,0:T(8,128)(2,1)S(1)}) custom-call(s32[1]{0:T(128)} %bitcast.me_ref, s32[64,128]{1,0:T(8,128)S(1)} %get-tuple-element.51.seeds_ref), custom_call_target="tpu_custom_call" | custom-call | flops 1300 | bytes 130 | tf_op jit(solution)/shard_map/restart/pallas_call | solution.py:350
  10.0 2.0 %collective-permute-start.7 = (bf16[272,256]{1,0:T(8,128)(2,1)S(1)}, bf16[272,256]{1,0:T(8,128)(2,1)S(1)}, u32[]{:S(2)}, u32[]{:S(2)}) collective-permute-start(bf16[272,256]{1,0:T(8,128)(2,1)S(1)} %collective-permute-done.refs_1_), channel_id=1, source_target_pairs={{0,2},{1,3},{2,0},{3,1},{4,6},{5,7},{6,4},{7,5},{8,10},{9,11},{10,... | collective-permute-start | bytes 417800 | tf_op jit(solution)/shard_map/ppermute | solution.py:277
  12.0 0.5 %collective-permute-start.9 = (bf16[272,256]{1,0:T(8,128)(2,1)S(1)}, bf16[272,256]{1,0:T(8,128)(2,1)S(1)}, u32[]{:S(2)}, u32[]{:S(2)}) collective-permute-start(bf16[272,256]{1,0:T(8,128)(2,1)S(1)} %collective-permute-done.1.refs_2_), channel_id=1, source_target_pairs={{0,1},{1,0},{2,3},{3,2},{4,5},{5,4},{6,7},{7,6},{8,9},{9,8},{10,11... | collective-permute-start | bytes 417800 | tf_op jit(solution)/shard_map/ppermute | solution.py:277
  12.5 0.9 %restart2.1.rt_ref = bf16[128,4096]{1,0:T(8,128)(2,1)S(1)} custom-call(s32[1]{0:T(128)} %bitcast.me_ref, s32[64,128]{1,0:T(8,128)S(1)} %get-tuple-element.51.seeds_ref, bf16[128,4096]{1,0:T(8,128)(2,1)S(1)} %get-tuple-element.54.refs_0_), custom_call_target="tpu_custom_call", output_to_operand_aliasing={{}: (2, {})} | custom-call | flops 1300 | bytes 130 | tf_op jit(solution)/shard_map/restart2/pallas_call | solution.py:362
  13.5 0.7 %stage0.1 = (bf16[4096,256]{1,0:T(8,128)(2,1)S(1)}, f32[32,2304]{1,0:T(8,128)S(1)}, bf16[4096,2304]{1,0:T(8,128)(2,1)S(1)}, f32[72,2048]{1,0:T(8,128)S(1)}, f32[8,128]{1,0:T(8,128)S(1)}) custom-call(s32[1]{0:T(128)} %bitcast.me_ref, bf16[128,4096]{1,0:T(8,128)(2,1)S(1)} %restart2.1.rt_ref, bf16[128,768]{1,0:T(8,128)(2,1)S(1)} %get-tuple-element.55.pick_ref, ...), custom_call_target="tpu_custom_call" | custom-call | flops 2500 | bytes 250 | tf_op jit(solution)/shard_map/stage0/pallas_call | solution.py:334
  14.1 0.9 %collective-permute-done.2.refs_0_ = bf16[272,256]{1,0:T(8,128)(2,1)S(1)} collective-permute-done((bf16[272,256]{1,0:T(8,128)(2,1)S(1)}, bf16[272,256]{1,0:T(8,128)(2,1)S(1)}, u32[]{:S(2)}, u32[]{:S(2)}) %collective-permute-start.2) | collective-permute-done | bytes 139296 | tf_op jit(solution)/shard_map/ppermute | solution.py:277
  15.1 0.8 %collective-permute-start.6 = (bf16[272,256]{1,0:T(8,128)(2,1)S(1)}, bf16[272,256]{1,0:T(8,128)(2,1)S(1)}, u32[]{:S(2)}, u32[]{:S(2)}) collective-permute-start(bf16[272,256]{1,0:T(8,128)(2,1)S(1)} %collective-permute-done.2.refs_0_), channel_id=1, source_target_pairs={{0,2},{1,3},{2,0},{3,1},{4,6},{5,7},{6,4},{7,5},{8,10},{9,11},{10,... | collective-permute-start | bytes 417800 | tf_op jit(solution)/shard_map/ppermute | solution.py:277
  15.8 0.8 %stage1.1 = (bf16[4096,256]{1,0:T(8,128)(2,1)S(1)}, f32[32,2304]{1,0:T(8,128)S(1)}, bf16[4096,2304]{1,0:T(8,128)(2,1)S(1)}, f32[72,2048]{1,0:T(8,128)S(1)}, f32[8,128]{1,0:T(8,128)S(1)}) custom-call(s32[1]{0:T(128)} %bitcast.me_ref, bf16[128,4096]{1,0:T(8,128)(2,1)S(1)} %restart2.1.rt_ref, ...), custom_call_target="tpu_custom_call", output_to_operand_aliasing={{0}: (5, {}), {1}: (6, {}), {2}: (7, {}), {3}: (8, {})} | custom-call | flops 2500 | bytes 250 | tf_op jit(solution)/shard_map/stage1/pallas_call | solution.py:334
  16.8 0.5 %collective-permute-start.11 = (bf16[272,256]{1,0:T(8,128)(2,1)S(1)}, bf16[272,256]{1,0:T(8,128)(2,1)S(1)}, u32[]{:S(2)}, u32[]{:S(2)}) collective-permute-start(bf16[272,256]{1,0:T(8,128)(2,1)S(1)} %collective-permute-done.7.refs_0_), channel_id=1, source_target_pairs={{0,1},{1,0},{2,3},{3,2},{4,5},{5,4},{6,7},{7,6},{8,9},{9,8},{10,11... | collective-permute-start | bytes 417800 | tf_op jit(solution)/shard_map/ppermute | solution.py:277
  17.3 2.7 %collective-permute-start.4 = (bf16[272,256]{1,0:T(8,128)(2,1)S(1)}, bf16[272,256]{1,0:T(8,128)(2,1)S(1)}, u32[]{:S(2)}, u32[]{:S(2)}) collective-permute-start(bf16[272,256]{1,0:T(8,128)(2,1)S(1)} %collective-permute-done.2.refs_0_), channel_id=1, source_target_pairs={{0,6},{1,7},{2,4},{3,5},{4,2},{5,3},{6,0},{7,1},{8,14},{9,15},{10,... | collective-permute-start | bytes 417800 | tf_op jit(solution)/shard_map/ppermute | solution.py:277
  20.0 1.1 %stage2.1 = (bf16[4096,256]{1,0:T(8,128)(2,1)S(1)}, f32[32,2304]{1,0:T(8,128)S(1)}, bf16[4096,2304]{1,0:T(8,128)(2,1)S(1)}, f32[72,2048]{1,0:T(8,128)S(1)}, f32[8,128]{1,0:T(8,128)S(1)}) custom-call(s32[1]{0:T(128)} %bitcast.me_ref, bf16[128,4096]{1,0:T(8,128)(2,1)S(1)} %restart2.1.rt_ref, ...), custom_call_target="tpu_custom_call", output_to_operand_aliasing={{0}: (6, {}), {1}: (7, {}), {2}: (8, {}), {3}: (9, {})} | custom-call | flops 2500 | bytes 250 | tf_op jit(solution)/shard_map/stage2/pallas_call | solution.py:334
  21.2 0.5 %collective-permute-start.14 = (bf16[272,256]{1,0:T(8,128)(2,1)S(1)}, bf16[272,256]{1,0:T(8,128)(2,1)S(1)}, u32[]{:S(2)}, u32[]{:S(2)}) collective-permute-start(bf16[272,256]{1,0:T(8,128)(2,1)S(1)} %collective-permute-done.6.refs_1_), channel_id=1, source_target_pairs={{0,1},{1,0},{2,3},{3,2},{4,5},{5,4},{6,7},{7,6},{8,9},{9,8},{10,11... | collective-permute-start | bytes 417800 | tf_op jit(solution)/shard_map/ppermute | solution.py:277
  21.7 2.3 %stage3.1 = (bf16[4096,256]{1,0:T(8,128)(2,1)S(1)}, f32[32,2304]{1,0:T(8,128)S(1)}, bf16[4096,2304]{1,0:T(8,128)(2,1)S(1)}, f32[72,2048]{1,0:T(8,128)S(1)}, f32[8,128]{1,0:T(8,128)S(1)}) custom-call(s32[1]{0:T(128)} %bitcast.me_ref, bf16[128,4096]{1,0:T(8,128)(2,1)S(1)} %restart2.1.rt_ref, ...), custom_call_target="tpu_custom_call", output_to_operand_aliasing={{0}: (7, {}), {1}: (8, {}), {2}: (9, {}), {3}: (10, {})} | custom-call | flops 2500 | bytes 250 | tf_op jit(solution)/shard_map/stage3/pallas_call | solution.py:334
  24.3 2.5 %stage4.1 = (bf16[4096,256]{1,0:T(8,128)(2,1)S(1)}, f32[32,2304]{1,0:T(8,128)S(1)}, bf16[4096,2304]{1,0:T(8,128)(2,1)S(1)}, f32[72,2048]{1,0:T(8,128)S(1)}) custom-call(s32[1]{0:T(128)} %bitcast.me_ref, bf16[128,4096]{1,0:T(8,128)(2,1)S(1)} %restart2.1.rt_ref, ...), custom_call_target="tpu_custom_call", output_to_operand_aliasing={{0}: (6, {}), {1}: (7, {}), {2}: (8, {}), {3}: (9, {})} | custom-call | flops 2500 | bytes 250 | tf_op jit(solution)/shard_map/stage4/pallas_call | solution.py:334
  26.7 1.0 %stage5.1 = (bf16[4096,256]{1,0:T(8,128)(2,1)S(1)}, f32[32,2304]{1,0:T(8,128)S(1)}, bf16[4096,2304]{1,0:T(8,128)(2,1)S(1)}, f32[72,2048]{1,0:T(8,128)S(1)}, bf16...) custom-call(s32[1]{0:T(128)} %bitcast.me_ref, ...), custom_call_target="tpu_custom_call", output_to_operand_aliasing={{0}: (4, {}), {1}: (5, {}), {2}: (6, {}), {3}: (7, {})} | custom-call | flops 2500 | bytes 250 | tf_op jit(solution)/shard_map/stage5/pallas_call | solution.py:334
  27.7 0.5 %collective-permute-start.15 = (bf16[64,2048]{1,0:T(8,128)(2,1)S(1)}, bf16[64,2048]{1,0:T(8,128)(2,1)S(1)}, u32[]{:S(2)}, u32[]{:S(2)}) collective-permute-start(bf16[64,2048]{1,0:T(8,128)(2,1)S(1)} %get-tuple-element.94.mine_ref), channel_id=1, source_target_pairs={{0,1},{1,0},{2,3},{3,2},{4,5},{5,4},{6,7},{7,6},{8,9},{9,8},{10,11... | collective-permute-start | bytes 786440 | tf_op jit(solution)/shard_map/ppermute | solution.py:277
  28.2 1.3 %half.1.half_ref = f32[64,2048]{1,0:T(8,128)S(1)} custom-call(bf16[4096,2304]{1,0:T(8,128)(2,1)S(1)} %get-tuple-element.93.kt_ref, bf16[64,2048]{1,0:T(8,128)(2,1)S(1)} %get-tuple-element.94.mine_ref), custom_call_target="tpu_custom_call" | custom-call | flops 1500 | bytes 150 | tf_op jit(solution)/shard_map/half/pallas_call | solution.py:404
  29.5 1.6 %step.1 = (f32[64,256]{1,0:T(8,128)S(1)}, f32[64,256]{1,0:T(8,128)S(1)}) custom-call(bf16[128,4096]{1,0:T(8,128)(2,1)S(1)} %restart2.1.rt_ref, bf16[4096,2304]{1,0:T(8,128)(2,1)S(1)} %get-tuple-element.93.kt_ref, f32[8,2048]{1,0:T(8,128)S(1)} %get-tuple-element.92.gain_ref, f32[64,2048]{1,0:T(8,128)S(1)} %half.1.half_ref, ...), custom_call_target="tpu_custom_call" | custom-call | flops 1500 | bytes 150 | tf_op jit(solution)/shard_map/step/pallas_call | solution.py:413
  31.4 1.0 %collective-permute-done.16.other_ref = f32[64,256]{1,0:T(8,128)S(1)} collective-permute-done((f32[64,256]{1,0:T(8,128)S(1)}, f32[64,256]{1,0:T(8,128)S(1)}, u32[]{:S(2)}, u32[]{:S(2)}) %collective-permute-start.16) | collective-permute-done | bytes 65568 | tf_op jit(solution)/shard_map/ppermute | solution.py:277
  32.4 0.6 %last.1 = f32[64,256]{1,0:T(8,128)} custom-call(bf16[128,4096]{1,0:T(8,128)(2,1)S(1)} %restart2.1.rt_ref, f32[8,2048]{1,0:T(8,128)S(1)} %get-tuple-element.92.gain_ref, f32[64,256]{1,0:T(8,128)S(1)} %get-tuple-element.95.mine_ref, f32[64,256]{1,0:T(8,128)S(1)} %collective-permute-done.16.other_ref), custom_call_target="tpu_custom_call" | custom-call | flops 500 | bytes 50 | tf_op jit(solution)/shard_map/last/pallas_call | solution.py:423
  (22 shorter events, 0.7 us)
Async XLA Ops:
  1.7 8.2 %collective-permute-start = (bf16[272,256]{1,0:T(8,128)(2,1)S(1)}, bf16[272,256]{1,0:T(8,128)(2,1)S(1)}, u32[]{:S(2)}, u32[]{:S(2)}) collective-permute-start(bf16[272,256]{1,0:T(8,128)(2,1)S(1)} %get-tuple-element.52.refs_0_), channel_id=1, source_target_pairs={{0,4},{1,5},{2,6},{3,7},{4,0},{5,1},{6,2},{7,3},{8,12},{9,13},{10,... | collective-permute-start | bytes 417800 | tf_op jit(solution)/shard_map/ppermute | solution.py:277
  4.8 5.2 %collective-permute-start.1 = (bf16[272,256]{1,0:T(8,128)(2,1)S(1)}, bf16[272,256]{1,0:T(8,128)(2,1)S(1)}, u32[]{:S(2)}, u32[]{:S(2)}) collective-permute-start(bf16[272,256]{1,0:T(8,128)(2,1)S(1)} %get-tuple-element.52.refs_0_), channel_id=1, source_target_pairs={{0,2},{1,3},{2,0},{3,1},{4,6},{5,7},{6,4},{7,5},{8,10},{9,11},{10,... | collective-permute-start | bytes 417800 | tf_op jit(solution)/shard_map/ppermute | solution.py:277
  6.3 8.7 %collective-permute-start.2 = (bf16[272,256]{1,0:T(8,128)(2,1)S(1)}, bf16[272,256]{1,0:T(8,128)(2,1)S(1)}, u32[]{:S(2)}, u32[]{:S(2)}) collective-permute-start(bf16[272,256]{1,0:T(8,128)(2,1)S(1)} %get-tuple-element.52.refs_0_), channel_id=1, source_target_pairs={{0,8},{1,9},{2,10},{3,11},{4,12},{5,13},{6,14},{7,15},{8,0},{9,1},... | collective-permute-start | bytes 417800 | tf_op jit(solution)/shard_map/ppermute | solution.py:277
  8.9 6.1 %collective-permute-start.3 = (bf16[272,256]{1,0:T(8,128)(2,1)S(1)}, bf16[272,256]{1,0:T(8,128)(2,1)S(1)}, u32[]{:S(2)}, u32[]{:S(2)}) collective-permute-start(bf16[272,256]{1,0:T(8,128)(2,1)S(1)} %get-tuple-element.52.refs_0_), channel_id=1, source_target_pairs={{0,1},{1,0},{2,3},{3,2},{4,5},{5,4},{6,7},{7,6},{8,9},{9,8},{10,11... | collective-permute-start | bytes 417800 | tf_op jit(solution)/shard_map/ppermute | solution.py:277
  10.0 6.7 %collective-permute-start.7 = (bf16[272,256]{1,0:T(8,128)(2,1)S(1)}, bf16[272,256]{1,0:T(8,128)(2,1)S(1)}, u32[]{:S(2)}, u32[]{:S(2)}) collective-permute-start(bf16[272,256]{1,0:T(8,128)(2,1)S(1)} %collective-permute-done.refs_1_), channel_id=1, source_target_pairs={{0,2},{1,3},{2,0},{3,1},{4,6},{5,7},{6,4},{7,5},{8,10},{9,11},{10,... | collective-permute-start | bytes 417800 | tf_op jit(solution)/shard_map/ppermute | solution.py:277
  12.0 4.8 %collective-permute-start.8 = (bf16[272,256]{1,0:T(8,128)(2,1)S(1)}, bf16[272,256]{1,0:T(8,128)(2,1)S(1)}, u32[]{:S(2)}, u32[]{:S(2)}) collective-permute-start(bf16[272,256]{1,0:T(8,128)(2,1)S(1)} %collective-permute-done.refs_1_), channel_id=1, source_target_pairs={{0,1},{1,0},{2,3},{3,2},{4,5},{5,4},{6,7},{7,6},{8,9},{9,8},{10,11... | collective-permute-start | bytes 417800 | tf_op jit(solution)/shard_map/ppermute | solution.py:277
  12.0 5.3 %collective-permute-start.9 = (bf16[272,256]{1,0:T(8,128)(2,1)S(1)}, bf16[272,256]{1,0:T(8,128)(2,1)S(1)}, u32[]{:S(2)}, u32[]{:S(2)}) collective-permute-start(bf16[272,256]{1,0:T(8,128)(2,1)S(1)} %collective-permute-done.1.refs_2_), channel_id=1, source_target_pairs={{0,1},{1,0},{2,3},{3,2},{4,5},{5,4},{6,7},{7,6},{8,9},{9,8},{10,11... | collective-permute-start | bytes 417800 | tf_op jit(solution)/shard_map/ppermute | solution.py:277
  15.1 6.1 %collective-permute-start.5 = (bf16[272,256]{1,0:T(8,128)(2,1)S(1)}, bf16[272,256]{1,0:T(8,128)(2,1)S(1)}, u32[]{:S(2)}, u32[]{:S(2)}) collective-permute-start(bf16[272,256]{1,0:T(8,128)(2,1)S(1)} %collective-permute-done.2.refs_0_), channel_id=1, source_target_pairs={{0,4},{1,5},{2,6},{3,7},{4,0},{5,1},{6,2},{7,3},{8,12},{9,13},{10,... | collective-permute-start | bytes 417800 | tf_op jit(solution)/shard_map/ppermute | solution.py:277
  15.1 6.1 %collective-permute-start.6 = (bf16[272,256]{1,0:T(8,128)(2,1)S(1)}, bf16[272,256]{1,0:T(8,128)(2,1)S(1)}, u32[]{:S(2)}, u32[]{:S(2)}) collective-permute-start(bf16[272,256]{1,0:T(8,128)(2,1)S(1)} %collective-permute-done.2.refs_0_), channel_id=1, source_target_pairs={{0,2},{1,3},{2,0},{3,1},{4,6},{5,7},{6,4},{7,5},{8,10},{9,11},{10,... | collective-permute-start | bytes 417800 | tf_op jit(solution)/shard_map/ppermute | solution.py:277
  16.7 5.1 %collective-permute-start.10 = (bf16[272,256]{1,0:T(8,128)(2,1)S(1)}, bf16[272,256]{1,0:T(8,128)(2,1)S(1)}, u32[]{:S(2)}, u32[]{:S(2)}) collective-permute-start(bf16[272,256]{1,0:T(8,128)(2,1)S(1)} %collective-permute-done.2.refs_0_), channel_id=1, source_target_pairs={{0,1},{1,0},{2,3},{3,2},{4,5},{5,4},{6,7},{7,6},{8,9},{9,8},{10,11... | collective-permute-start | bytes 417800 | tf_op jit(solution)/shard_map/ppermute | solution.py:277
  16.8 5.0 %collective-permute-start.11 = (bf16[272,256]{1,0:T(8,128)(2,1)S(1)}, bf16[272,256]{1,0:T(8,128)(2,1)S(1)}, u32[]{:S(2)}, u32[]{:S(2)}) collective-permute-start(bf16[272,256]{1,0:T(8,128)(2,1)S(1)} %collective-permute-done.7.refs_0_), channel_id=1, source_target_pairs={{0,1},{1,0},{2,3},{3,2},{4,5},{5,4},{6,7},{7,6},{8,9},{9,8},{10,11... | collective-permute-start | bytes 417800 | tf_op jit(solution)/shard_map/ppermute | solution.py:277
  17.3 6.8 %collective-permute-start.4 = (bf16[272,256]{1,0:T(8,128)(2,1)S(1)}, bf16[272,256]{1,0:T(8,128)(2,1)S(1)}, u32[]{:S(2)}, u32[]{:S(2)}) collective-permute-start(bf16[272,256]{1,0:T(8,128)(2,1)S(1)} %collective-permute-done.2.refs_0_), channel_id=1, source_target_pairs={{0,6},{1,7},{2,4},{3,5},{4,2},{5,3},{6,0},{7,1},{8,14},{9,15},{10,... | collective-permute-start | bytes 417800 | tf_op jit(solution)/shard_map/ppermute | solution.py:277
  21.2 3.1 %collective-permute-start.13 = (bf16[272,256]{1,0:T(8,128)(2,1)S(1)}, bf16[272,256]{1,0:T(8,128)(2,1)S(1)}, u32[]{:S(2)}, u32[]{:S(2)}) collective-permute-start(bf16[272,256]{1,0:T(8,128)(2,1)S(1)} %collective-permute-done.5.refs_0_), channel_id=1, source_target_pairs={{0,1},{1,0},{2,3},{3,2},{4,5},{5,4},{6,7},{7,6},{8,9},{9,8},{10,11... | collective-permute-start | bytes 417800 | tf_op jit(solution)/shard_map/ppermute | solution.py:277
  21.2 3.0 %collective-permute-start.14 = (bf16[272,256]{1,0:T(8,128)(2,1)S(1)}, bf16[272,256]{1,0:T(8,128)(2,1)S(1)}, u32[]{:S(2)}, u32[]{:S(2)}) collective-permute-start(bf16[272,256]{1,0:T(8,128)(2,1)S(1)} %collective-permute-done.6.refs_1_), channel_id=1, source_target_pairs={{0,1},{1,0},{2,3},{3,2},{4,5},{5,4},{6,7},{7,6},{8,9},{9,8},{10,11... | collective-permute-start | bytes 417800 | tf_op jit(solution)/shard_map/ppermute | solution.py:277
  24.1 2.6 %collective-permute-start.12 = (bf16[272,256]{1,0:T(8,128)(2,1)S(1)}, bf16[272,256]{1,0:T(8,128)(2,1)S(1)}, u32[]{:S(2)}, u32[]{:S(2)}) collective-permute-start(bf16[272,256]{1,0:T(8,128)(2,1)S(1)} %collective-permute-done.4.refs_0_), channel_id=1, source_target_pairs={{0,1},{1,0},{2,3},{3,2},{4,5},{5,4},{6,7},{7,6},{8,9},{9,8},{10,11... | collective-permute-start | bytes 417800 | tf_op jit(solution)/shard_map/ppermute | solution.py:277
  27.7 1.8 %collective-permute-start.15 = (bf16[64,2048]{1,0:T(8,128)(2,1)S(1)}, bf16[64,2048]{1,0:T(8,128)(2,1)S(1)}, u32[]{:S(2)}, u32[]{:S(2)}) collective-permute-start(bf16[64,2048]{1,0:T(8,128)(2,1)S(1)} %get-tuple-element.94.mine_ref), channel_id=1, source_target_pairs={{0,1},{1,0},{2,3},{3,2},{4,5},{5,4},{6,7},{7,6},{8,9},{9,8},{10,11... | collective-permute-start | bytes 786440 | tf_op jit(solution)/shard_map/ppermute | solution.py:277
  31.1 1.3 %collective-permute-start.16 = (f32[64,256]{1,0:T(8,128)S(1)}, f32[64,256]{1,0:T(8,128)S(1)}, u32[]{:S(2)}, u32[]{:S(2)}) collective-permute-start(f32[64,256]{1,0:T(8,128)S(1)} %get-tuple-element.96), channel_id=1, source_target_pairs={{0,1},{1,0},{2,3},{3,2},{4,5},{5,4},{6,7},{7,6},{8,9},{9,8},{10,11... | collective-permute-start | bytes 196616 | tf_op jit(solution)/shard_map/ppermute | solution.py:277
